TPU v7x, 128 devices: a whole 4x4x4 slice. The times are simulated.
128 devices in a mesh: level: 8 (over z_hi, x), tile: 16 (over z_lo, y, core).
Axes of the slice: x: 4, y: 4, z: 4 (z_hi: 2, z_lo: 2; z = z_hi * 2 + z_lo), core: 2. Of those that a mesh axis runs over, the one named last changes fastest.
Arguments:
- level_state: float32 [8, 16, 256, 2048], P('level', None, 'tile'), may hold values from -2.5 to 2.5
- history: float32 [8, 3, 16, 256, 2048], P('level', None, None, 'tile'), may hold values from -4 to 4
- diffusion: float32 [16], replicated, may hold values from 0.02 to 0.2
- linear_rates: float32 [16, 16], replicated, may hold values from -1.5 to 1.5
- coupling: float32 [16, 16], replicated, may hold values from -1.5 to 1.5
Outputs:
- advanced_state: float32 [8, 16, 256, 2048], P('level', None, 'tile')
All inputs are finite; a program needn't handle non-finite values.
Results may differ from a plain program's by a relative error of at most 0.0003.
Values sent between devices are 32-bit elements; how exact they have to be, the bound alone decides.
No kernel may reach another device: no remote copies, remote signals or barrier semaphores. Data moves between devices by JAX's collectives and lax.ppermute only.
A program may use at most 128 MiB of HBM per device.

v0:
```python
import jax
import jax.numpy as jnp
from jax import lax
from jax.sharding import PartitionSpec as P

TICKS = 4


STEP_SIZE = 0.4
QUAD_WEIGHTS = (1.0 / 24.0, -5.0 / 24.0, 19.0 / 24.0, 9.0 / 24.0)
DIFF_TAPS = (-1.0 / 12.0, 16.0 / 12.0, -30.0 / 12.0, 16.0 / 12.0, -1.0 / 12.0)


def with_halo(cells, sides, width):
    for axis, dim in sides:
        count = lax.axis_size(axis)
        head = lax.slice_in_dim(cells, 0, width, axis=dim)
        tail = lax.slice_in_dim(cells, cells.shape[dim] - width, cells.shape[dim], axis=dim)
        cells = jnp.concatenate(
            [
                lax.ppermute(tail, axis, [(i, (i + 1) % count) for i in range(count)]),
                cells,
                lax.ppermute(head, axis, [((i + 1) % count, i) for i in range(count)]),
            ],
            axis=dim,
        )
    return cells


def passed_along(value, axis, by):
    peers = lax.axis_size(axis)
    pairs = [(i, i + by) for i in range(peers) if 0 <= i + by < peers]
    return lax.ppermute(value, axis, pairs)


def local_rates(padded, diffusion, linear_rates, coupling):
    height = padded.shape[1] - 4
    centre = padded[:, 2 : 2 + height, :]
    laplace_sum = jnp.zeros_like(centre)
    for offset in range(5):
        laplace_sum = laplace_sum + DIFF_TAPS[offset] * padded[:, offset : offset + height, :]
        laplace_sum = laplace_sum + DIFF_TAPS[offset] * jnp.roll(centre, 2 - offset, axis=2)
    linear = jnp.einsum("ab,brc->arc", linear_rates, centre, precision=lax.Precision.HIGHEST)
    saturated = jnp.tanh(
        jnp.einsum("ab,brc->arc", coupling, centre, precision=lax.Precision.HIGHEST)
    )
    cubic = centre * centre * centre / 3.0
    return diffusion[:, None, None] * laplace_sum + linear + saturated - cubic


def quadrature(older, middle, newest, current):
    total = QUAD_WEIGHTS[0] * older + QUAD_WEIGHTS[1] * middle
    total = total + (QUAD_WEIGHTS[2] - 1.0) * newest + QUAD_WEIGHTS[3] * current
    return STEP_SIZE * total


def local(level_state, history, diffusion, linear_rates, coupling):
    current_state = level_state[0]
    older = history[0, 0]
    middle = history[0, 1]
    newest = history[0, 2]
    for step_index in range(TICKS):
        padded = with_halo(current_state, (("tile", 1),), 2)
        current = local_rates(padded, diffusion, linear_rates, coupling)
        base_state = current_state
        outgoing = quadrature(older, middle, newest, current)
        incoming = passed_along(outgoing, "level", 1)
        older, middle, newest = (middle, newest, current)
        current_state = base_state + STEP_SIZE * current + incoming
    return current_state[None]


def solution(mesh):
    placed = (P("level", None, "tile", None), P("level", None, None, "tile", None), P(), P(), P())
    return jax.shard_map(
        local, mesh=mesh, in_specs=placed, out_specs=P("level", None, "tile", None), check_vma=False
    )
```

profile of v0, /device:TPU:89, one launch (start us, length us, event | category | flops | bytes accessed | tf_op | source)
XLA Modules:
  0.0 307.8 jit_solution(14850224834954582449)
XLA Ops:
  0.0 2.8 copy.42
  8.2 4.2 %collective-permute-done.1 = f32[16,2,2048]{2,0,1:T(8,128)S(1)} collective-permute-done((f32[16,2,2048]{2,0,1:T(8,128)S(1)}, f32[16,2,2048]{2,0,1:T(8,128)S(1)}, u32[]{:S(2)}, u32[]{:S(2)}) %collective-permute-start.1) | collective-permute-done | bytes 262176 | tf_op jit(solution)/shard_map/ppermute | solution.py:23
  12.4 3.4 %convolution_add_fusion = f32[16,16,2048]{2,0,1:T(8,128)S(1)} fusion(f32[16,16,2048]{2,0,1:T(8,128)S(1)} %bitcast.101, f32[16,2,2048]{2,0,1:T(8,128)S(1)} %collective-permute-done.1, f32[16,2,2048]{2,0,1:T(8,128)S(1)} %collective-permute-done, f32[16,16,2046]{2,0,1:T(8,128)S(1)} %get-tuple-element.39, f32[16,16,2]{2,0,1:T(8,128)S(1)} %get-tuple-element.41, ...), kind=kOutput, calls=%fused_computation.29 | convolution fusion | flops 114819072 | bytes 15737344 | tf_op jit(solution)/shard_map/ab,brc->arc/dot_general | solution.py:43
  15.9 8.0 %fusion.78 = (f32[16,16,2048]{2,0,1:T(8,128)S(1)}, f32[16,16,2048]{2,0,1:T(8,128)S(1)}) fusion(f32[1,1,16,16,2048]{4,3,2,1,0:T(8,128)S(1)} %get-tuple-element.7, f32[1,1,16,16,2048]{4,3,2,1,0:T(8,128)S(1)} %get-tuple-element.6, f32[1,1,16,16,2048]{4,3,2,1,0:T(8,128)S(1)} %get-tuple-element.5, f32[1,16,16,2048]{3,2,1,0:T(8,128)S(1)} %copy-done.1, ...), kind=kOutput, calls=%fused_computation.131 | convolution fusion | flops 107479040 | bytes 14681088 | tf_op jit(solution)/shard_map/ab,brc->arc/dot_general | solution.py:45
  23.9 3.3 %collective-permute-start.2 = (f32[16,16,2048]{2,0,1:T(8,128)S(1)}, f32[16,16,2048]{2,0,1:T(8,128)S(1)}, u32[]{:S(2)}, u32[]{:S(2)}) collective-permute-start(f32[16,16,2048]{2,0,1:T(8,128)S(1)} %get-tuple-element.48), channel_id=1, source_target_pairs={{0,16},{16,32},{32,48},{48,64},{64,80},{80,96},{96,112},{1,17},{17... | collective-permute-start | bytes 6291464 | tf_op jit(solution)/shard_map/ppermute | solution.py:33
  27.2 47.0 %collective-permute-done.2 = f32[16,16,2048]{2,0,1:T(8,128)S(1)} collective-permute-done((f32[16,16,2048]{2,0,1:T(8,128)S(1)}, f32[16,16,2048]{2,0,1:T(8,128)S(1)}, u32[]{:S(2)}, u32[]{:S(2)}) %collective-permute-start.2) | collective-permute-done | bytes 2097184 | tf_op jit(solution)/shard_map/ppermute | solution.py:33
  75.9 2.0 fusion.8
  77.9 2.1 fusion.103
  80.0 2.7 fusion.105
  82.7 2.6 collective-permute-start.3
  85.5 3.1 %collective-permute-done.3 = f32[16,2,2048]{2,0,1:T(8,128)S(1)} collective-permute-done((f32[16,2,2048]{2,0,1:T(8,128)S(1)}, f32[16,2,2048]{2,0,1:T(8,128)S(1)}, u32[]{:S(2)}, u32[]{:S(2)}) %collective-permute-start.3) | collective-permute-done | bytes 262176 | tf_op jit(solution)/shard_map/ppermute | solution.py:21
  88.6 4.6 %collective-permute-done.4 = f32[16,2,2048]{2,0,1:T(8,128)S(1)} collective-permute-done((f32[16,2,2048]{2,0,1:T(8,128)S(1)}, f32[16,2,2048]{2,0,1:T(8,128)S(1)}, u32[]{:S(2)}, u32[]{:S(2)}) %collective-permute-start.4) | collective-permute-done | bytes 262176 | tf_op jit(solution)/shard_map/ppermute | solution.py:23
  93.2 11.5 %fusion.83 = (f32[16,16,2048]{2,0,1:T(8,128)}, f32[16,16,2048]{2,0,1:T(8,128)S(1)}) fusion(f32[1,1,16,16,2048]{4,3,2,1,0:T(8,128)S(1)} %get-tuple-element.6, f32[16,16,2048]{2,0,1:T(8,128)S(1)} %get-tuple-element.49, f32[1,1,16,16,2048]{4,3,2,1,0:T(8,128)S(1)} %get-tuple-element.5, f32[16,16,2048]{2,0,1:T(8,128)S(1)} %add_add_fusion.6, ...), kind=kOutput, calls=%fused_computation.138 | convolution fusion | flops 121634816 | bytes 26219008 | tf_op jit(solution)/shard_map/ab,brc->arc/dot_general | solution.py:43
  104.7 2.1 collective-permute-start.5
  106.8 45.8 %collective-permute-done.5 = f32[16,16,2048]{2,0,1:T(8,128)S(1)} collective-permute-done((f32[16,16,2048]{2,0,1:T(8,128)}, f32[16,16,2048]{2,0,1:T(8,128)S(1)}, u32[]{:S(2)}, u32[]{:S(2)}) %collective-permute-start.5) | collective-permute-done | bytes 2097184 | tf_op jit(solution)/shard_map/ppermute | solution.py:33
  153.3 2.0 fusion.4
  155.3 2.1 fusion.98
  157.3 2.7 fusion.100
  160.1 3.5 %collective-permute-start.6 = (f32[16,2,2048]{2,0,1:T(8,128)S(1)}, f32[16,2,2048]{2,0,1:T(8,128)S(1)}, u32[]{:S(2)}, u32[]{:S(2)}) collective-permute-start(f32[16,2,2048]{2,0,1:T(8,128)S(1)} %get-tuple-element.26), channel_id=1, source_target_pairs={{0,1},{1,2},{2,3},{3,4},{4,5},{5,6},{6,7},{7,8},{8,9},{9,10},{10,1... | collective-permute-start | bytes 786440 | tf_op jit(solution)/shard_map/ppermute | solution.py:21
  163.8 3.1 %collective-permute-done.6 = f32[16,2,2048]{2,0,1:T(8,128)S(1)} collective-permute-done((f32[16,2,2048]{2,0,1:T(8,128)S(1)}, f32[16,2,2048]{2,0,1:T(8,128)S(1)}, u32[]{:S(2)}, u32[]{:S(2)}) %collective-permute-start.6) | collective-permute-done | bytes 262176 | tf_op jit(solution)/shard_map/ppermute | solution.py:21
  166.9 4.6 %collective-permute-done.7 = f32[16,2,2048]{2,0,1:T(8,128)S(1)} collective-permute-done((f32[16,2,2048]{2,0,1:T(8,128)S(1)}, f32[16,2,2048]{2,0,1:T(8,128)S(1)}, u32[]{:S(2)}, u32[]{:S(2)}) %collective-permute-start.7) | collective-permute-done | bytes 262176 | tf_op jit(solution)/shard_map/ppermute | solution.py:23
  171.5 9.5 %fusion.81 = (f32[16,16,2048]{2,0,1:T(8,128)}, f32[16,16,2048]{2,0,1:T(8,128)S(1)}) fusion(f32[1,1,16,16,2048]{4,3,2,1,0:T(8,128)S(1)} %get-tuple-element.5, f32[16,16,2048]{2,0,1:T(8,128)S(1)} %get-tuple-element.51, f32[16,16,2048]{2,0,1:T(8,128)S(1)} %get-tuple-element.49, f32[16,16,2048]{2,0,1:T(8,128)S(1)} %add_add_fusion.5, ...), kind=kOutput, calls=%fused_computation.135 | convolution fusion | flops 121634816 | bytes 26219008 | tf_op jit(solution)/shard_map/ab,brc->arc/dot_general | solution.py:43
  182.9 45.2 %collective-permute-done.8 = f32[16,16,2048]{2,0,1:T(8,128)S(1)} collective-permute-done((f32[16,16,2048]{2,0,1:T(8,128)}, f32[16,16,2048]{2,0,1:T(8,128)S(1)}, u32[]{:S(2)}, u32[]{:S(2)}) %collective-permute-start.8) | collective-permute-done | bytes 2097184 | tf_op jit(solution)/shard_map/ppermute | solution.py:33
  228.8 2.0 fusion
  231.6 2.8 fusion.95
  234.4 5.7 %collective-permute-start.9 = (f32[16,2,2048]{2,0,1:T(8,128)S(1)}, f32[16,2,2048]{2,0,1:T(8,128)S(1)}, u32[]{:S(2)}, u32[]{:S(2)}) collective-permute-start(f32[16,2,2048]{2,0,1:T(8,128)S(1)} %get-tuple-element.16), channel_id=1, source_target_pairs={{0,1},{1,2},{2,3},{3,4},{4,5},{5,6},{6,7},{7,8},{8,9},{9,10},{10,1... | collective-permute-start | bytes 786440 | tf_op jit(solution)/shard_map/ppermute | solution.py:21
  240.3 3.1 %collective-permute-done.9 = f32[16,2,2048]{2,0,1:T(8,128)S(1)} collective-permute-done((f32[16,2,2048]{2,0,1:T(8,128)S(1)}, f32[16,2,2048]{2,0,1:T(8,128)S(1)}, u32[]{:S(2)}, u32[]{:S(2)}) %collective-permute-start.9) | collective-permute-done | bytes 262176 | tf_op jit(solution)/shard_map/ppermute | solution.py:21
  243.4 4.6 %collective-permute-done.10 = f32[16,2,2048]{2,0,1:T(8,128)S(1)} collective-permute-done((f32[16,2,2048]{2,0,1:T(8,128)S(1)}, f32[16,2,2048]{2,0,1:T(8,128)S(1)}, u32[]{:S(2)}, u32[]{:S(2)}) %collective-permute-start.10) | collective-permute-done | bytes 262176 | tf_op jit(solution)/shard_map/ppermute | solution.py:23
  248.0 8.0 %add_multiply_fusion = (f32[16,16,2048]{2,0,1:T(8,128)}, f32[16,16,2048]{2,0,1:T(8,128)}) fusion(f32[16,16,2048]{2,0,1:T(8,128)S(1)} %get-tuple-element.53, f32[16,16,2048]{2,0,1:T(8,128)S(1)} %get-tuple-element.49, f32[16,16,2048]{2,0,1:T(8,128)S(1)} %get-tuple-element.51, f32[16,16,2048]{2,0,1:T(8,128)S(1)} %add_add_fusion.4, ...), kind=kOutput, calls=%fused_computation.141 | convolution fusion | flops 121634816 | bytes 26221056 | tf_op jit(solution)/shard_map/ab,brc->arc/dot_general | solution.py:43
  257.9 45.2 %collective-permute-done.11 = f32[16,16,2048]{2,0,1:T(8,128)S(1)} collective-permute-done((f32[16,16,2048]{2,0,1:T(8,128)}, f32[16,16,2048]{2,0,1:T(8,128)S(1)}, u32[]{:S(2)}, u32[]{:S(2)}) %collective-permute-start.11) | collective-permute-done | bytes 2097184 | tf_op jit(solution)/shard_map/ppermute | solution.py:33
  303.2 2.1 add_bitcast_fusion
  305.3 2.5 copy.10
  (40 shorter events, 13.5 us)
Async XLA Ops:
  0.0 12.4 %copy-start = (f32[16,16]{1,0:T(8,128)S(1)}, f32[16,16]{1,0:T(8,128)}, u32[]{:S(2)}) copy-start(f32[16,16]{1,0:T(8,128)} %param.8) | copy-start | bytes 3076
  2.9 5.3 %collective-permute-start = (f32[16,2,2048]{2,0,1:T(8,128)S(1)}, f32[16,2,2048]{2,0,1:T(8,128)S(1)}, u32[]{:S(2)}, u32[]{:S(2)}) collective-permute-start(f32[16,2,2048]{2,0,1:T(8,128)S(1)} %get-tuple-element.46), channel_id=1, source_target_pairs={{0,1},{1,2},{2,3},{3,4},{4,5},{5,6},{6,7},{7,8},{8,9},{9,10},{10,1... | collective-permute-start | bytes 786440 | tf_op jit(solution)/shard_map/ppermute | solution.py:21
  4.5 7.9 %collective-permute-start.1 = (f32[16,2,2048]{2,0,1:T(8,128)S(1)}, f32[16,2,2048]{2,0,1:T(8,128)S(1)}, u32[]{:S(2)}, u32[]{:S(2)}) collective-permute-start(f32[16,2,2048]{2,0,1:T(8,128)S(1)} %get-tuple-element.47), channel_id=1, source_target_pairs={{1,0},{2,1},{3,2},{4,3},{5,4},{6,5},{7,6},{8,7},{9,8},{10,9},{11,1... | collective-permute-start | bytes 786440 | tf_op jit(solution)/shard_map/ppermute | solution.py:23
  4.5 2.2 slice-start
  5.3 2.3 slice-start.1
  7.6 4.8 %copy-start.3 = (f32[16]{0:T(128)S(1)}, f32[16]{0:T(128)}, u32[]{:S(2)}) copy-start(f32[16]{0:T(128)} %param.7) | copy-start | bytes 196
  12.4 3.4 %copy-start.1 = (f32[1,16,16,2048]{3,2,1,0:T(8,128)S(1)}, f32[1,16,16,2048]{3,2,1,0:T(8,128)}, u32[]{:S(2)}) copy-start(f32[1,16,16,2048]{3,2,1,0:T(8,128)} %param.5) | copy-start | bytes 6291460
  12.4 3.4 %copy-start.2 = (f32[16,16]{1,0:T(8,128)S(1)}, f32[16,16]{1,0:T(8,128)}, u32[]{:S(2)}) copy-start(f32[16,16]{1,0:T(8,128)} %param.9) | copy-start | bytes 3076
  23.9 50.3 %collective-permute-start.2 = (f32[16,16,2048]{2,0,1:T(8,128)S(1)}, f32[16,16,2048]{2,0,1:T(8,128)S(1)}, u32[]{:S(2)}, u32[]{:S(2)}) collective-permute-start(f32[16,16,2048]{2,0,1:T(8,128)S(1)} %get-tuple-element.48), channel_id=1, source_target_pairs={{0,16},{16,32},{32,48},{48,64},{64,80},{80,96},{96,112},{1,17},{17... | collective-permute-start | bytes 6291464 | tf_op jit(solution)/shard_map/ppermute | solution.py:33
  82.7 5.9 %collective-permute-start.3 = (f32[16,2,2048]{2,0,1:T(8,128)S(1)}, f32[16,2,2048]{2,0,1:T(8,128)S(1)}, u32[]{:S(2)}, u32[]{:S(2)}) collective-permute-start(f32[16,2,2048]{2,0,1:T(8,128)S(1)} %get-tuple-element.36), channel_id=1, source_target_pairs={{0,1},{1,2},{2,3},{3,4},{4,5},{5,6},{6,7},{7,8},{8,9},{9,10},{10,1... | collective-permute-start | bytes 786440 | tf_op jit(solution)/shard_map/ppermute | solution.py:21
  85.3 7.9 %collective-permute-start.4 = (f32[16,2,2048]{2,0,1:T(8,128)S(1)}, f32[16,2,2048]{2,0,1:T(8,128)S(1)}, u32[]{:S(2)}, u32[]{:S(2)}) collective-permute-start(f32[16,2,2048]{2,0,1:T(8,128)S(1)} %get-tuple-element.37), channel_id=1, source_target_pairs={{1,0},{2,1},{3,2},{4,3},{5,4},{6,5},{7,6},{8,7},{9,8},{10,9},{11,1... | collective-permute-start | bytes 786440 | tf_op jit(solution)/shard_map/ppermute | solution.py:23
  104.7 48.0 %collective-permute-start.5 = (f32[16,16,2048]{2,0,1:T(8,128)}, f32[16,16,2048]{2,0,1:T(8,128)S(1)}, u32[]{:S(2)}, u32[]{:S(2)}) collective-permute-start(f32[16,16,2048]{2,0,1:T(8,128)} %get-tuple-element.50), channel_id=1, source_target_pairs={{0,16},{16,32},{32,48},{48,64},{64,80},{80,96},{96,112},{1,17},{17... | collective-permute-start | bytes 6291464 | tf_op jit(solution)/shard_map/ppermute | solution.py:33
  160.1 6.8 %collective-permute-start.6 = (f32[16,2,2048]{2,0,1:T(8,128)S(1)}, f32[16,2,2048]{2,0,1:T(8,128)S(1)}, u32[]{:S(2)}, u32[]{:S(2)}) collective-permute-start(f32[16,2,2048]{2,0,1:T(8,128)S(1)} %get-tuple-element.26), channel_id=1, source_target_pairs={{0,1},{1,2},{2,3},{3,4},{4,5},{5,6},{6,7},{7,8},{8,9},{9,10},{10,1... | collective-permute-start | bytes 786440 | tf_op jit(solution)/shard_map/ppermute | solution.py:21
  163.6 7.9 %collective-permute-start.7 = (f32[16,2,2048]{2,0,1:T(8,128)S(1)}, f32[16,2,2048]{2,0,1:T(8,128)S(1)}, u32[]{:S(2)}, u32[]{:S(2)}) collective-permute-start(f32[16,2,2048]{2,0,1:T(8,128)S(1)} %get-tuple-element.27), channel_id=1, source_target_pairs={{1,0},{2,1},{3,2},{4,3},{5,4},{6,5},{7,6},{8,7},{9,8},{10,9},{11,1... | collective-permute-start | bytes 786440 | tf_op jit(solution)/shard_map/ppermute | solution.py:23
  181.0 47.2 %collective-permute-start.8 = (f32[16,16,2048]{2,0,1:T(8,128)}, f32[16,16,2048]{2,0,1:T(8,128)S(1)}, u32[]{:S(2)}, u32[]{:S(2)}) collective-permute-start(f32[16,16,2048]{2,0,1:T(8,128)} %get-tuple-element.52), channel_id=1, source_target_pairs={{0,16},{16,32},{32,48},{48,64},{64,80},{80,96},{96,112},{1,17},{17... | collective-permute-start | bytes 6291464 | tf_op jit(solution)/shard_map/ppermute | solution.py:33
  234.4 9.0 %collective-permute-start.9 = (f32[16,2,2048]{2,0,1:T(8,128)S(1)}, f32[16,2,2048]{2,0,1:T(8,128)S(1)}, u32[]{:S(2)}, u32[]{:S(2)}) collective-permute-start(f32[16,2,2048]{2,0,1:T(8,128)S(1)} %get-tuple-element.16), channel_id=1, source_target_pairs={{0,1},{1,2},{2,3},{3,4},{4,5},{5,6},{6,7},{7,8},{8,9},{9,10},{10,1... | collective-permute-start | bytes 786440 | tf_op jit(solution)/shard_map/ppermute | solution.py:21
  240.1 7.9 %collective-permute-start.10 = (f32[16,2,2048]{2,0,1:T(8,128)S(1)}, f32[16,2,2048]{2,0,1:T(8,128)S(1)}, u32[]{:S(2)}, u32[]{:S(2)}) collective-permute-start(f32[16,2,2048]{2,0,1:T(8,128)S(1)} %get-tuple-element.17), channel_id=1, source_target_pairs={{1,0},{2,1},{3,2},{4,3},{5,4},{6,5},{7,6},{8,7},{9,8},{10,9},{11,1... | collective-permute-start | bytes 786440 | tf_op jit(solution)/shard_map/ppermute | solution.py:23
  256.0 47.2 %collective-permute-start.11 = (f32[16,16,2048]{2,0,1:T(8,128)}, f32[16,16,2048]{2,0,1:T(8,128)S(1)}, u32[]{:S(2)}, u32[]{:S(2)}) collective-permute-start(f32[16,16,2048]{2,0,1:T(8,128)} %get-tuple-element.54), channel_id=1, source_target_pairs={{0,16},{16,32},{32,48},{48,64},{64,80},{80,96},{96,112},{1,17},{17... | collective-permute-start | bytes 6291464 | tf_op jit(solution)/shard_map/ppermute | solution.py:33
where the time goes:
time: 308 us
  waiting for transfers between devices  211 us (69%)
  matrix products  46.4 us (15%)
  local copies, waits for them, and re-layouts  22.9 us (7%)
  starting transfers between devices  22.7 us (7%)
  other arithmetic  5.02 us (2%)
    ppermute x4, waiting for transfers between devices, passed_along(): return lax.ppermute(value, axis, pairs)  183 us
    dot_general x4, matrix products, local_rates(): jnp.einsum('ab,brc->arc', linear_rates, centre, precision=lax.Precision.H...  32.5 us
    ppermute x4, waiting for transfers between devices, with_halo(): lax.ppermute(head, axis, [((i + 1) % count, i) for i in range(count)])  18 us
    slice x16, local copies, waits for them, and re-layouts, local_rates(): jnp.roll(centre, 2 - offset, axis=2)  15.4 us
    dot_general x4, matrix products, local_rates(): jnp.einsum('ab,brc->arc', coupling, centre, precision=lax.Precision.HIGHEST)  13.9 us
    ppermute x4, starting transfers between devices, with_halo(): lax.ppermute(tail, axis, [(i, (i + 1) % count) for i in range(count)])  13.4 us
    ppermute x4, waiting for transfers between devices, with_halo(): lax.ppermute(tail, axis, [(i, (i + 1) % count) for i in range(count)])  9.34 us
    ppermute x4, starting transfers between devices, passed_along(): return lax.ppermute(value, axis, pairs)  9.24 us
  transfers between devices with their start and end apart: 12, of which 11 were waited for; matrix products, arithmetic and copies ran while one was open for 1% of the time, Pallas kernels for 0%

commit v1 on v0

v1 whole, which is shorter than its diff:
```python
import functools

import jax
import jax.numpy as jnp
from jax import lax
from jax.experimental import pallas as pl
from jax.experimental.pallas import tpu as pltpu
from jax.sharding import PartitionSpec as P

SPECIES = 16
ROWS = 16
CELLS = SPECIES * ROWS
HALF = CELLS // 2
NCOL = 2048
RING = 4
CHUNK = NCOL // RING
HALO = 8
WIDE = CHUNK + 2 * HALO
EDGE = 2 * SPECIES
STEP = 0.4
W0, W1, W2, W3 = (1.0 / 24.0, -5.0 / 24.0, 19.0 / 24.0, 9.0 / 24.0)
TAPS = (-1.0 / 12.0, 16.0 / 12.0, -30.0 / 12.0, 16.0 / 12.0, -1.0 / 12.0)
SHIFTS = (1, 3, 2)
PAD = 8

f32 = jnp.float32
bf16 = jnp.bfloat16
dot = functools.partial(jnp.dot, preferred_element_type=f32)


def params(mib=24, **kw):
    return pltpu.CompilerParams(vmem_limit_bytes=mib * 1024 * 1024, **kw)


def vmem():
    return pl.BlockSpec(memory_space=pltpu.VMEM)


def hbm():
    return pl.BlockSpec(memory_space=pl.ANY)


def x_shift(by, skip_last=False):
    pairs = []
    for level in range(8):
        if skip_last and level == 7:
            continue
        high, x = divmod(level, RING)
        for tile in range(16):
            pairs.append((level * 16 + tile, (high * RING + (x + by) % RING) * 16 + tile))
    return pairs


def z_up():
    return [((x * 16) + t, ((RING + x) * 16) + t) for x in range(RING) for t in range(16)]


def tile_shift(by):
    return [(l * 16 + t, l * 16 + (t + by) % 16) for l in range(8) for t in range(16)]


def send(value, pairs):
    return lax.ppermute(value, ("level", "tile"), pairs)


def my_x():
    return lax.rem(lax.axis_index("level"), RING)


def my_high():
    return lax.div(lax.axis_index("level"), RING)


def turned(read):
    return jnp.concatenate([read(row) for row in range(ROWS)], axis=0).T


def place(scratch, n, value):
    i = pl.program_id(0)
    at = pl.multiple_of(i * 128, 128) + HALO
    scratch[n, pl.ds(pl.multiple_of(at, 8), 128), :] = value

    @pl.when(i == 0)
    def _():
        scratch[n, NCOL + HALO :, :] = value[:HALO]

    @pl.when(i == NCOL // 128 - 1)
    def _():
        scratch[n, :HALO, :] = value[128 - HALO :]


def hand_out(scratch, outs, sem):
    x = my_x()

    @pl.when(pl.program_id(0) == NCOL // 128 - 1)
    def _():
        copies = []
        for k, out_ref in enumerate(outs):
            n, by = divmod(k, RING)
            base = pl.multiple_of(lax.rem(x + by, RING) * CHUNK, 128)
            copies.append(pltpu.make_async_copy(scratch.at[n, pl.ds(base, WIDE), :], out_ref, sem.at[k]))
        for copy in copies:
            copy.start()
        for copy in copies:
            copy.wait()


def cut_state_kernel(state_ref, *refs):
    outs, scratch, sem = refs[:RING], *refs[RING:]
    place(scratch, 0, turned(lambda row: state_ref[pl.ds(row, SPECIES, stride=ROWS), :]))
    hand_out(scratch, outs, sem)


def cut_history_kernel(older_ref, middle_ref, newest_ref, *refs):
    outs, scratch, sem = refs[: 3 * RING], *refs[3 * RING :]

    def parts(row):
        rows = pl.ds(row, SPECIES, stride=ROWS)
        return older_ref[0, rows, :], middle_ref[0, rows, :], newest_ref[0, rows, :]

    def first(row):
        p, q, r = parts(row)
        return STEP * (W0 * p + W1 * q + (W2 - 1.0) * r)

    def second(row):
        _, q, r = parts(row)
        return STEP * (W0 * q + W1 * r)

    def third(row):
        return (STEP * W0) * parts(row)[2]

    for n, read in enumerate((first, second, third)):
        place(scratch, n, turned(read))
    hand_out(scratch, outs, sem)


def cut_state(state):
    return pl.pallas_call(
        cut_state_kernel,
        grid=(NCOL // 128,),
        out_shape=[jax.ShapeDtypeStruct((WIDE, CELLS), f32)] * RING,
        in_specs=[pl.BlockSpec((CELLS, 128), lambda i: (0, i))],
        out_specs=[hbm()] * RING,
        scratch_shapes=[pltpu.VMEM((1, NCOL + 2 * HALO, CELLS), f32), pltpu.SemaphoreType.DMA((RING,))],
        compiler_params=params(),
        name="cut_state",
    )(state)


def cut_history(hist):
    part = lambda n: pl.BlockSpec((1, CELLS, 128), lambda i: (n, 0, i))
    return pl.pallas_call(
        cut_history_kernel,
        grid=(NCOL // 128,),
        out_shape=[jax.ShapeDtypeStruct((WIDE, CELLS), f32)] * (3 * RING),
        in_specs=[part(0), part(1), part(2)],
        out_specs=[hbm()] * (3 * RING),
        scratch_shapes=[pltpu.VMEM((3, NCOL + 2 * HALO, CELLS), f32), pltpu.SemaphoreType.DMA((3 * RING,))],
        compiler_params=params(),
        name="cut_history",
    )(hist, hist, hist)


def update_kernel(step, *refs):
    refs = list(refs)
    take = lambda n: [refs.pop(0) for _ in range(n)]
    new_field = take(RING) if step < 4 else None
    old_field = take(RING) if step > 0 else None
    y_ref, g_ref = take(2) if step > 0 else (None, None)
    z_ref = take(1)[0] if step > 1 else None
    u_ref, down_ref, up_ref = take(3)
    pay_ref = take(1)[0] if step > 0 else None
    x, high = my_x(), my_high()
    level_of = lambda by: lax.rem(x + RING - by, RING)

    def plain(field):
        for by in range(RING):
            u_ref[level_of(by)] = field[by][...]

    def added(field, with_pay):
        for by in range(RING):
            level = level_of(by)

            @pl.when(level < RING - 1)
            def _(by=by, level=level):
                u_ref[level + 1] = y_ref[level + 1] + field[by][...]

            if with_pay:

                @pl.when(level == RING - 1)
                def _(by=by):
                    pay_ref[...] = g_ref[...] + field[by][...]

    @pl.when(high == 0)
    def _():
        if step == 0:
            plain(new_field)
        elif step < 4:
            u_ref[0] = y_ref[0]
            added(new_field, True)
        else:
            u_ref[...] = y_ref[...]
            pay_ref[...] = g_ref[...]

    @pl.when(high == 1)
    def _():
        if step == 0:
            u_ref[...] = jnp.zeros_like(u_ref)
        elif step == 1:
            plain(old_field)
        else:
            u_ref[0] = y_ref[0] + z_ref[...]
            added(old_field, False)
        if step > 0:
            pay_ref[...] = jnp.zeros_like(pay_ref)

    lane = lax.broadcasted_iota(jnp.int32, (WIDE, HALF), 1)
    down = up = None
    for level in range(RING):
        here = (lane >= level * EDGE) & (lane < (level + 1) * EDGE)
        top = u_ref[level, :, :HALF]
        bottom = u_ref[level, :, HALF:]
        top = pltpu.roll(top, level * EDGE, 1) if level else top
        bottom = pltpu.roll(bottom, (level + 1) * EDGE, 1) if level < RING - 1 else bottom
        down = top if level == 0 else jnp.where(here, top, down)
        up = bottom if level == 0 else jnp.where(here, bottom, up)
    down_ref[...] = down
    up_ref[...] = up


def update(step, new_field, old_field, y, g, z):
    operands = []
    if step < 4:
        operands += new_field
    if step > 0:
        operands += old_field + [y, g]
    if step > 1:
        operands.append(z)
    outs = [pltpu.VMEM((RING, WIDE, CELLS), f32)] + [jax.ShapeDtypeStruct((WIDE, HALF), f32)] * 2
    if step > 0:
        outs.append(jax.ShapeDtypeStruct((WIDE, CELLS), f32))
    return pl.pallas_call(
        functools.partial(update_kernel, step),
        out_shape=outs,
        in_specs=[vmem()] * len(operands),
        out_specs=[vmem()] * len(outs),
        compiler_params=params(),
        name=f"update_{step}",
    )(*operands)


def rates_kernel(step, n_in, n_out, u_ref, above_ref, below_ref, main_ref, edge_ref, diff_ref, *refs):
    older = refs[:n_in]
    y_ref, g_ref = refs[n_in : n_in + 2]
    newer = refs[n_in + 2 : n_in + 2 + n_out]
    padded, stack, edges = refs[n_in + 2 + n_out :]

    def split(into, at, value):
        high_part = value.astype(bf16)
        width = value.shape[1]
        into[:, at : at + width] = high_part
        into[:, CELLS + at : CELLS + at + width] = (value - high_part.astype(f32)).astype(bf16)
        into[:, 2 * CELLS + at : 2 * CELLS + at + width] = high_part

    def work():
        padded[:, :PAD, :] = jnp.zeros((2, PAD, HALF), f32)
        padded[:, PAD + WIDE :, :] = jnp.zeros((2, PAD, HALF), f32)
        split(stack, 0, above_ref[...])
        split(stack, HALF, below_ref[...])
        edges[...] = dot(stack[...], edge_ref[...])
        g_ref[...] = jnp.zeros_like(g_ref)
        for level in range(RING):
            for side in range(2):
                part = u_ref[level, :, side * HALF : (side + 1) * HALF]
                padded[side, PAD : PAD + WIDE, :] = part
                split(stack, side * HALF, part)
            products = dot(stack[...], main_ref[...])
            for side in range(2):
                at = slice(side * HALF, (side + 1) * HALF)
                lane = lax.broadcasted_iota(jnp.int32, (48, HALF), 1)
                near_edge = lane >= HALF - EDGE if side else lane < EDGE
                turn = (HALF - EDGE - level * EDGE if side else HALF - level * EDGE) % HALF
                diff = diff_ref[0:1, at]
                for begin in range(0, WIDE, 48):
                    rows = slice(begin, begin + 48)
                    moved = lambda by: padded[side, PAD + begin + by : PAD + begin + by + 48, :]
                    u = moved(0)
                    near = moved(-1) + moved(1)
                    far = moved(-2) + moved(2)
                    edge = edges[rows, at]
                    edge = pltpu.roll(edge, turn, 1) if turn else edge
                    rate = products[rows, at] + jnp.where(near_edge, edge, 0.0)
                    rate = rate + diff * (16.0 * near - far)
                    rate = rate + jnp.tanh(products[rows, CELLS + side * HALF : CELLS + (side + 1) * HALF])
                    scaled = STEP * (rate - u * u * u * (1.0 / 3.0))
                    y_ref[level, rows, at] = u + scaled + g_ref[rows, at]
                    out = W3 * scaled
                    if n_in > 0:
                        out = out + older[0][level, rows, at]
                    g_ref[rows, at] = out
                    for k, weight in zip(range(n_out), (W2 - 1.0, W1, W0)):
                        value = weight * scaled
                        if k + 1 < n_in:
                            value = value + older[k + 1][level, rows, at]
                        newer[k][level, rows, at] = value

    if step < 4:
        work()
    else:
        high = my_high()
        pl.when(high == 1)(work)

        @pl.when(high == 0)
        def _():
            y_ref[...] = u_ref[...]
            g_ref[...] = jnp.zeros_like(g_ref)


def rates(step, u, above, below, weights, older, n_out):
    n_in = len(older)
    full = pltpu.VMEM((RING, WIDE, CELLS), f32)
    outs = pl.pallas_call(
        functools.partial(rates_kernel, step, n_in, n_out),
        out_shape=[full, pltpu.VMEM((WIDE, CELLS), f32)] + [full] * n_out,
        in_specs=[vmem()] * (6 + n_in),
        out_specs=[vmem()] * (2 + n_out),
        scratch_shapes=[
            pltpu.VMEM((2, WIDE + 2 * PAD, HALF), f32),
            pltpu.VMEM((WIDE, 3 * CELLS), bf16),
            pltpu.VMEM((WIDE, CELLS), f32),
        ],
        compiler_params=params(),
        name=f"rates_{step}",
    )(u, above, below, *weights, *older)
    return outs[0], outs[1], list(outs[2:])


def weights_kernel(lin_ref, coup_ref, diff_ref, main_ref, edge_ref, diff_out):
    exact = functools.partial(lax.dot_general, precision=lax.Precision.HIGHEST, preferred_element_type=f32)
    last = (((1,), (1,)), ((), ()))
    iota = lambda shape, dim: lax.broadcasted_iota(jnp.int32, shape, dim)
    pick = (iota((CELLS, SPECIES), 0) % SPECIES == iota((CELLS, SPECIES), 1)).astype(f32)
    source, target = iota((CELLS, CELLS), 0), iota((CELLS, CELLS), 1)
    same_row = source // SPECIES == target // SPECIES
    same_species = source % SPECIES == target % SPECIES
    diffusion = exact(diff_ref[...], pick, last)

    def tiled(matrix):
        return jnp.where(same_row, exact(exact(pick, matrix, last), pick, last), 0.0)

    def stencil(offset, middle):
        value = jnp.where(offset == 0, middle, 0.0)
        value = value + jnp.where((offset == 1) | (offset == -1), TAPS[1], 0.0)
        return value + jnp.where((offset == 2) | (offset == -2), TAPS[0], 0.0)

    def put(into, at, value):
        high_part = value.astype(bf16)
        into[:CELLS, at : at + CELLS] = high_part
        into[CELLS : 2 * CELLS, at : at + CELLS] = high_part
        into[2 * CELLS :, at : at + CELLS] = (value - high_part.astype(f32)).astype(bf16)

    offset = source // SPECIES - target // SPECIES
    spread = jnp.where(same_species, stencil(offset, 2.0 * TAPS[2]) * diffusion[0:1], 0.0)
    put(main_ref, 0, tiled(lin_ref[...]) + spread)
    put(main_ref, CELLS, tiled(coup_ref[...]))
    row_from = (source // SPECIES) % 2 + jnp.where(source < HALF, -2, ROWS)
    row_to = (target // SPECIES) % 2 + jnp.where(target < HALF, 0, ROWS - 2)
    alike = same_species & (source // EDGE == target // EDGE)
    put(edge_ref, 0, jnp.where(alike, stencil(row_from - row_to, 0.0) * diffusion[0:1], 0.0))
    diff_out[...] = diffusion * (1.0 / 12.0)


def make_weights(diffusion, linear_rates, coupling):
    return pl.pallas_call(
        weights_kernel,
        out_shape=[
            pltpu.VMEM((3 * CELLS, 2 * CELLS), bf16),
            pltpu.VMEM((3 * CELLS, CELLS), bf16),
            pltpu.VMEM((8, CELLS), f32),
        ],
        in_specs=[vmem()] * 3,
        out_specs=[vmem()] * 3,
        compiler_params=params(),
        name="weights",
    )(linear_rates, coupling, jnp.broadcast_to(diffusion[None], (8, SPECIES)))


def finish_kernel(y_ref, z_ref, *outs):
    x, high = my_x(), my_high()
    inner = slice(HALO, HALO + CHUNK)
    for by, out_ref in enumerate(outs):
        level = lax.rem(x + by, RING)
        takes = (level == 0) & (high == 1)

        @pl.when(takes)
        def _(out_ref=out_ref):
            out_ref[...] = y_ref[0, inner, :] + z_ref[inner, :]

        @pl.when(jnp.logical_not(takes))
        def _(out_ref=out_ref, level=level):
            out_ref[...] = y_ref[level, inner, :]


def finish(y, z):
    return pl.pallas_call(
        finish_kernel,
        out_shape=[jax.ShapeDtypeStruct((CHUNK, CELLS), f32)] * RING,
        in_specs=[vmem(), vmem()],
        out_specs=[vmem()] * RING,
        compiler_params=params(),
        name="finish",
    )(y, z)


def join_kernel(x_ref, *refs):
    parts, out_ref = refs[:RING], refs[RING]
    by = pl.program_id(0)
    for k, part in enumerate(parts):

        @pl.when(by == k)
        def _(part=part):
            value = part[...].T
            for row in range(ROWS):
                out_ref[pl.ds(row, SPECIES, stride=ROWS), :] = value[row * SPECIES : (row + 1) * SPECIES]


def join(parts, x):
    blocks = CHUNK // 128

    def spec(k):
        return pl.BlockSpec(
            (128, CELLS), lambda by, i, x_ref: (jnp.where(by == k, i, jnp.where(by < k, 0, blocks - 1)), 0)
        )

    return pl.pallas_call(
        join_kernel,
        grid_spec=pltpu.PrefetchScalarGridSpec(
            num_scalar_prefetch=1,
            grid=(RING, blocks),
            in_specs=[spec(k) for k in range(RING)],
            out_specs=pl.BlockSpec(
                (CELLS, 128), lambda by, i, x_ref: (0, lax.rem(x_ref[0] + RING - by, RING) * blocks + i)
            ),
        ),
        out_shape=jax.ShapeDtypeStruct((CELLS, NCOL), f32),
        compiler_params=params(dimension_semantics=("arbitrary", "arbitrary")),
        name="join",
    )(x, *parts)


def exchange(parts, earlier, skip_last=False):
    got = [parts[0], None, None, None]
    for by in SHIFTS:
        part = parts[by]
        if earlier is not None:
            part, _ = lax.optimization_barrier((part, earlier[by]))
        got[by] = send(part, x_shift(by, skip_last))
    return got


def local(level_state, history, diffusion, linear_rates, coupling):
    state = level_state.reshape(CELLS, NCOL)
    hist = history.reshape(3, CELLS, NCOL)
    weights = make_weights(diffusion, linear_rates, coupling)
    cut = cut_history(hist)
    fields = [exchange(cut_state(state), None)]
    for f in range(3):
        fields.append(exchange(cut[f * RING : (f + 1) * RING], fields[-1], True))

    y = g = z = None
    older = []
    n_outs = (3, 3, 2, 1, 0)
    for step in range(5):
        new_field = fields[step] if step < 4 else None
        old_field = fields[step - 1] if step > 0 else None
        u, down, up, *pay = update(step, new_field, old_field, y, g, z)
        above = send(up, tile_shift(1))
        below = send(down, tile_shift(-1))
        z = send(pay[0], z_up()) if pay else None
        y, g, older = rates(step, u, above, below, weights, older, n_outs[step])
    parts = finish(y, z)
    out = join(exchange(parts, None), my_x()[None])
    return out.reshape(1, SPECIES, ROWS, NCOL)


def solution(mesh):
    placed = (P("level", None, "tile", None), P("level", None, None, "tile", None), P(), P(), P())
    return jax.shard_map(
        local, mesh=mesh, in_specs=placed, out_specs=P("level", None, "tile", None), check_vma=False
    )
```

time: 308 us -> 202 us (0.66)
  waiting for transfers between devices: 211 us -> 103 us
  matrix products: 46.4 us -> 0 us
  Pallas kernels: 0 us -> 43.9 us
  starting transfers between devices: 22.7 us -> 48.1 us
  local copies, waits for them, and re-layouts: 22.9 us -> 4.4 us
  other arithmetic: 5.02 us -> 0 us
    ppermute x12 -> x29, waiting for transfers between devices: 211 us -> 103 us  [send(): return lax.ppermute(value, ('level', 'tile'), pairs)]
    dot_general x8 -> x0, matrix products: 46.4 us -> none  [the longest x4 32.5 us: local_rates(): jnp.einsum('ab,brc->arc', linear_rates, centre, precision=lax.Precision.H...]
    pallas_call x0 -> x15, Pallas kernels: none -> 43.9 us  [the longest x5 19.5 us: rates(): pl.pallas_call(functools.partial(rates_kernel, step, n_in, n_out), out_sh...]
    ppermute x12 -> x29, starting transfers between devices: 22.7 us -> 48.1 us  [send(): return lax.ppermute(value, ('level', 'tile'), pairs)]
    slice x21 -> x0, local copies, waits for them, and re-layouts: 16 us -> none  [the longest x16 15.4 us: local_rates(): jnp.roll(centre, 2 - offset, axis=2)]
  transfers between devices with their start and end apart: 12 -> 29, of which waited for: 11 -> 20; matrix products, arithmetic and copies ran while one was open for 1% -> 0% of each run, Pallas kernels for 0% -> 16%
where the time goes in v1:
time: 202 us; the launch traced here: 200 us
  waiting for transfers between devices  103 us (51%)
  starting transfers between devices  48.1 us (24%)
  Pallas kernels  43.9 us (22%)
  local copies, waits for them, and re-layouts  4.4 us (2%)
    ppermute x29, waiting for transfers between devices, send(): return lax.ppermute(value, ('level', 'tile'), pairs)  103 us
    ppermute x29, starting transfers between devices, send(): return lax.ppermute(value, ('level', 'tile'), pairs)  48.1 us
    pallas_call x5, Pallas kernels, rates(): pl.pallas_call(functools.partial(rates_kernel, step, n_in, n_out), out_sh...  19.5 us
    pallas_call x1, Pallas kernels, cut_history(): pl.pallas_call(cut_history_kernel, grid=(NCOL // 128,), out_shape=[jax.Sh...  9.97 us
    pallas_call x1, Pallas kernels, join(): pl.pallas_call(join_kernel, grid_spec=pltpu.PrefetchScalarGridSpec(num_sc...  6.29 us
    unnamed x10, local copies, waits for them, and re-layouts  4.39 us
  transfers between devices with their start and end apart: 29, of which 20 were waited for; matrix products, arithmetic and copies ran while one was open for 0% of the time, Pallas kernels for 16%

profile of v1, /device:TPU:89, one launch (start us, length us, event | category | flops | bytes accessed | tf_op | source)
XLA Modules:
  0.0 199.7 jit_solution(7626498167947574880)
XLA Ops:
  1.6 2.5 %cut_state.1 = (f32[528,256]{1,0:T(8,128)S(1)}, f32[528,256]{1,0:T(8,128)S(1)}, f32[528,256]{1,0:T(8,128)S(1)}, f32[528,256]{1,0:T(8,128)S(1)}) custom-call(f32[256,2048]{1,0:T(8,128)S(1)} %bitcast.7), custom_call_target="tpu_custom_call" | custom-call | tf_op jit(solution)/shard_map/cut_state/pallas_call | solution.py:138
  5.4 2.5 %collective-permute-start.4 = (f32[528,256]{1,0:T(8,128)S(1)}, f32[528,256]{1,0:T(8,128)S(1)}, u32[]{:S(2)}, u32[]{:S(2)}) collective-permute-start(f32[528,256]{1,0:T(8,128)S(1)} %get-tuple-element.85), channel_id=1, source_target_pairs={{0,32},{1,33},{2,34},{3,35},{4,36},{5,37},{6,38},{7,39},{8,40},{9,... | collective-permute-start | bytes 1622024 | tf_op jit(solution)/shard_map/ppermute | solution.py:63
  9.0 2.8 %copy-done = f32[1,3,16,16,2048]{4,3,2,1,0:T(8,128)S(1)} copy-done((f32[1,3,16,16,2048]{4,3,2,1,0:T(8,128)S(1)}, f32[1,3,16,16,2048]{4,3,2,1,0:T(8,128)}, u32[]{:S(2)}) %copy-start) | copy-done | bytes 6291480
  11.8 10.0 %cut_history.1 = (f32[528,256]{1,0:T(8,128)S(1)}, f32[528,256]{1,0:T(8,128)S(1)}, f32[528,256]{1,0:T(8,128)S(1)}, f32[528,256]{1,0:T(8,128)S(1)}, f32[528,256]{1...) custom-call(f32[3,256,2048]{2,1,0:T(8,128)S(1)} %bitcast.4, ...), custom_call_target="tpu_custom_call" | custom-call | tf_op jit(solution)/shard_map/cut_history/pallas_call | solution.py:152
  24.1 7.0 %collective-permute-done.4.refs_2_.refs_6_ = f32[528,256]{1,0:T(8,128)S(1)} collective-permute-done((f32[528,256]{1,0:T(8,128)S(1)}, f32[528,256]{1,0:T(8,128)S(1)}, u32[]{:S(2)}, u32[]{:S(2)}) %collective-permute-start.4) | collective-permute-done | bytes 540704 | tf_op jit(solution)/shard_map/ppermute | solution.py:63
  31.1 2.5 %collective-permute-start.5 = (f32[528,256]{1,0:T(8,128)S(1)}, f32[528,256]{1,0:T(8,128)S(1)}, u32[]{:S(2)}, u32[]{:S(2)}) collective-permute-start(f32[528,256]{1,0:T(8,128)S(1)} %get-tuple-element.86), channel_id=1, source_target_pairs={{0,32},{1,33},{2,34},{3,35},{4,36},{5,37},{6,38},{7,39},{8,40},{9,... | collective-permute-start | bytes 1622024 | tf_op jit(solution)/shard_map/ppermute | solution.py:63
  33.6 3.8 %collective-permute-start.9 = (f32[528,256]{1,0:T(8,128)S(1)}, f32[528,256]{1,0:T(8,128)S(1)}, u32[]{:S(2)}, u32[]{:S(2)}) collective-permute-start(f32[528,256]{1,0:T(8,128)S(1)} %get-tuple-element.93), channel_id=1, source_target_pairs={{0,48},{1,49},{2,50},{3,51},{4,52},{5,53},{6,54},{7,55},{8,56},{9,... | collective-permute-start | bytes 1622024 | tf_op jit(solution)/shard_map/ppermute | solution.py:63
  43.5 4.9 %collective-permute-done.13.below_ref = f32[528,128]{1,0:T(8,128)S(1)} collective-permute-done((f32[528,128]{1,0:T(8,128)S(1)}, f32[528,128]{1,0:T(8,128)S(1)}, u32[]{:S(2)}, u32[]{:S(2)}) %collective-permute-start.13) | collective-permute-done | bytes 270368 | tf_op jit(solution)/shard_map/ppermute | solution.py:63
  48.4 3.5 %rates_0.1 = (f32[4,528,256]{2,1,0:T(8,128)S(1)}, f32[528,256]{1,0:T(8,128)S(1)}, f32[4,528,256]{2,1,0:T(8,128)S(1)}, f32[4,528,256]{2,1,0:T(8,128)S(1)}, f32[4,528,256]{2,1,0:T(8,128)S(1)}) custom-call(f32[4,528,256]{2,1,0:T(8,128)S(1)} %get-tuple-element.99.u_ref, f32[528,128]{1,0:T(8,128)S(1)} %collective-permute-done.12.above_ref, ...), custom_call_target="tpu_custom_call" | custom-call | tf_op jit(solution)/shard_map/rates_0/pallas_call | solution.py:322
  54.9 2.5 %collective-permute-start.14 = (f32[528,128]{1,0:T(8,128)S(1)}, f32[528,128]{1,0:T(8,128)S(1)}, u32[]{:S(2)}, u32[]{:S(2)}) collective-permute-start(f32[528,128]{1,0:T(8,128)S(1)} %get-tuple-element.108), channel_id=1, source_target_pairs={{0,1},{1,2},{2,3},{3,4},{4,5},{5,6},{6,7},{7,8},{8,9},{9,10},{10,1... | collective-permute-start | bytes 811016 | tf_op jit(solution)/shard_map/ppermute | solution.py:63
  58.7 3.9 %collective-permute-start.10 = (f32[528,256]{1,0:T(8,128)S(1)}, f32[528,256]{1,0:T(8,128)S(1)}, u32[]{:S(2)}, u32[]{:S(2)}) collective-permute-start(f32[528,256]{1,0:T(8,128)S(1)} %get-tuple-element.94), channel_id=1, source_target_pairs={{0,48},{1,49},{2,50},{3,51},{4,52},{5,53},{6,54},{7,55},{8,56},{9,... | collective-permute-start | bytes 1622024 | tf_op jit(solution)/shard_map/ppermute | solution.py:63
  66.8 8.3 %collective-permute-done.15.below_ref = f32[528,128]{1,0:T(8,128)S(1)} collective-permute-done((f32[528,128]{1,0:T(8,128)S(1)}, f32[528,128]{1,0:T(8,128)S(1)}, u32[]{:S(2)}, u32[]{:S(2)}) %collective-permute-start.15) | collective-permute-done | bytes 270368 | tf_op jit(solution)/shard_map/ppermute | solution.py:63
  75.1 4.0 %rates_1.1 = (f32[4,528,256]{2,1,0:T(8,128)S(1)}, f32[528,256]{1,0:T(8,128)S(1)}, f32[4,528,256]{2,1,0:T(8,128)S(1)}, f32[4,528,256]{2,1,0:T(8,128)S(1)}, f32[4,528,256]{2,1,0:T(8,128)S(1)}) custom-call(f32[4,528,256]{2,1,0:T(8,128)S(1)} %get-tuple-element.107.u_ref, f32[528,128]{1,0:T(8,128)S(1)} %collective-permute-done.14.above_ref, ...), custom_call_target="tpu_custom_call" | custom-call | tf_op jit(solution)/shard_map/rates_1/pallas_call | solution.py:322
  79.1 6.9 %collective-permute-done.10.refs_3_.refs_7_ = f32[528,256]{1,0:T(8,128)S(1)} collective-permute-done((f32[528,256]{1,0:T(8,128)S(1)}, f32[528,256]{1,0:T(8,128)S(1)}, u32[]{:S(2)}, u32[]{:S(2)}) %collective-permute-start.10) | collective-permute-done | bytes 540704 | tf_op jit(solution)/shard_map/ppermute | solution.py:63
  90.7 6.4 %collective-permute-start.11 = (f32[528,256]{1,0:T(8,128)S(1)}, f32[528,256]{1,0:T(8,128)S(1)}, u32[]{:S(2)}, u32[]{:S(2)}) collective-permute-start(f32[528,256]{1,0:T(8,128)S(1)} %get-tuple-element.95), channel_id=1, source_target_pairs={{0,48},{1,49},{2,50},{3,51},{4,52},{5,53},{6,54},{7,55},{8,56},{9,... | collective-permute-start | bytes 1622024 | tf_op jit(solution)/shard_map/ppermute | solution.py:63
  101.1 8.3 %collective-permute-done.18.below_ref = f32[528,128]{1,0:T(8,128)S(1)} collective-permute-done((f32[528,128]{1,0:T(8,128)S(1)}, f32[528,128]{1,0:T(8,128)S(1)}, u32[]{:S(2)}, u32[]{:S(2)}) %collective-permute-start.18) | collective-permute-done | bytes 270368 | tf_op jit(solution)/shard_map/ppermute | solution.py:63
  109.3 3.9 %rates_2.1 = (f32[4,528,256]{2,1,0:T(8,128)S(1)}, f32[528,256]{1,0:T(8,128)S(1)}, f32[4,528,256]{2,1,0:T(8,128)S(1)}, f32[4,528,256]{2,1,0:T(8,128)S(1)}) custom-call(f32[4,528,256]{2,1,0:T(8,128)S(1)} %get-tuple-element.116.u_ref, f32[528,128]{1,0:T(8,128)S(1)} %collective-permute-done.17.above_ref, f32[528,128]{1,0:T(8,128)S(1)} %collective-permute-done.18.below_ref, ...), custom_call_target="tpu_custom_call" | custom-call | tf_op jit(solution)/shard_map/rates_2/pallas_call | solution.py:322
  114.1 6.7 %collective-permute-done.11.refs_3_ = f32[528,256]{1,0:T(8,128)S(1)} collective-permute-done((f32[528,256]{1,0:T(8,128)S(1)}, f32[528,256]{1,0:T(8,128)S(1)}, u32[]{:S(2)}, u32[]{:S(2)}) %collective-permute-start.11) | collective-permute-done | bytes 540704 | tf_op jit(solution)/shard_map/ppermute | solution.py:63
  125.6 3.4 %collective-permute-done.20.above_ref = f32[528,128]{1,0:T(8,128)S(1)} collective-permute-done((f32[528,128]{1,0:T(8,128)S(1)}, f32[528,128]{1,0:T(8,128)S(1)}, u32[]{:S(2)}, u32[]{:S(2)}) %collective-permute-start.20) | collective-permute-done | bytes 270368 | tf_op jit(solution)/shard_map/ppermute | solution.py:63
  129.0 4.6 %collective-permute-done.21.below_ref = f32[528,128]{1,0:T(8,128)S(1)} collective-permute-done((f32[528,128]{1,0:T(8,128)S(1)}, f32[528,128]{1,0:T(8,128)S(1)}, u32[]{:S(2)}, u32[]{:S(2)}) %collective-permute-start.21) | collective-permute-done | bytes 270368 | tf_op jit(solution)/shard_map/ppermute | solution.py:63
  133.6 3.8 %rates_3.1 = (f32[4,528,256]{2,1,0:T(8,128)S(1)}, f32[528,256]{1,0:T(8,128)S(1)}, f32[4,528,256]{2,1,0:T(8,128)S(1)}) custom-call(f32[4,528,256]{2,1,0:T(8,128)S(1)} %get-tuple-element.125.u_ref, f32[528,128]{1,0:T(8,128)S(1)} %collective-permute-done.20.above_ref, f32[528,128]{1,0:T(8,128)S(1)} %collective-permute-done.21.below_ref, ...), custom_call_target="tpu_custom_call" | custom-call | tf_op jit(solution)/shard_map/rates_3/pallas_call | solution.py:322
  137.4 9.9 %collective-permute-done.22.refs_6_ = f32[528,256]{1,0:T(8,128)S(1)} collective-permute-done((f32[528,256]{1,0:T(8,128)S(1)}, f32[528,256]{1,0:T(8,128)S(1)}, u32[]{:S(2)}, u32[]{:S(2)}) %collective-permute-start.22) | collective-permute-done | bytes 540704 | tf_op jit(solution)/shard_map/ppermute | solution.py:63
  149.3 2.5 %collective-permute-start.23 = (f32[528,128]{1,0:T(8,128)S(1)}, f32[528,128]{1,0:T(8,128)S(1)}, u32[]{:S(2)}, u32[]{:S(2)}) collective-permute-start(f32[528,128]{1,0:T(8,128)S(1)} %get-tuple-element.134), channel_id=1, source_target_pairs={{0,1},{1,2},{2,3},{3,4},{4,5},{5,6},{6,7},{7,8},{8,9},{9,10},{10,1... | collective-permute-start | bytes 811016 | tf_op jit(solution)/shard_map/ppermute | solution.py:63
  151.8 3.4 %collective-permute-done.23.above_ref = f32[528,128]{1,0:T(8,128)S(1)} collective-permute-done((f32[528,128]{1,0:T(8,128)S(1)}, f32[528,128]{1,0:T(8,128)S(1)}, u32[]{:S(2)}, u32[]{:S(2)}) %collective-permute-start.23) | collective-permute-done | bytes 270368 | tf_op jit(solution)/shard_map/ppermute | solution.py:63
  155.2 4.6 %collective-permute-done.24.below_ref = f32[528,128]{1,0:T(8,128)S(1)} collective-permute-done((f32[528,128]{1,0:T(8,128)S(1)}, f32[528,128]{1,0:T(8,128)S(1)}, u32[]{:S(2)}, u32[]{:S(2)}) %collective-permute-start.24) | collective-permute-done | bytes 270368 | tf_op jit(solution)/shard_map/ppermute | solution.py:63
  159.8 4.3 %rates_4.1 = (f32[4,528,256]{2,1,0:T(8,128)S(1)}, f32[528,256]{1,0:T(8,128)}) custom-call(f32[4,528,256]{2,1,0:T(8,128)S(1)} %get-tuple-element.133.u_ref, f32[528,128]{1,0:T(8,128)S(1)} %collective-permute-done.23.above_ref, f32[528,128]{1,0:T(8,128)S(1)} %collective-permute-done.24.below_ref, bf16[768,512]{1,0:T(8,128)(2,1)S(1)} %get-tuple-element.102.main_ref, ...), custom_call_target="tpu_custom_call" | custom-call | tf_op jit(solution)/shard_map/rates_4/pallas_call | solution.py:322
  164.1 3.0 %collective-permute-done.25.z_ref = f32[528,256]{1,0:T(8,128)S(1)} collective-permute-done((f32[528,256]{1,0:T(8,128)S(1)}, f32[528,256]{1,0:T(8,128)S(1)}, u32[]{:S(2)}, u32[]{:S(2)}) %collective-permute-start.25) | collective-permute-done | bytes 540704 | tf_op jit(solution)/shard_map/ppermute | solution.py:63
  168.4 2.4 %collective-permute-start.28 = (f32[512,256]{1,0:T(8,128)S(1)}, f32[512,256]{1,0:T(8,128)S(1)}, u32[]{:S(2)}, u32[]{:S(2)}) collective-permute-start(f32[512,256]{1,0:T(8,128)S(1)} %get-tuple-element.142), channel_id=1, source_target_pairs={{0,48},{1,49},{2,50},{3,51},{4,52},{5,53},{6,54},{7,55},{8,56},{9,... | collective-permute-start | bytes 1572872 | tf_op jit(solution)/shard_map/ppermute | solution.py:63
  170.8 13.2 %collective-permute-done.26.refs_1_ = f32[512,256]{1,0:T(8,128)S(1)} collective-permute-done((f32[512,256]{1,0:T(8,128)}, f32[512,256]{1,0:T(8,128)S(1)}, u32[]{:S(2)}, u32[]{:S(2)}) %collective-permute-start.26) | collective-permute-done | bytes 524320 | tf_op jit(solution)/shard_map/ppermute | solution.py:63
  184.0 5.5 %collective-permute-done.27.refs_2_ = f32[512,256]{1,0:T(8,128)S(1)} collective-permute-done((f32[512,256]{1,0:T(8,128)S(1)}, f32[512,256]{1,0:T(8,128)S(1)}, u32[]{:S(2)}, u32[]{:S(2)}) %collective-permute-start.27) | collective-permute-done | bytes 524320 | tf_op jit(solution)/shard_map/ppermute | solution.py:63
  189.5 3.9 %collective-permute-done.28.refs_3_ = f32[512,256]{1,0:T(8,128)S(1)} collective-permute-done((f32[512,256]{1,0:T(8,128)S(1)}, f32[512,256]{1,0:T(8,128)S(1)}, u32[]{:S(2)}, u32[]{:S(2)}) %collective-permute-start.28) | collective-permute-done | bytes 524320 | tf_op jit(solution)/shard_map/ppermute | solution.py:63
  193.4 6.3 %join.1 = f32[256,2048]{1,0:T(8,128)} custom-call(s32[1]{0:T(128)} %bitcast.x_ref, f32[512,256]{1,0:T(8,128)S(1)} %get-tuple-element.139.refs_0_, f32[512,256]{1,0:T(8,128)S(1)} %collective-permute-done.26.refs_1_, f32[512,256]{1,0:T(8,128)S(1)} %collective-permute-done.27.refs_2_, f32[512,256]{1,0:T(8,128)S(1)} %collective-permute-done.28.refs_3_), custom_call_target="tpu_custom_call" | custom-call | tf_op jit(solution)/shard_map/join/pallas_call | solution.py:435
  (52 shorter events, 38.4 us)
Async XLA Ops:
  4.1 17.7 %collective-permute-start = (f32[528,256]{1,0:T(8,128)S(1)}, f32[528,256]{1,0:T(8,128)S(1)}, u32[]{:S(2)}, u32[]{:S(2)}) collective-permute-start(f32[528,256]{1,0:T(8,128)S(1)} %get-tuple-element.78), channel_id=1, source_target_pairs={{0,16},{1,17},{2,18},{3,19},{4,20},{5,21},{6,22},{7,23},{8,24},{9,... | collective-permute-start | bytes 1622024 | tf_op jit(solution)/shard_map/ppermute | solution.py:63
  5.4 25.7 %collective-permute-start.4 = (f32[528,256]{1,0:T(8,128)S(1)}, f32[528,256]{1,0:T(8,128)S(1)}, u32[]{:S(2)}, u32[]{:S(2)}) collective-permute-start(f32[528,256]{1,0:T(8,128)S(1)} %get-tuple-element.85), channel_id=1, source_target_pairs={{0,32},{1,33},{2,34},{3,35},{4,36},{5,37},{6,38},{7,39},{8,40},{9,... | collective-permute-start | bytes 1622024 | tf_op jit(solution)/shard_map/ppermute | solution.py:63
  7.8 25.7 %collective-permute-start.8 = (f32[528,256]{1,0:T(8,128)S(1)}, f32[528,256]{1,0:T(8,128)S(1)}, u32[]{:S(2)}, u32[]{:S(2)}) collective-permute-start(f32[528,256]{1,0:T(8,128)S(1)} %get-tuple-element.92), channel_id=1, source_target_pairs={{0,48},{1,49},{2,50},{3,51},{4,52},{5,53},{6,54},{7,55},{8,56},{9,... | collective-permute-start | bytes 1622024 | tf_op jit(solution)/shard_map/ppermute | solution.py:63
  21.8 18.4 %copy-start.4 = (f32[16]{0:T(128)S(1)}, f32[16]{0:T(128)}, u32[]{:S(2)}) copy-start(f32[16]{0:T(128)} %param.7) | copy-start | bytes 196
  21.8 18.3 %copy-start.2 = (f32[16,16]{1,0:T(8,128)S(1)}, f32[16,16]{1,0:T(8,128)}, u32[]{:S(2)}) copy-start(f32[16,16]{1,0:T(8,128)} %lin_ref.1) | copy-start | bytes 3076
  21.8 18.3 %copy-start.3 = (f32[16,16]{1,0:T(8,128)S(1)}, f32[16,16]{1,0:T(8,128)}, u32[]{:S(2)}) copy-start(f32[16,16]{1,0:T(8,128)} %coup_ref.1) | copy-start | bytes 3076
  21.8 30.1 %collective-permute-start.1 = (f32[528,256]{1,0:T(8,128)S(1)}, f32[528,256]{1,0:T(8,128)S(1)}, u32[]{:S(2)}, u32[]{:S(2)}) collective-permute-start(f32[528,256]{1,0:T(8,128)S(1)} %get-tuple-element.79), channel_id=1, source_target_pairs={{0,16},{1,17},{2,18},{3,19},{4,20},{5,21},{6,22},{7,23},{8,24},{9,... | collective-permute-start | bytes 1622024 | tf_op jit(solution)/shard_map/ppermute | solution.py:63
  31.1 23.2 %collective-permute-start.5 = (f32[528,256]{1,0:T(8,128)S(1)}, f32[528,256]{1,0:T(8,128)S(1)}, u32[]{:S(2)}, u32[]{:S(2)}) collective-permute-start(f32[528,256]{1,0:T(8,128)S(1)} %get-tuple-element.86), channel_id=1, source_target_pairs={{0,32},{1,33},{2,34},{3,35},{4,36},{5,37},{6,38},{7,39},{8,40},{9,... | collective-permute-start | bytes 1622024 | tf_op jit(solution)/shard_map/ppermute | solution.py:63
  33.6 20.7 %collective-permute-start.9 = (f32[528,256]{1,0:T(8,128)S(1)}, f32[528,256]{1,0:T(8,128)S(1)}, u32[]{:S(2)}, u32[]{:S(2)}) collective-permute-start(f32[528,256]{1,0:T(8,128)S(1)} %get-tuple-element.93), channel_id=1, source_target_pairs={{0,48},{1,49},{2,50},{3,51},{4,52},{5,53},{6,54},{7,55},{8,56},{9,... | collective-permute-start | bytes 1622024 | tf_op jit(solution)/shard_map/ppermute | solution.py:63
  38.0 5.5 %collective-permute-start.12 = (f32[528,128]{1,0:T(8,128)S(1)}, f32[528,128]{1,0:T(8,128)S(1)}, u32[]{:S(2)}, u32[]{:S(2)}) collective-permute-start(f32[528,128]{1,0:T(8,128)S(1)} %get-tuple-element.100), channel_id=1, source_target_pairs={{0,1},{1,2},{2,3},{3,4},{4,5},{5,6},{6,7},{7,8},{8,9},{9,10},{10,1... | collective-permute-start | bytes 811016 | tf_op jit(solution)/shard_map/ppermute | solution.py:63
  40.1 8.3 %collective-permute-start.13 = (f32[528,128]{1,0:T(8,128)S(1)}, f32[528,128]{1,0:T(8,128)S(1)}, u32[]{:S(2)}, u32[]{:S(2)}) collective-permute-start(f32[528,128]{1,0:T(8,128)S(1)} %get-tuple-element.101), channel_id=1, source_target_pairs={{0,15},{1,0},{2,1},{3,2},{4,3},{5,4},{6,5},{7,6},{8,7},{9,8},{10,9... | collective-permute-start | bytes 811016 | tf_op jit(solution)/shard_map/ppermute | solution.py:63
  54.9 11.6 %collective-permute-start.14 = (f32[528,128]{1,0:T(8,128)S(1)}, f32[528,128]{1,0:T(8,128)S(1)}, u32[]{:S(2)}, u32[]{:S(2)}) collective-permute-start(f32[528,128]{1,0:T(8,128)S(1)} %get-tuple-element.108), channel_id=1, source_target_pairs={{0,1},{1,2},{2,3},{3,4},{4,5},{5,6},{6,7},{7,8},{8,9},{9,10},{10,1... | collective-permute-start | bytes 811016 | tf_op jit(solution)/shard_map/ppermute | solution.py:63
  57.4 21.6 %collective-permute-start.16 = (f32[528,256]{1,0:T(8,128)S(1)}, f32[528,256]{1,0:T(8,128)S(1)}, u32[]{:S(2)}, u32[]{:S(2)}) collective-permute-start(f32[528,256]{1,0:T(8,128)S(1)} %get-tuple-element.115), channel_id=1, source_target_pairs={{0,64},{1,65},{2,66},{3,67},{4,68},{5,69},{6,70},{7,71},{8,72},{9,... | collective-permute-start | bytes 1622024 | tf_op jit(solution)/shard_map/ppermute | solution.py:63
  58.7 27.2 %collective-permute-start.10 = (f32[528,256]{1,0:T(8,128)S(1)}, f32[528,256]{1,0:T(8,128)S(1)}, u32[]{:S(2)}, u32[]{:S(2)}) collective-permute-start(f32[528,256]{1,0:T(8,128)S(1)} %get-tuple-element.94), channel_id=1, source_target_pairs={{0,48},{1,49},{2,50},{3,51},{4,52},{5,53},{6,54},{7,55},{8,56},{9,... | collective-permute-start | bytes 1622024 | tf_op jit(solution)/shard_map/ppermute | solution.py:63
  62.7 23.3 %collective-permute-start.6 = (f32[528,256]{1,0:T(8,128)S(1)}, f32[528,256]{1,0:T(8,128)S(1)}, u32[]{:S(2)}, u32[]{:S(2)}) collective-permute-start(f32[528,256]{1,0:T(8,128)S(1)} %get-tuple-element.87), channel_id=1, source_target_pairs={{0,32},{1,33},{2,34},{3,35},{4,36},{5,37},{6,38},{7,39},{8,40},{9,... | collective-permute-start | bytes 1622024 | tf_op jit(solution)/shard_map/ppermute | solution.py:63
  64.6 23.3 %collective-permute-start.2 = (f32[528,256]{1,0:T(8,128)S(1)}, f32[528,256]{1,0:T(8,128)S(1)}, u32[]{:S(2)}, u32[]{:S(2)}) collective-permute-start(f32[528,256]{1,0:T(8,128)S(1)} %get-tuple-element.80), channel_id=1, source_target_pairs={{0,16},{1,17},{2,18},{3,19},{4,20},{5,21},{6,22},{7,23},{8,24},{9,... | collective-permute-start | bytes 1622024 | tf_op jit(solution)/shard_map/ppermute | solution.py:63
  66.5 8.5 %collective-permute-start.15 = (f32[528,128]{1,0:T(8,128)S(1)}, f32[528,128]{1,0:T(8,128)S(1)}, u32[]{:S(2)}, u32[]{:S(2)}) collective-permute-start(f32[528,128]{1,0:T(8,128)S(1)} %get-tuple-element.109), channel_id=1, source_target_pairs={{0,15},{1,0},{2,1},{3,2},{4,3},{5,4},{6,5},{7,6},{8,7},{9,8},{10,9... | collective-permute-start | bytes 811016 | tf_op jit(solution)/shard_map/ppermute | solution.py:63
  88.7 12.3 %collective-permute-start.17 = (f32[528,128]{1,0:T(8,128)S(1)}, f32[528,128]{1,0:T(8,128)S(1)}, u32[]{:S(2)}, u32[]{:S(2)}) collective-permute-start(f32[528,128]{1,0:T(8,128)S(1)} %get-tuple-element.117), channel_id=1, source_target_pairs={{0,1},{1,2},{2,3},{3,4},{4,5},{5,6},{6,7},{7,8},{8,9},{9,10},{10,1... | collective-permute-start | bytes 811016 | tf_op jit(solution)/shard_map/ppermute | solution.py:63
  89.4 24.7 %collective-permute-start.19 = (f32[528,256]{1,0:T(8,128)S(1)}, f32[528,256]{1,0:T(8,128)S(1)}, u32[]{:S(2)}, u32[]{:S(2)}) collective-permute-start(f32[528,256]{1,0:T(8,128)S(1)} %get-tuple-element.124), channel_id=1, source_target_pairs={{0,64},{1,65},{2,66},{3,67},{4,68},{5,69},{6,70},{7,71},{8,72},{9,... | collective-permute-start | bytes 1622024 | tf_op jit(solution)/shard_map/ppermute | solution.py:63
  90.7 30.1 %collective-permute-start.11 = (f32[528,256]{1,0:T(8,128)S(1)}, f32[528,256]{1,0:T(8,128)S(1)}, u32[]{:S(2)}, u32[]{:S(2)}) collective-permute-start(f32[528,256]{1,0:T(8,128)S(1)} %get-tuple-element.95), channel_id=1, source_target_pairs={{0,48},{1,49},{2,50},{3,51},{4,52},{5,53},{6,54},{7,55},{8,56},{9,... | collective-permute-start | bytes 1622024 | tf_op jit(solution)/shard_map/ppermute | solution.py:63
  97.1 23.7 %collective-permute-start.7 = (f32[528,256]{1,0:T(8,128)S(1)}, f32[528,256]{1,0:T(8,128)S(1)}, u32[]{:S(2)}, u32[]{:S(2)}) collective-permute-start(f32[528,256]{1,0:T(8,128)S(1)} %get-tuple-element.88), channel_id=1, source_target_pairs={{0,32},{1,33},{2,34},{3,35},{4,36},{5,37},{6,38},{7,39},{8,40},{9,... | collective-permute-start | bytes 1622024 | tf_op jit(solution)/shard_map/ppermute | solution.py:63
  99.0 23.7 %collective-permute-start.3 = (f32[528,256]{1,0:T(8,128)S(1)}, f32[528,256]{1,0:T(8,128)S(1)}, u32[]{:S(2)}, u32[]{:S(2)}) collective-permute-start(f32[528,256]{1,0:T(8,128)S(1)} %get-tuple-element.81), channel_id=1, source_target_pairs={{0,16},{1,17},{2,18},{3,19},{4,20},{5,21},{6,22},{7,23},{8,24},{9,... | collective-permute-start | bytes 1622024 | tf_op jit(solution)/shard_map/ppermute | solution.py:63
  101.0 8.4 %collective-permute-start.18 = (f32[528,128]{1,0:T(8,128)S(1)}, f32[528,128]{1,0:T(8,128)S(1)}, u32[]{:S(2)}, u32[]{:S(2)}) collective-permute-start(f32[528,128]{1,0:T(8,128)S(1)} %get-tuple-element.118), channel_id=1, source_target_pairs={{0,15},{1,0},{2,1},{3,2},{4,3},{5,4},{6,5},{7,6},{8,7},{9,8},{10,9... | collective-permute-start | bytes 811016 | tf_op jit(solution)/shard_map/ppermute | solution.py:63
  123.5 23.7 %collective-permute-start.22 = (f32[528,256]{1,0:T(8,128)S(1)}, f32[528,256]{1,0:T(8,128)S(1)}, u32[]{:S(2)}, u32[]{:S(2)}) collective-permute-start(f32[528,256]{1,0:T(8,128)S(1)} %get-tuple-element.132), channel_id=1, source_target_pairs={{0,64},{1,65},{2,66},{3,67},{4,68},{5,69},{6,70},{7,71},{8,72},{9,... | collective-permute-start | bytes 1622024 | tf_op jit(solution)/shard_map/ppermute | solution.py:63
  124.8 4.2 %collective-permute-start.20 = (f32[528,128]{1,0:T(8,128)S(1)}, f32[528,128]{1,0:T(8,128)S(1)}, u32[]{:S(2)}, u32[]{:S(2)}) collective-permute-start(f32[528,128]{1,0:T(8,128)S(1)} %get-tuple-element.126), channel_id=1, source_target_pairs={{0,1},{1,2},{2,3},{3,4},{4,5},{5,6},{6,7},{7,8},{8,9},{9,10},{10,1... | collective-permute-start | bytes 811016 | tf_op jit(solution)/shard_map/ppermute | solution.py:63
  125.6 8.0 %collective-permute-start.21 = (f32[528,128]{1,0:T(8,128)S(1)}, f32[528,128]{1,0:T(8,128)S(1)}, u32[]{:S(2)}, u32[]{:S(2)}) collective-permute-start(f32[528,128]{1,0:T(8,128)S(1)} %get-tuple-element.127), channel_id=1, source_target_pairs={{0,15},{1,0},{2,1},{3,2},{4,3},{5,4},{6,5},{7,6},{8,7},{9,8},{10,9... | collective-permute-start | bytes 811016 | tf_op jit(solution)/shard_map/ppermute | solution.py:63
  148.0 19.1 %collective-permute-start.25 = (f32[528,256]{1,0:T(8,128)S(1)}, f32[528,256]{1,0:T(8,128)S(1)}, u32[]{:S(2)}, u32[]{:S(2)}) collective-permute-start(f32[528,256]{1,0:T(8,128)S(1)} %get-tuple-element.138), channel_id=1, source_target_pairs={{0,64},{1,65},{2,66},{3,67},{4,68},{5,69},{6,70},{7,71},{8,72},{9,... | collective-permute-start | bytes 1622024 | tf_op jit(solution)/shard_map/ppermute | solution.py:63
  149.3 5.9 %collective-permute-start.23 = (f32[528,128]{1,0:T(8,128)S(1)}, f32[528,128]{1,0:T(8,128)S(1)}, u32[]{:S(2)}, u32[]{:S(2)}) collective-permute-start(f32[528,128]{1,0:T(8,128)S(1)} %get-tuple-element.134), channel_id=1, source_target_pairs={{0,1},{1,2},{2,3},{3,4},{4,5},{5,6},{6,7},{7,8},{8,9},{9,10},{10,1... | collective-permute-start | bytes 811016 | tf_op jit(solution)/shard_map/ppermute | solution.py:63
  151.8 8.0 %collective-permute-start.24 = (f32[528,128]{1,0:T(8,128)S(1)}, f32[528,128]{1,0:T(8,128)S(1)}, u32[]{:S(2)}, u32[]{:S(2)}) collective-permute-start(f32[528,128]{1,0:T(8,128)S(1)} %get-tuple-element.135), channel_id=1, source_target_pairs={{0,15},{1,0},{2,1},{3,2},{4,3},{5,4},{6,5},{7,6},{8,7},{9,8},{10,9... | collective-permute-start | bytes 811016 | tf_op jit(solution)/shard_map/ppermute | solution.py:63
  168.2 15.9 %collective-permute-start.26 = (f32[512,256]{1,0:T(8,128)}, f32[512,256]{1,0:T(8,128)S(1)}, u32[]{:S(2)}, u32[]{:S(2)}) collective-permute-start(f32[512,256]{1,0:T(8,128)} %get-tuple-element.140), channel_id=1, source_target_pairs={{0,16},{1,17},{2,18},{3,19},{4,20},{5,21},{6,22},{7,23},{8,24},{9,... | collective-permute-start | bytes 1572872 | tf_op jit(solution)/shard_map/ppermute | solution.py:63
  168.2 21.3 %collective-permute-start.27 = (f32[512,256]{1,0:T(8,128)S(1)}, f32[512,256]{1,0:T(8,128)S(1)}, u32[]{:S(2)}, u32[]{:S(2)}) collective-permute-start(f32[512,256]{1,0:T(8,128)S(1)} %get-tuple-element.141), channel_id=1, source_target_pairs={{0,32},{1,33},{2,34},{3,35},{4,36},{5,37},{6,38},{7,39},{8,40},{9,... | collective-permute-start | bytes 1572872 | tf_op jit(solution)/shard_map/ppermute | solution.py:63
  168.4 24.9 %collective-permute-start.28 = (f32[512,256]{1,0:T(8,128)S(1)}, f32[512,256]{1,0:T(8,128)S(1)}, u32[]{:S(2)}, u32[]{:S(2)}) collective-permute-start(f32[512,256]{1,0:T(8,128)S(1)} %get-tuple-element.142), channel_id=1, source_target_pairs={{0,48},{1,49},{2,50},{3,51},{4,52},{5,53},{6,54},{7,55},{8,56},{9,... | collective-permute-start | bytes 1572872 | tf_op jit(solution)/shard_map/ppermute | solution.py:63
  (2 other events, 4.4 us)

commit v2 on v1

v2 whole, which is shorter than its diff:
```python
import functools

import jax
import jax.numpy as jnp
from jax import lax
from jax.experimental import pallas as pl
from jax.experimental.pallas import tpu as pltpu
from jax.sharding import PartitionSpec as P

SPECIES = 16
ROWS = 16
CELLS = SPECIES * ROWS
HALF = CELLS // 2
NCOL = 2048
RING = 4
CHUNK = NCOL // RING
HALO = 8
WIDE = CHUNK + 2 * HALO
EDGE = 2 * SPECIES
STEP = 0.4
W0, W1, W2, W3 = (1.0 / 24.0, -5.0 / 24.0, 19.0 / 24.0, 9.0 / 24.0)
TAPS = (-1.0 / 12.0, 16.0 / 12.0, -30.0 / 12.0, 16.0 / 12.0, -1.0 / 12.0)
SHIFTS = (1, 3, 2)
PAD = 8

LONG = pl.CostEstimate(flops=10**10, bytes_accessed=10**8, transcendentals=0)

f32 = jnp.float32
bf16 = jnp.bfloat16
dot = functools.partial(jnp.dot, preferred_element_type=f32)


def params(mib=24, **kw):
    return pltpu.CompilerParams(vmem_limit_bytes=mib * 1024 * 1024, **kw)


def vmem():
    return pl.BlockSpec(memory_space=pltpu.VMEM)


def hbm():
    return pl.BlockSpec(memory_space=pl.ANY)


def x_swap(by, skip_last=False):
    pairs = []
    for level in range(8):
        if skip_last and level == 7:
            continue
        for tile in range(16):
            pairs.append((level * 16 + tile, (level ^ by) * 16 + tile))
    return pairs


def z_up():
    return [((x * 16) + t, ((RING + x) * 16) + t) for x in range(RING) for t in range(16)]


def core_swap():
    return [(l * 16 + t, l * 16 + (t ^ 1)) for l in range(8) for t in range(16)]


def chip_swap():
    return [(l * 16 + t, l * 16 + (t + (1 if t % 2 else 15)) % 16) for l in range(8) for t in range(16)]


def send(value, pairs):
    return lax.ppermute(value, ("level", "tile"), pairs)


def send_up(value, pieces):
    rows = value.shape[0] // pieces
    return [send(value[i * rows : (i + 1) * rows], z_up()) for i in range(pieces)]


def my_x():
    return lax.rem(lax.axis_index("level"), RING)


def my_core():
    return lax.rem(lax.axis_index("tile"), 2)


def my_high():
    return lax.div(lax.axis_index("level"), RING)


def turned(read):
    return jnp.concatenate([read(row) for row in range(ROWS)], axis=0).T


def place(scratch, n, value):
    i = pl.program_id(0)
    at = pl.multiple_of(i * 128, 128) + HALO
    scratch[n, pl.ds(pl.multiple_of(at, 8), 128), :] = value

    @pl.when(i == 0)
    def _():
        scratch[n, NCOL + HALO :, :] = value[:HALO]

    @pl.when(i == NCOL // 128 - 1)
    def _():
        scratch[n, :HALO, :] = value[128 - HALO :]


def hand_out(scratch, outs, sem):
    x = my_x()

    @pl.when(pl.program_id(0) == NCOL // 128 - 1)
    def _():
        copies = []
        for k, (n, by, out_ref) in enumerate(outs):
            base = pl.multiple_of(lax.bitwise_xor(x, by) * CHUNK, 128)
            copies.append(pltpu.make_async_copy(scratch.at[n, pl.ds(base, WIDE), :], out_ref, sem.at[k]))
        for copy in copies:
            copy.start()
        for copy in copies:
            copy.wait()


def cut_state_kernel(state_ref, *refs):
    outs, scratch, sem = refs[:RING], *refs[RING:]
    place(scratch, 0, turned(lambda row: state_ref[pl.ds(row, SPECIES, stride=ROWS), :]))
    hand_out(scratch, [(0, by, out_ref) for by, out_ref in enumerate(outs)], sem)


def cut_history_kernel(older_ref, middle_ref, newest_ref, *refs):
    pairs, lasts, (scratch, sem) = refs[:RING], refs[RING : 2 * RING], refs[2 * RING :]

    def parts(row):
        rows = pl.ds(row, SPECIES, stride=ROWS)
        return older_ref[0, rows, :], middle_ref[0, rows, :], newest_ref[0, rows, :]

    def first(row):
        p, q, r = parts(row)
        return STEP * (W0 * p + W1 * q + (W2 - 1.0) * r)

    def second(row):
        _, q, r = parts(row)
        return STEP * (W0 * q + W1 * r)

    def third(row):
        return (STEP * W0) * parts(row)[2]

    for n, read in enumerate((first, second, third)):
        place(scratch, n, turned(read))
    pieces = [(n, by, pairs[by].at[n * WIDE : (n + 1) * WIDE]) for n in range(2) for by in range(RING)]
    hand_out(scratch, pieces + [(2, by, lasts[by]) for by in range(RING)], sem)


def cut_state(state):
    return pl.pallas_call(
        cut_state_kernel,
        grid=(NCOL // 128,),
        out_shape=[jax.ShapeDtypeStruct((WIDE, CELLS), f32)] * RING,
        in_specs=[pl.BlockSpec((CELLS, 128), lambda i: (0, i))],
        out_specs=[hbm()] * RING,
        scratch_shapes=[pltpu.VMEM((1, NCOL + 2 * HALO, CELLS), f32), pltpu.SemaphoreType.DMA((RING,))],
        compiler_params=params(),
        name="cut_state",
    )(state)


def cut_history(hist):
    part = lambda n: pl.BlockSpec((1, CELLS, 128), lambda i: (n, 0, i))
    return pl.pallas_call(
        cut_history_kernel,
        grid=(NCOL // 128,),
        out_shape=[jax.ShapeDtypeStruct((2 * WIDE, CELLS), f32)] * RING
        + [jax.ShapeDtypeStruct((WIDE, CELLS), f32)] * RING,
        in_specs=[part(0), part(1), part(2)],
        out_specs=[hbm()] * (2 * RING),
        scratch_shapes=[pltpu.VMEM((3, NCOL + 2 * HALO, CELLS), f32), pltpu.SemaphoreType.DMA((3 * RING,))],
        compiler_params=params(),
        name="cut_history",
    )(hist, hist, hist)


def update_kernel(step, starts, pieces, *refs):
    refs = list(refs)
    take = lambda n: [refs.pop(0) for _ in range(n)]
    new_field = take(RING) if step < 4 else None
    old_field = take(RING) if step > 0 else None
    piece = lambda field, k: field[starts[k] : starts[k] + WIDE, :]
    y_ref, g_ref = take(2) if step > 0 else (None, None)
    z_refs = take(pieces) if step > 1 else None
    u_ref, inner_ref, outer_ref = take(3)
    pay_ref = take(1)[0] if 0 < step < 4 else None
    x, high = my_x(), my_high()
    level_of = lambda by: lax.bitwise_xor(x, by)

    def plain(field, k):
        for by in range(RING):
            u_ref[level_of(by)] = piece(field[by], k)

    def added(field, k, with_pay):
        for by in range(RING):
            level = level_of(by)

            @pl.when(level < RING - 1)
            def _(by=by, level=level):
                u_ref[level + 1] = y_ref[level + 1] + piece(field[by], k)

            if with_pay:

                @pl.when(level == RING - 1)
                def _(by=by):
                    pay_ref[...] = g_ref[...] + piece(field[by], k)

    @pl.when(high == 0)
    def _():
        if step == 0:
            plain(new_field, 0)
        elif step < 4:
            u_ref[0] = y_ref[0]
            added(new_field, 0, True)
        else:
            u_ref[...] = y_ref[...]

    @pl.when(high == 1)
    def _():
        if step == 0:
            u_ref[...] = jnp.zeros_like(u_ref)
        elif step == 1:
            plain(old_field, 1)
        else:
            for i, z_ref in enumerate(z_refs):
                rows = slice(i * (WIDE // pieces), (i + 1) * (WIDE // pieces))
                u_ref[0, rows, :] = y_ref[0, rows, :] + z_ref[...]
            added(old_field, 1, False)
        if 0 < step < 4:
            pay_ref[...] = jnp.zeros_like(pay_ref)

    lane = lax.broadcasted_iota(jnp.int32, (WIDE, HALF), 1)
    down = up = None
    for level in range(RING):
        here = (lane >= level * EDGE) & (lane < (level + 1) * EDGE)
        top = u_ref[level, :, :HALF]
        bottom = u_ref[level, :, HALF:]
        top = pltpu.roll(top, level * EDGE, 1) if level else top
        bottom = pltpu.roll(bottom, (level + 1) * EDGE, 1) if level < RING - 1 else bottom
        down = top if level == 0 else jnp.where(here, top, down)
        up = bottom if level == 0 else jnp.where(here, bottom, up)
    first_core = my_core() == 0
    inner_ref[...] = jnp.where(first_core, up, down)
    outer_ref[...] = jnp.where(first_core, down, up)


def update(step, new_field, old_field, y, g, z):
    operands, starts = [], [0, 0]
    if step < 4:
        operands += new_field[0]
        starts[0] = new_field[1]
    if step > 0:
        operands += old_field[0] + [y, g]
        starts[1] = old_field[1]
    if step > 1:
        operands += z
    outs = [pltpu.VMEM((RING, WIDE, CELLS), f32)] + [jax.ShapeDtypeStruct((WIDE, HALF), f32)] * 2
    if 0 < step < 4:
        outs.append(jax.ShapeDtypeStruct((WIDE, CELLS), f32))
    return pl.pallas_call(
        functools.partial(update_kernel, step, starts, len(z) if z else 0),
        out_shape=outs,
        in_specs=[vmem()] * len(operands),
        out_specs=[vmem()] * len(outs),
        cost_estimate=LONG,
        compiler_params=params(),
        name=f"update_{step}",
    )(*operands)


def split(into, at, value):
    high_part = value.astype(bf16)
    width = value.shape[1]
    into[:, at : at + width] = high_part
    into[:, CELLS + at : CELLS + at + width] = (value - high_part.astype(f32)).astype(bf16)
    into[:, 2 * CELLS + at : 2 * CELLS + at + width] = high_part


def unless_done(step, work):
    if step < 4:
        work()
    else:
        pl.when(my_high() == 1)(work)


def inner_kernel(step, u_ref, main_ref, diff_ref, rate_ref, padded, stack):
    def work():
        padded[:, :PAD, :] = jnp.zeros((2, PAD, HALF), f32)
        padded[:, PAD + WIDE :, :] = jnp.zeros((2, PAD, HALF), f32)
        for level in range(RING):
            for side in range(2):
                part = u_ref[level, :, side * HALF : (side + 1) * HALF]
                padded[side, PAD : PAD + WIDE, :] = part
                split(stack, side * HALF, part)
            products = dot(stack[...], main_ref[...])
            for side in range(2):
                at = slice(side * HALF, (side + 1) * HALF)
                diff = diff_ref[0:1, at]
                for begin in range(0, WIDE, 48):
                    rows = slice(begin, begin + 48)
                    moved = lambda by: padded[side, PAD + begin + by : PAD + begin + by + 48, :]
                    u = moved(0)
                    near = moved(-1) + moved(1)
                    far = moved(-2) + moved(2)
                    rate = products[rows, at] + diff * (16.0 * near - far)
                    rate = rate + jnp.tanh(products[rows, CELLS + side * HALF : CELLS + (side + 1) * HALF])
                    rate_ref[level, rows, at] = rate - u * u * u * (1.0 / 3.0)

    unless_done(step, work)


def inner_rates(step, u, weights):
    main, _, diff = weights
    return pl.pallas_call(
        functools.partial(inner_kernel, step),
        out_shape=pltpu.VMEM((RING, WIDE, CELLS), f32),
        in_specs=[vmem()] * 3,
        out_specs=vmem(),
        scratch_shapes=[pltpu.VMEM((2, WIDE + 2 * PAD, HALF), f32), pltpu.VMEM((WIDE, 3 * CELLS), bf16)],
        compiler_params=params(),
        name=f"inner_{step}",
    )(u, main, diff)


def rates_kernel(step, n_in, n_out, u_ref, rate_ref, inner_ref, outer_ref, edge_ref, *refs):
    older = refs[:n_in]
    y_ref, g_ref = refs[n_in : n_in + 2]
    newer = refs[n_in + 2 : n_in + 2 + n_out]
    stack, edges = refs[n_in + 2 + n_out :]

    def work():
        first_core = my_core() == 0
        split(stack, 0, jnp.where(first_core, outer_ref[...], inner_ref[...]))
        split(stack, HALF, jnp.where(first_core, inner_ref[...], outer_ref[...]))
        edges[...] = dot(stack[...], edge_ref[...])
        lane = lax.broadcasted_iota(jnp.int32, (48, HALF), 1)
        for side in range(2):
            at = slice(side * HALF, (side + 1) * HALF)
            near_edge = lane >= HALF - EDGE if side else lane < EDGE
            for begin in range(0, WIDE, 48):
                rows = slice(begin, begin + 48)
                below = None
                for level in range(RING):
                    turn = (HALF - EDGE - level * EDGE if side else HALF - level * EDGE) % HALF
                    edge = edges[rows, at]
                    edge = pltpu.roll(edge, turn, 1) if turn else edge
                    scaled = STEP * (rate_ref[level, rows, at] + jnp.where(near_edge, edge, 0.0))
                    y = u_ref[level, rows, at] + scaled
                    y_ref[level, rows, at] = y if below is None else y + below
                    below = W3 * scaled
                    if n_in > 0:
                        below = below + older[0][level, rows, at]
                    for k, weight in zip(range(n_out), (W2 - 1.0, W1, W0)):
                        value = weight * scaled
                        if k + 1 < n_in:
                            value = value + older[k + 1][level, rows, at]
                        newer[k][level, rows, at] = value
                g_ref[rows, at] = below

    unless_done(step, work)
    if step == 4:

        @pl.when(my_high() == 0)
        def _():
            y_ref[...] = u_ref[...]
            g_ref[...] = jnp.zeros_like(g_ref)


def rates(step, u, rate, inner, outer, weights, older, n_out):
    n_in = len(older)
    full = pltpu.VMEM((RING, WIDE, CELLS), f32)
    outs = pl.pallas_call(
        functools.partial(rates_kernel, step, n_in, n_out),
        out_shape=[full, pltpu.VMEM((WIDE, CELLS), f32)] + [full] * n_out,
        in_specs=[vmem()] * (5 + n_in),
        out_specs=[vmem()] * (2 + n_out),
        scratch_shapes=[pltpu.VMEM((WIDE, 3 * CELLS), bf16), pltpu.VMEM((WIDE, CELLS), f32)],
        compiler_params=params(),
        name=f"rates_{step}",
    )(u, rate, inner, outer, weights[1], *older)
    return outs[0], outs[1], list(outs[2:])


def weights_kernel(lin_ref, coup_ref, diff_ref, main_ref, edge_ref, diff_out):
    exact = functools.partial(lax.dot_general, precision=lax.Precision.HIGHEST, preferred_element_type=f32)
    last = (((1,), (1,)), ((), ()))
    iota = lambda shape, dim: lax.broadcasted_iota(jnp.int32, shape, dim)
    pick = (iota((CELLS, SPECIES), 0) % SPECIES == iota((CELLS, SPECIES), 1)).astype(f32)
    source, target = iota((CELLS, CELLS), 0), iota((CELLS, CELLS), 1)
    same_row = source // SPECIES == target // SPECIES
    same_species = source % SPECIES == target % SPECIES
    diffusion = exact(diff_ref[...], pick, last)

    def tiled(matrix):
        return jnp.where(same_row, exact(exact(pick, matrix, last), pick, last), 0.0)

    def stencil(offset, middle):
        value = jnp.where(offset == 0, middle, 0.0)
        value = value + jnp.where((offset == 1) | (offset == -1), TAPS[1], 0.0)
        return value + jnp.where((offset == 2) | (offset == -2), TAPS[0], 0.0)

    def put(into, at, value):
        high_part = value.astype(bf16)
        into[:CELLS, at : at + CELLS] = high_part
        into[CELLS : 2 * CELLS, at : at + CELLS] = high_part
        into[2 * CELLS :, at : at + CELLS] = (value - high_part.astype(f32)).astype(bf16)

    offset = source // SPECIES - target // SPECIES
    spread = jnp.where(same_species, stencil(offset, 2.0 * TAPS[2]) * diffusion[0:1], 0.0)
    put(main_ref, 0, tiled(lin_ref[...]) + spread)
    put(main_ref, CELLS, tiled(coup_ref[...]))
    row_from = (source // SPECIES) % 2 + jnp.where(source < HALF, -2, ROWS)
    row_to = (target // SPECIES) % 2 + jnp.where(target < HALF, 0, ROWS - 2)
    alike = same_species & (source // EDGE == target // EDGE)
    put(edge_ref, 0, jnp.where(alike, stencil(row_from - row_to, 0.0) * diffusion[0:1], 0.0))
    diff_out[...] = diffusion * (1.0 / 12.0)


def make_weights(diffusion, linear_rates, coupling):
    return pl.pallas_call(
        weights_kernel,
        out_shape=[
            pltpu.VMEM((3 * CELLS, 2 * CELLS), bf16),
            pltpu.VMEM((3 * CELLS, CELLS), bf16),
            pltpu.VMEM((8, CELLS), f32),
        ],
        in_specs=[vmem()] * 3,
        out_specs=[vmem()] * 3,
        compiler_params=params(),
        name="weights",
    )(linear_rates, coupling, jnp.broadcast_to(diffusion[None], (8, SPECIES)))


def finish_kernel(y_ref, z_ref, *outs):
    x, high = my_x(), my_high()
    inner = slice(HALO, HALO + CHUNK)
    for by, out_ref in enumerate(outs):
        level = lax.bitwise_xor(x, by)
        takes = (level == 0) & (high == 1)

        @pl.when(takes)
        def _(out_ref=out_ref):
            out_ref[...] = y_ref[0, inner, :] + z_ref[inner, :]

        @pl.when(jnp.logical_not(takes))
        def _(out_ref=out_ref, level=level):
            out_ref[...] = y_ref[level, inner, :]


def finish(y, z):
    return pl.pallas_call(
        finish_kernel,
        out_shape=[jax.ShapeDtypeStruct((CHUNK, CELLS), f32)] * RING,
        in_specs=[vmem(), vmem()],
        out_specs=[vmem()] * RING,
        compiler_params=params(),
        name="finish",
    )(y, z)


def join_kernel(*refs):
    parts, (out_ref, turn, whole, sem) = refs[:RING], refs[RING:]
    x = my_x()
    copies = []
    for half in range(2):
        for by, part in enumerate(parts):
            base = lax.bitwise_xor(x, by) * CHUNK
            for i in range(CHUNK // 128):
                slot = by * (CHUNK // 128) + i
                turn[slot] = part[i * 128 : (i + 1) * 128, half * HALF : (half + 1) * HALF].T
                columns = pl.ds(pl.multiple_of(base + i * 128, 128), 128)
                for species in range(SPECIES):
                    whole[half, species, :, columns] = turn[slot, pl.ds(species, ROWS // 2, stride=SPECIES), :]
        target = out_ref.at[:, half * (ROWS // 2) : (half + 1) * (ROWS // 2), :]
        copies.append(pltpu.make_async_copy(whole.at[half], target, sem.at[half]))
        copies[-1].start()
    for copy in copies:
        copy.wait()


def join(parts):
    return pl.pallas_call(
        join_kernel,
        out_shape=jax.ShapeDtypeStruct((SPECIES, ROWS, NCOL), f32),
        in_specs=[vmem()] * RING,
        out_specs=hbm(),
        scratch_shapes=[
            pltpu.VMEM((NCOL // 128, HALF, 128), f32),
            pltpu.VMEM((2, SPECIES, ROWS // 2, NCOL), f32),
            pltpu.SemaphoreType.DMA((2,)),
        ],
        compiler_params=params(),
        name="join",
    )(*parts)


def after(value, *earlier):
    return lax.optimization_barrier((value, *earlier))[0]


def exchange(parts, skip_last=False):
    got = [parts[0], None, None, None]
    for by in SHIFTS:
        got[by] = send(parts[by], x_swap(by, skip_last))
    return got


def local(level_state, history, diffusion, linear_rates, coupling):
    state = level_state.reshape(CELLS, NCOL)
    hist = history.reshape(3, CELLS, NCOL)
    weights = make_weights(diffusion, linear_rates, coupling)
    cut = cut_history(hist)
    first = exchange(cut_state(state))
    pair = exchange([after(part, *first[1:]) for part in cut[:RING]], True)
    last = [after(part, *pair[1:]) for part in cut[RING:]]
    got = {by: send(last[by], x_swap(by, True)) for by in (1, 3)}
    got[2] = send(after(last[2], got[1], got[3]), x_swap(2, True))
    last = [last[0], got[1], got[2], got[3]]
    fields = [(first, 0), (pair, 0), (pair, WIDE), (last, 0)]

    y = g = z = None
    older = []
    n_outs = (3, 3, 2, 1, 0)
    for step in range(5):
        new_field = fields[step] if step < 4 else None
        old_field = fields[step - 1] if step > 0 else None
        if step == 2:
            y = after(y, last[1], last[3])
        u, inner, outer, *pay = update(step, new_field, old_field, y, g, z)
        outer = send(outer, chip_swap())
        inner = send(inner, core_swap())
        if pay:
            z = send_up(pay[0], 1)
        if step == 2:
            u = after(u, last[2])
        rate = inner_rates(step, u, weights)
        y, g, older = rates(step, u, rate, inner, outer, weights, older, n_outs[step])
        if step == 3:
            z_last = send_up(g, 1)
    parts = finish(y, z_last[0])
    return join(exchange(parts))[None]


def solution(mesh):
    placed = (P("level", None, "tile", None), P("level", None, None, "tile", None), P(), P(), P())
    return jax.shard_map(
        local, mesh=mesh, in_specs=placed, out_specs=P("level", None, "tile", None), check_vma=False
    )
```

time: 202 us -> 196 us (0.970)
  Pallas kernels: 43.9 us -> 38.4 us
  waiting for transfers between devices: 103 us -> 98.8 us
  starting transfers between devices: 48.1 us -> 51.7 us
    pallas_call x5, Pallas kernels: 19.5 us -> 6.2 us  [rates(): pl.pallas_call(functools.partial(rates_kernel, step, n_in, n_out), out_sh...]
    pallas_call x6 -> x11, Pallas kernels: 9.96 us -> 18.7 us  [the longest x5 13.1 us: inner_rates(): pl.pallas_call(functools.partial(inner_kernel, step), out_shape=pltpu.VME...]
    ppermute x29 -> x26, waiting for transfers between devices: 103 us -> 98.8 us  [send(): return lax.ppermute(value, ('level', 'tile'), pairs)]
    ppermute x29 -> x26, starting transfers between devices: 48.1 us -> 51.7 us  [send(): return lax.ppermute(value, ('level', 'tile'), pairs)]
    unnamed x10 -> x18, local copies, waits for them, and re-layouts: 4.39 us -> 4.41 us
  transfers between devices with their start and end apart: 29 -> 26, of which waited for: 20 -> 15; matrix products, arithmetic and copies ran while one was open for 0% -> 0% of each run, Pallas kernels for 16% -> 17%
where the time goes in v2:
time: 196 us; the launch traced here: 194 us
  waiting for transfers between devices  98.8 us (50%)
  starting transfers between devices  51.7 us (26%)
  Pallas kernels  38.4 us (20%)
  local copies, waits for them, and re-layouts  4.41 us (2%)
    ppermute x26, waiting for transfers between devices, send(): return lax.ppermute(value, ('level', 'tile'), pairs)  98.8 us
    ppermute x26, starting transfers between devices, send(): return lax.ppermute(value, ('level', 'tile'), pairs)  51.7 us
    pallas_call x5, Pallas kernels, inner_rates(): pl.pallas_call(functools.partial(inner_kernel, step), out_shape=pltpu.VME...  13.1 us
    pallas_call x1, Pallas kernels, cut_history(): pl.pallas_call(cut_history_kernel, grid=(NCOL // 128,), out_shape=[jax.Sh...  9.9 us
    pallas_call x5, Pallas kernels, rates(): pl.pallas_call(functools.partial(rates_kernel, step, n_in, n_out), out_sh...  6.2 us
    unnamed x18, local copies, waits for them, and re-layouts  4.41 us
  transfers between devices with their start and end apart: 26, of which 15 were waited for; matrix products, arithmetic and copies ran while one was open for 0% of the time, Pallas kernels for 17%

profile of v2, /device:TPU:89, one launch (start us, length us, event | category | flops | bytes accessed | tf_op | source)
XLA Modules:
  0.0 193.8 jit_solution(10561644095993252244)
XLA Ops:
  1.6 2.5 %cut_state.1 = (f32[528,256]{1,0:T(8,128)S(1)}, f32[528,256]{1,0:T(8,128)S(1)}, f32[528,256]{1,0:T(8,128)S(1)}, f32[528,256]{1,0:T(8,128)S(1)}) custom-call(f32[256,2048]{1,0:T(8,128)S(1)} %bitcast.6), custom_call_target="tpu_custom_call" | custom-call | tf_op jit(solution)/shard_map/cut_state/pallas_call | solution.py:152
  5.4 2.5 %collective-permute-start.1 = (f32[528,256]{1,0:T(8,128)S(1)}, f32[528,256]{1,0:T(8,128)S(1)}, u32[]{:S(2)}, u32[]{:S(2)}) collective-permute-start(f32[528,256]{1,0:T(8,128)S(1)} %get-tuple-element.74), channel_id=1, source_target_pairs={{0,32},{1,33},{2,34},{3,35},{4,36},{5,37},{6,38},{7,39},{8,40},{9,... | collective-permute-start | bytes 1622024 | tf_op jit(solution)/shard_map/ppermute | solution.py:68
  8.0 2.8 %copy-done = f32[1,3,16,16,2048]{4,3,2,1,0:T(8,128)S(1)} copy-done((f32[1,3,16,16,2048]{4,3,2,1,0:T(8,128)S(1)}, f32[1,3,16,16,2048]{4,3,2,1,0:T(8,128)}, u32[]{:S(2)}) %copy-start) | copy-done | bytes 6291480
  10.8 9.9 %cut_history.1 = (f32[1056,256]{1,0:T(8,128)S(1)}, f32[1056,256]{1,0:T(8,128)S(1)}, f32[1056,256]{1,0:T(8,128)S(1)}, f32[1056,256]{1,0:T(8,128)S(1)}, f32[528,25...) custom-call(f32[3,256,2048]{2,1,0:T(8,128)S(1)} %bitcast.3, ...), custom_call_target="tpu_custom_call" | custom-call | tf_op jit(solution)/shard_map/cut_history/pallas_call | solution.py:166
  20.8 10.4 %collective-permute-done.1.refs_2_.refs_6_ = f32[528,256]{1,0:T(8,128)S(1)} collective-permute-done((f32[528,256]{1,0:T(8,128)S(1)}, f32[528,256]{1,0:T(8,128)S(1)}, u32[]{:S(2)}, u32[]{:S(2)}) %collective-permute-start.1) | collective-permute-done | bytes 540704 | tf_op jit(solution)/shard_map/ppermute | solution.py:68
  31.1 2.0 %collective-permute-done.2.refs_3_.refs_7_ = f32[528,256]{1,0:T(8,128)S(1)} collective-permute-done((f32[528,256]{1,0:T(8,128)S(1)}, f32[528,256]{1,0:T(8,128)S(1)}, u32[]{:S(2)}, u32[]{:S(2)}) %collective-permute-start.2) | collective-permute-done | bytes 540704 | tf_op jit(solution)/shard_map/ppermute | solution.py:68
  33.2 2.2 %collective-permute-start.5 = (f32[1056,256]{1,0:T(8,128)S(1)}, f32[1056,256]{1,0:T(8,128)S(1)}, u32[]{:S(2)}, u32[]{:S(2)}) collective-permute-start(f32[1056,256]{1,0:T(8,128)S(1)} %get-tuple-element.80), channel_id=1, source_target_pairs={{0,48},{1,49},{2,50},{3,51},{4,52},{5,53},{6,54},{7,55},{8,56},{9,... | collective-permute-start | bytes 3244040 | tf_op jit(solution)/shard_map/ppermute | solution.py:68
  39.9 3.0 %collective-permute-start.9 = (f32[528,128]{1,0:T(8,128)S(1)}, f32[528,128]{1,0:T(8,128)S(1)}, u32[]{:S(2)}, u32[]{:S(2)}) collective-permute-start(f32[528,128]{1,0:T(8,128)S(1)} %get-tuple-element.95), channel_id=1, source_target_pairs={{0,1},{1,0},{2,3},{3,2},{4,5},{5,4},{6,7},{7,6},{8,9},{9,8},{10,11... | collective-permute-start | bytes 811016 | tf_op jit(solution)/shard_map/ppermute | solution.py:68
  44.9 2.6 %inner_0.1.rate_ref = f32[4,528,256]{2,1,0:T(8,128)S(1)} custom-call(f32[4,528,256]{2,1,0:T(8,128)S(1)} %get-tuple-element.92.u_ref, bf16[768,512]{1,0:T(8,128)(2,1)S(1)} %get-tuple-element.93.main_ref, f32[8,256]{1,0:T(8,128)S(1)} %get-tuple-element.94.diff_ref), custom_call_target="tpu_custom_call" | custom-call | tf_op jit(solution)/shard_map/inner_0/pallas_call | solution.py:316
  47.5 3.7 %collective-permute-done.10.outer_ref = f32[528,128]{1,0:T(8,128)S(1)} collective-permute-done((f32[528,128]{1,0:T(8,128)S(1)}, f32[528,128]{1,0:T(8,128)S(1)}, u32[]{:S(2)}, u32[]{:S(2)}) %collective-permute-start.10) | collective-permute-done | bytes 270368 | tf_op jit(solution)/shard_map/ppermute | solution.py:68
  52.4 28.0 %collective-permute-done.5.refs_3_.refs_7_ = f32[1056,256]{1,0:T(8,128)S(1)} collective-permute-done((f32[1056,256]{1,0:T(8,128)S(1)}, f32[1056,256]{1,0:T(8,128)S(1)}, u32[]{:S(2)}, u32[]{:S(2)}) %collective-permute-start.5) | collective-permute-done | bytes 1081376 | tf_op jit(solution)/shard_map/ppermute | solution.py:68
  82.1 3.0 %collective-permute-start.6 = (f32[528,256]{1,0:T(8,128)S(1)}, f32[528,256]{1,0:T(8,128)S(1)}, u32[]{:S(2)}, u32[]{:S(2)}) collective-permute-start(f32[528,256]{1,0:T(8,128)S(1)} %get-tuple-element.83), channel_id=1, source_target_pairs={{0,16},{1,17},{2,18},{3,19},{4,20},{5,21},{6,22},{7,23},{8,24},{9,... | collective-permute-start | bytes 1622024 | tf_op jit(solution)/shard_map/ppermute | solution.py:68
  85.1 3.3 %collective-permute-start.7 = (f32[528,256]{1,0:T(8,128)S(1)}, f32[528,256]{1,0:T(8,128)S(1)}, u32[]{:S(2)}, u32[]{:S(2)}) collective-permute-start(f32[528,256]{1,0:T(8,128)S(1)} %get-tuple-element.87), channel_id=1, source_target_pairs={{0,48},{1,49},{2,50},{3,51},{4,52},{5,53},{6,54},{7,55},{8,56},{9,... | collective-permute-start | bytes 1622024 | tf_op jit(solution)/shard_map/ppermute | solution.py:68
  90.3 3.7 %collective-permute-start.11 = (f32[528,128]{1,0:T(8,128)S(1)}, f32[528,128]{1,0:T(8,128)S(1)}, u32[]{:S(2)}, u32[]{:S(2)}) collective-permute-start(f32[528,128]{1,0:T(8,128)S(1)} %get-tuple-element.101), channel_id=1, source_target_pairs={{0,1},{1,0},{2,3},{3,2},{4,5},{5,4},{6,7},{7,6},{8,9},{9,8},{10,11... | collective-permute-start | bytes 811016 | tf_op jit(solution)/shard_map/ppermute | solution.py:68
  95.2 2.6 %inner_1.1.rate_ref = f32[4,528,256]{2,1,0:T(8,128)S(1)} custom-call(f32[4,528,256]{2,1,0:T(8,128)S(1)} %get-tuple-element.100.u_ref, bf16[768,512]{1,0:T(8,128)(2,1)S(1)} %get-tuple-element.93.main_ref, f32[8,256]{1,0:T(8,128)S(1)} %get-tuple-element.94.diff_ref), custom_call_target="tpu_custom_call" | custom-call | tf_op jit(solution)/shard_map/inner_1/pallas_call | solution.py:316
  97.9 4.2 %collective-permute-done.12.outer_ref = f32[528,128]{1,0:T(8,128)S(1)} collective-permute-done((f32[528,128]{1,0:T(8,128)S(1)}, f32[528,128]{1,0:T(8,128)S(1)}, u32[]{:S(2)}, u32[]{:S(2)}) %collective-permute-start.12) | collective-permute-done | bytes 270368 | tf_op jit(solution)/shard_map/ppermute | solution.py:68
  103.4 3.7 %collective-permute-start.8 = (f32[528,256]{1,0:T(8,128)S(1)}, f32[528,256]{1,0:T(8,128)S(1)}, u32[]{:S(2)}, u32[]{:S(2)}) collective-permute-start(f32[528,256]{1,0:T(8,128)S(1)} %get-tuple-element.88), channel_id=1, source_target_pairs={{0,32},{1,33},{2,34},{3,35},{4,36},{5,37},{6,38},{7,39},{8,40},{9,... | collective-permute-start | bytes 1622024 | tf_op jit(solution)/shard_map/ppermute | solution.py:68
  109.3 2.9 %collective-permute-start.14 = (f32[528,128]{1,0:T(8,128)S(1)}, f32[528,128]{1,0:T(8,128)S(1)}, u32[]{:S(2)}, u32[]{:S(2)}) collective-permute-start(f32[528,128]{1,0:T(8,128)S(1)} %get-tuple-element.112), channel_id=1, source_target_pairs={{0,1},{1,0},{2,3},{3,2},{4,5},{5,4},{6,7},{7,6},{8,9},{9,8},{10,11... | collective-permute-start | bytes 811016 | tf_op jit(solution)/shard_map/ppermute | solution.py:68
  113.2 6.2 %collective-permute-done.8.refs_2_ = f32[528,256]{1,0:T(8,128)S(1)} collective-permute-done((f32[528,256]{1,0:T(8,128)S(1)}, f32[528,256]{1,0:T(8,128)S(1)}, u32[]{:S(2)}, u32[]{:S(2)}) %collective-permute-start.8) | collective-permute-done | bytes 540704 | tf_op jit(solution)/shard_map/ppermute | solution.py:68
  119.4 2.6 %inner_2.1.rate_ref = f32[4,528,256]{2,1,0:T(8,128)S(1)} custom-call(f32[4,528,256]{2,1,0:T(8,128)S(1)} %get-tuple-element.111.u_ref, bf16[768,512]{1,0:T(8,128)(2,1)S(1)} %get-tuple-element.93.main_ref, f32[8,256]{1,0:T(8,128)S(1)} %get-tuple-element.94.diff_ref), custom_call_target="tpu_custom_call" | custom-call | tf_op jit(solution)/shard_map/inner_2/pallas_call | solution.py:316
  123.2 2.8 %collective-permute-done.16.refs_10_ = f32[528,256]{1,0:T(8,128)S(1)} collective-permute-done((f32[528,256]{1,0:T(8,128)S(1)}, f32[528,256]{1,0:T(8,128)S(1)}, u32[]{:S(2)}, u32[]{:S(2)}) %collective-permute-start.16) | collective-permute-done | bytes 540704 | tf_op jit(solution)/shard_map/ppermute | solution.py:68
  128.2 3.4 %collective-permute-start.17 = (f32[528,128]{1,0:T(8,128)S(1)}, f32[528,128]{1,0:T(8,128)S(1)}, u32[]{:S(2)}, u32[]{:S(2)}) collective-permute-start(f32[528,128]{1,0:T(8,128)S(1)} %get-tuple-element.121), channel_id=1, source_target_pairs={{0,1},{1,0},{2,3},{3,2},{4,5},{5,4},{6,7},{7,6},{8,9},{9,8},{10,11... | collective-permute-start | bytes 811016 | tf_op jit(solution)/shard_map/ppermute | solution.py:68
  131.6 2.6 %inner_3.1.rate_ref = f32[4,528,256]{2,1,0:T(8,128)S(1)} custom-call(f32[4,528,256]{2,1,0:T(8,128)S(1)} %get-tuple-element.120.u_ref, bf16[768,512]{1,0:T(8,128)(2,1)S(1)} %get-tuple-element.93.main_ref, f32[8,256]{1,0:T(8,128)S(1)} %get-tuple-element.94.diff_ref), custom_call_target="tpu_custom_call" | custom-call | tf_op jit(solution)/shard_map/inner_3/pallas_call | solution.py:316
  134.2 5.4 %collective-permute-done.18.outer_ref = f32[528,128]{1,0:T(8,128)S(1)} collective-permute-done((f32[528,128]{1,0:T(8,128)S(1)}, f32[528,128]{1,0:T(8,128)S(1)}, u32[]{:S(2)}, u32[]{:S(2)}) %collective-permute-start.18) | collective-permute-done | bytes 270368 | tf_op jit(solution)/shard_map/ppermute | solution.py:68
  144.3 4.6 %collective-permute-start.20 = (f32[528,128]{1,0:T(8,128)S(1)}, f32[528,128]{1,0:T(8,128)S(1)}, u32[]{:S(2)}, u32[]{:S(2)}) collective-permute-start(f32[528,128]{1,0:T(8,128)S(1)} %get-tuple-element.129), channel_id=1, source_target_pairs={{0,1},{1,0},{2,3},{3,2},{4,5},{5,4},{6,7},{7,6},{8,9},{9,8},{10,11... | collective-permute-start | bytes 811016 | tf_op jit(solution)/shard_map/ppermute | solution.py:68
  148.9 2.6 %inner_4.1.rate_ref = f32[4,528,256]{2,1,0:T(8,128)S(1)} custom-call(f32[4,528,256]{2,1,0:T(8,128)S(1)} %get-tuple-element.128.u_ref, bf16[768,512]{1,0:T(8,128)(2,1)S(1)} %get-tuple-element.93.main_ref, f32[8,256]{1,0:T(8,128)S(1)} %get-tuple-element.94.diff_ref), custom_call_target="tpu_custom_call" | custom-call | tf_op jit(solution)/shard_map/inner_4/pallas_call | solution.py:316
  151.6 5.4 %collective-permute-done.21.outer_ref = f32[528,128]{1,0:T(8,128)S(1)} collective-permute-done((f32[528,128]{1,0:T(8,128)S(1)}, f32[528,128]{1,0:T(8,128)S(1)}, u32[]{:S(2)}, u32[]{:S(2)}) %collective-permute-start.21) | collective-permute-done | bytes 270368 | tf_op jit(solution)/shard_map/ppermute | solution.py:68
  158.5 3.1 %collective-permute-done.22.z_ref = f32[528,256]{1,0:T(8,128)S(1)} collective-permute-done((f32[528,256]{1,0:T(8,128)S(1)}, f32[528,256]{1,0:T(8,128)S(1)}, u32[]{:S(2)}, u32[]{:S(2)}) %collective-permute-start.22) | collective-permute-done | bytes 540704 | tf_op jit(solution)/shard_map/ppermute | solution.py:68
  162.0 5.7 %collective-permute-start.24 = (f32[512,256]{1,0:T(8,128)S(1)}, f32[512,256]{1,0:T(8,128)S(1)}, u32[]{:S(2)}, u32[]{:S(2)}) collective-permute-start(f32[512,256]{1,0:T(8,128)S(1)} %get-tuple-element.135), channel_id=1, source_target_pairs={{0,32},{1,33},{2,34},{3,35},{4,36},{5,37},{6,38},{7,39},{8,40},{9,... | collective-permute-start | bytes 1572872 | tf_op jit(solution)/shard_map/ppermute | solution.py:68
  167.6 7.1 %collective-permute-done.23.refs_1_ = f32[512,256]{1,0:T(8,128)S(1)} collective-permute-done((f32[512,256]{1,0:T(8,128)S(1)}, f32[512,256]{1,0:T(8,128)S(1)}, u32[]{:S(2)}, u32[]{:S(2)}) %collective-permute-start.23) | collective-permute-done | bytes 524320 | tf_op jit(solution)/shard_map/ppermute | solution.py:68
  174.7 14.9 %collective-permute-done.24.refs_2_ = f32[512,256]{1,0:T(8,128)S(1)} collective-permute-done((f32[512,256]{1,0:T(8,128)S(1)}, f32[512,256]{1,0:T(8,128)S(1)}, u32[]{:S(2)}, u32[]{:S(2)}) %collective-permute-start.24) | collective-permute-done | bytes 524320 | tf_op jit(solution)/shard_map/ppermute | solution.py:68
  189.6 2.1 %collective-permute-done.25.refs_3_ = f32[512,256]{1,0:T(8,128)S(1)} collective-permute-done((f32[512,256]{1,0:T(8,128)S(1)}, f32[512,256]{1,0:T(8,128)S(1)}, u32[]{:S(2)}, u32[]{:S(2)}) %collective-permute-start.25) | collective-permute-done | bytes 524320 | tf_op jit(solution)/shard_map/ppermute | solution.py:68
  (59 shorter events, 31.8 us)
Async XLA Ops:
  4.1 16.6 %collective-permute-start = (f32[528,256]{1,0:T(8,128)S(1)}, f32[528,256]{1,0:T(8,128)S(1)}, u32[]{:S(2)}, u32[]{:S(2)}) collective-permute-start(f32[528,256]{1,0:T(8,128)S(1)} %get-tuple-element.73), channel_id=1, source_target_pairs={{0,16},{1,17},{2,18},{3,19},{4,20},{5,21},{6,22},{7,23},{8,24},{9,... | collective-permute-start | bytes 1622024 | tf_op jit(solution)/shard_map/ppermute | solution.py:68
  5.4 25.8 %collective-permute-start.1 = (f32[528,256]{1,0:T(8,128)S(1)}, f32[528,256]{1,0:T(8,128)S(1)}, u32[]{:S(2)}, u32[]{:S(2)}) collective-permute-start(f32[528,256]{1,0:T(8,128)S(1)} %get-tuple-element.74), channel_id=1, source_target_pairs={{0,32},{1,33},{2,34},{3,35},{4,36},{5,37},{6,38},{7,39},{8,40},{9,... | collective-permute-start | bytes 1622024 | tf_op jit(solution)/shard_map/ppermute | solution.py:68
  7.8 25.3 %collective-permute-start.2 = (f32[528,256]{1,0:T(8,128)S(1)}, f32[528,256]{1,0:T(8,128)S(1)}, u32[]{:S(2)}, u32[]{:S(2)}) collective-permute-start(f32[528,256]{1,0:T(8,128)S(1)} %get-tuple-element.75), channel_id=1, source_target_pairs={{0,48},{1,49},{2,50},{3,51},{4,52},{5,53},{6,54},{7,55},{8,56},{9,... | collective-permute-start | bytes 1622024 | tf_op jit(solution)/shard_map/ppermute | solution.py:68
  20.7 105.3 %copy-start.4 = (f32[528,256]{1,0:T(8,128)}, f32[528,256]{1,0:T(8,128)S(1)}, u32[]{:S(2)}) copy-start(f32[528,256]{1,0:T(8,128)S(1)} %get-tuple-element.81.refs_0_) | copy-start | bytes 1622020
  33.2 47.2 %collective-permute-start.5 = (f32[1056,256]{1,0:T(8,128)S(1)}, f32[1056,256]{1,0:T(8,128)S(1)}, u32[]{:S(2)}, u32[]{:S(2)}) collective-permute-start(f32[1056,256]{1,0:T(8,128)S(1)} %get-tuple-element.80), channel_id=1, source_target_pairs={{0,48},{1,49},{2,50},{3,51},{4,52},{5,53},{6,54},{7,55},{8,56},{9,... | collective-permute-start | bytes 3244040 | tf_op jit(solution)/shard_map/ppermute | solution.py:68
  35.3 45.0 %collective-permute-start.4 = (f32[1056,256]{1,0:T(8,128)S(1)}, f32[1056,256]{1,0:T(8,128)S(1)}, u32[]{:S(2)}, u32[]{:S(2)}) collective-permute-start(f32[1056,256]{1,0:T(8,128)S(1)} %get-tuple-element.78), channel_id=1, source_target_pairs={{0,32},{1,33},{2,34},{3,35},{4,36},{5,37},{6,38},{7,39},{8,40},{9,... | collective-permute-start | bytes 3244040 | tf_op jit(solution)/shard_map/ppermute | solution.py:68
  37.3 44.9 %collective-permute-start.3 = (f32[1056,256]{1,0:T(8,128)S(1)}, f32[1056,256]{1,0:T(8,128)S(1)}, u32[]{:S(2)}, u32[]{:S(2)}) collective-permute-start(f32[1056,256]{1,0:T(8,128)S(1)} %get-tuple-element.76), channel_id=1, source_target_pairs={{0,16},{1,17},{2,18},{3,19},{4,20},{5,21},{6,22},{7,23},{8,24},{9,... | collective-permute-start | bytes 3244040 | tf_op jit(solution)/shard_map/ppermute | solution.py:68
  39.2 4.7 %copy-start.8 = (f32[16]{0:T(128)S(1)}, f32[16]{0:T(128)}, u32[]{:S(2)}) copy-start(f32[16]{0:T(128)} %param.7) | copy-start | bytes 196
  39.2 4.7 %copy-start.2 = (f32[16,16]{1,0:T(8,128)S(1)}, f32[16,16]{1,0:T(8,128)}, u32[]{:S(2)}) copy-start(f32[16,16]{1,0:T(8,128)} %lin_ref.1) | copy-start | bytes 3076
  39.2 4.7 %copy-start.3 = (f32[16,16]{1,0:T(8,128)S(1)}, f32[16,16]{1,0:T(8,128)}, u32[]{:S(2)}) copy-start(f32[16,16]{1,0:T(8,128)} %coup_ref.1) | copy-start | bytes 3076
  39.9 7.6 %collective-permute-start.9 = (f32[528,128]{1,0:T(8,128)S(1)}, f32[528,128]{1,0:T(8,128)S(1)}, u32[]{:S(2)}, u32[]{:S(2)}) collective-permute-start(f32[528,128]{1,0:T(8,128)S(1)} %get-tuple-element.95), channel_id=1, source_target_pairs={{0,1},{1,0},{2,3},{3,2},{4,5},{5,4},{6,7},{7,6},{8,9},{9,8},{10,11... | collective-permute-start | bytes 811016 | tf_op jit(solution)/shard_map/ppermute | solution.py:68
  42.9 8.3 %collective-permute-start.10 = (f32[528,128]{1,0:T(8,128)S(1)}, f32[528,128]{1,0:T(8,128)S(1)}, u32[]{:S(2)}, u32[]{:S(2)}) collective-permute-start(f32[528,128]{1,0:T(8,128)S(1)} %get-tuple-element.96), channel_id=1, source_target_pairs={{0,15},{1,2},{2,1},{3,4},{4,3},{5,6},{6,5},{7,8},{8,7},{9,10},{10,... | collective-permute-start | bytes 811016 | tf_op jit(solution)/shard_map/ppermute | solution.py:68
  82.1 21.3 %collective-permute-start.6 = (f32[528,256]{1,0:T(8,128)S(1)}, f32[528,256]{1,0:T(8,128)S(1)}, u32[]{:S(2)}, u32[]{:S(2)}) collective-permute-start(f32[528,256]{1,0:T(8,128)S(1)} %get-tuple-element.83), channel_id=1, source_target_pairs={{0,16},{1,17},{2,18},{3,19},{4,20},{5,21},{6,22},{7,23},{8,24},{9,... | collective-permute-start | bytes 1622024 | tf_op jit(solution)/shard_map/ppermute | solution.py:68
  85.1 18.3 %collective-permute-start.7 = (f32[528,256]{1,0:T(8,128)S(1)}, f32[528,256]{1,0:T(8,128)S(1)}, u32[]{:S(2)}, u32[]{:S(2)}) collective-permute-start(f32[528,256]{1,0:T(8,128)S(1)} %get-tuple-element.87), channel_id=1, source_target_pairs={{0,48},{1,49},{2,50},{3,51},{4,52},{5,53},{6,54},{7,55},{8,56},{9,... | collective-permute-start | bytes 1622024 | tf_op jit(solution)/shard_map/ppermute | solution.py:68
  89.0 18.1 %collective-permute-start.13 = (f32[528,256]{1,0:T(8,128)S(1)}, f32[528,256]{1,0:T(8,128)S(1)}, u32[]{:S(2)}, u32[]{:S(2)}) collective-permute-start(f32[528,256]{1,0:T(8,128)S(1)} %get-tuple-element.109), channel_id=1, source_target_pairs={{0,64},{1,65},{2,66},{3,67},{4,68},{5,69},{6,70},{7,71},{8,72},{9,... | collective-permute-start | bytes 1622024 | tf_op jit(solution)/shard_map/ppermute | solution.py:68
  90.3 7.5 %collective-permute-start.11 = (f32[528,128]{1,0:T(8,128)S(1)}, f32[528,128]{1,0:T(8,128)S(1)}, u32[]{:S(2)}, u32[]{:S(2)}) collective-permute-start(f32[528,128]{1,0:T(8,128)S(1)} %get-tuple-element.101), channel_id=1, source_target_pairs={{0,1},{1,0},{2,3},{3,2},{4,5},{5,4},{6,7},{7,6},{8,9},{9,8},{10,11... | collective-permute-start | bytes 811016 | tf_op jit(solution)/shard_map/ppermute | solution.py:68
  94.1 8.0 %collective-permute-start.12 = (f32[528,128]{1,0:T(8,128)S(1)}, f32[528,128]{1,0:T(8,128)S(1)}, u32[]{:S(2)}, u32[]{:S(2)}) collective-permute-start(f32[528,128]{1,0:T(8,128)S(1)} %get-tuple-element.102), channel_id=1, source_target_pairs={{0,15},{1,2},{2,1},{3,4},{4,3},{5,6},{6,5},{7,8},{8,7},{9,10},{10,... | collective-permute-start | bytes 811016 | tf_op jit(solution)/shard_map/ppermute | solution.py:68
  103.4 4.6 %copy-start.6 = (f32[528,256]{1,0:T(8,128)}, f32[528,256]{1,0:T(8,128)S(1)}, u32[]{:S(2)}) copy-start(f32[528,256]{1,0:T(8,128)S(1)} %collective-permute-done.7.refs_3_) | copy-start | bytes 1622020
  103.4 16.0 %collective-permute-start.8 = (f32[528,256]{1,0:T(8,128)S(1)}, f32[528,256]{1,0:T(8,128)S(1)}, u32[]{:S(2)}, u32[]{:S(2)}) collective-permute-start(f32[528,256]{1,0:T(8,128)S(1)} %get-tuple-element.88), channel_id=1, source_target_pairs={{0,32},{1,33},{2,34},{3,35},{4,36},{5,37},{6,38},{7,39},{8,40},{9,... | collective-permute-start | bytes 1622024 | tf_op jit(solution)/shard_map/ppermute | solution.py:68
  108.0 18.1 %collective-permute-start.16 = (f32[528,256]{1,0:T(8,128)S(1)}, f32[528,256]{1,0:T(8,128)S(1)}, u32[]{:S(2)}, u32[]{:S(2)}) collective-permute-start(f32[528,256]{1,0:T(8,128)S(1)} %get-tuple-element.119), channel_id=1, source_target_pairs={{0,64},{1,65},{2,66},{3,67},{4,68},{5,69},{6,70},{7,71},{8,72},{9,... | collective-permute-start | bytes 1622024 | tf_op jit(solution)/shard_map/ppermute | solution.py:68
  109.3 12.8 %collective-permute-start.14 = (f32[528,128]{1,0:T(8,128)S(1)}, f32[528,128]{1,0:T(8,128)S(1)}, u32[]{:S(2)}, u32[]{:S(2)}) collective-permute-start(f32[528,128]{1,0:T(8,128)S(1)} %get-tuple-element.112), channel_id=1, source_target_pairs={{0,1},{1,0},{2,3},{3,2},{4,5},{5,4},{6,7},{7,6},{8,9},{9,8},{10,11... | collective-permute-start | bytes 811016 | tf_op jit(solution)/shard_map/ppermute | solution.py:68
  112.2 9.8 %collective-permute-start.15 = (f32[528,128]{1,0:T(8,128)S(1)}, f32[528,128]{1,0:T(8,128)S(1)}, u32[]{:S(2)}, u32[]{:S(2)}) collective-permute-start(f32[528,128]{1,0:T(8,128)S(1)} %get-tuple-element.113), channel_id=1, source_target_pairs={{0,15},{1,2},{2,1},{3,4},{4,3},{5,6},{6,5},{7,8},{8,7},{9,10},{10,... | collective-permute-start | bytes 811016 | tf_op jit(solution)/shard_map/ppermute | solution.py:68
  126.9 16.7 %collective-permute-start.19 = (f32[528,256]{1,0:T(8,128)S(1)}, f32[528,256]{1,0:T(8,128)S(1)}, u32[]{:S(2)}, u32[]{:S(2)}) collective-permute-start(f32[528,256]{1,0:T(8,128)S(1)} %get-tuple-element.127), channel_id=1, source_target_pairs={{0,64},{1,65},{2,66},{3,67},{4,68},{5,69},{6,70},{7,71},{8,72},{9,... | collective-permute-start | bytes 1622024 | tf_op jit(solution)/shard_map/ppermute | solution.py:68
  128.2 6.1 %collective-permute-start.17 = (f32[528,128]{1,0:T(8,128)S(1)}, f32[528,128]{1,0:T(8,128)S(1)}, u32[]{:S(2)}, u32[]{:S(2)}) collective-permute-start(f32[528,128]{1,0:T(8,128)S(1)} %get-tuple-element.121), channel_id=1, source_target_pairs={{0,1},{1,0},{2,3},{3,2},{4,5},{5,4},{6,7},{7,6},{8,9},{9,8},{10,11... | collective-permute-start | bytes 811016 | tf_op jit(solution)/shard_map/ppermute | solution.py:68
  131.6 8.0 %collective-permute-start.18 = (f32[528,128]{1,0:T(8,128)S(1)}, f32[528,128]{1,0:T(8,128)S(1)}, u32[]{:S(2)}, u32[]{:S(2)}) collective-permute-start(f32[528,128]{1,0:T(8,128)S(1)} %get-tuple-element.122), channel_id=1, source_target_pairs={{0,15},{1,2},{2,1},{3,4},{4,3},{5,6},{6,5},{7,8},{8,7},{9,10},{10,... | collective-permute-start | bytes 811016 | tf_op jit(solution)/shard_map/ppermute | solution.py:68
  139.6 4.0 %copy-start.5 = (f32[528,256]{1,0:T(8,128)S(1)}, f32[528,256]{1,0:T(8,128)}, u32[]{:S(2)}) copy-start(f32[528,256]{1,0:T(8,128)} %copy-done.4) | copy-start | bytes 1622020
  140.6 21.1 %collective-permute-start.22 = (f32[528,256]{1,0:T(8,128)S(1)}, f32[528,256]{1,0:T(8,128)S(1)}, u32[]{:S(2)}, u32[]{:S(2)}) collective-permute-start(f32[528,256]{1,0:T(8,128)S(1)} %get-tuple-element.126.refs_5_), channel_id=1, source_target_pairs={{0,64},{1,65},{2,66},{3,67},{4,68},{5,69},{6,70},{7,71},{8,72},{9,... | collective-permute-start | bytes 1622024 | tf_op jit(solution)/shard_map/ppermute | solution.py:68
  144.3 7.2 %collective-permute-start.20 = (f32[528,128]{1,0:T(8,128)S(1)}, f32[528,128]{1,0:T(8,128)S(1)}, u32[]{:S(2)}, u32[]{:S(2)}) collective-permute-start(f32[528,128]{1,0:T(8,128)S(1)} %get-tuple-element.129), channel_id=1, source_target_pairs={{0,1},{1,0},{2,3},{3,2},{4,5},{5,4},{6,7},{7,6},{8,9},{9,8},{10,11... | collective-permute-start | bytes 811016 | tf_op jit(solution)/shard_map/ppermute | solution.py:68
  148.9 8.0 %collective-permute-start.21 = (f32[528,128]{1,0:T(8,128)S(1)}, f32[528,128]{1,0:T(8,128)S(1)}, u32[]{:S(2)}, u32[]{:S(2)}) collective-permute-start(f32[528,128]{1,0:T(8,128)S(1)} %get-tuple-element.130), channel_id=1, source_target_pairs={{0,15},{1,2},{2,1},{3,4},{4,3},{5,6},{6,5},{7,8},{8,7},{9,10},{10,... | collective-permute-start | bytes 811016 | tf_op jit(solution)/shard_map/ppermute | solution.py:68
  161.9 12.9 %collective-permute-start.23 = (f32[512,256]{1,0:T(8,128)S(1)}, f32[512,256]{1,0:T(8,128)S(1)}, u32[]{:S(2)}, u32[]{:S(2)}) collective-permute-start(f32[512,256]{1,0:T(8,128)S(1)} %get-tuple-element.134), channel_id=1, source_target_pairs={{0,16},{1,17},{2,18},{3,19},{4,20},{5,21},{6,22},{7,23},{8,24},{9,... | collective-permute-start | bytes 1572872 | tf_op jit(solution)/shard_map/ppermute | solution.py:68
  162.0 27.7 %collective-permute-start.24 = (f32[512,256]{1,0:T(8,128)S(1)}, f32[512,256]{1,0:T(8,128)S(1)}, u32[]{:S(2)}, u32[]{:S(2)}) collective-permute-start(f32[512,256]{1,0:T(8,128)S(1)} %get-tuple-element.135), channel_id=1, source_target_pairs={{0,32},{1,33},{2,34},{3,35},{4,36},{5,37},{6,38},{7,39},{8,40},{9,... | collective-permute-start | bytes 1572872 | tf_op jit(solution)/shard_map/ppermute | solution.py:68
  167.6 24.1 %collective-permute-start.25 = (f32[512,256]{1,0:T(8,128)S(1)}, f32[512,256]{1,0:T(8,128)S(1)}, u32[]{:S(2)}, u32[]{:S(2)}) collective-permute-start(f32[512,256]{1,0:T(8,128)S(1)} %get-tuple-element.136), channel_id=1, source_target_pairs={{0,48},{1,49},{2,50},{3,51},{4,52},{5,53},{6,54},{7,55},{8,56},{9,... | collective-permute-start | bytes 1572872 | tf_op jit(solution)/shard_map/ppermute | solution.py:68
  (3 other events, 8.4 us)

commit v3 on v0

v3 whole, which is shorter than its diff:
```python
import functools

import jax
import jax.numpy as jnp
from jax import lax
from jax.experimental import pallas as pl
from jax.experimental.pallas import tpu as pltpu
from jax.sharding import PartitionSpec as P

SPECIES = 16
ROWS = 16
CELLS = SPECIES * ROWS
HALF = CELLS // 2
NCOL = 2048
LEVELS = 8
CHUNK = NCOL // LEVELS
HALO = 8
WIDE = CHUNK + 2 * HALO
EDGE = 2 * SPECIES
STEP = 0.4
W0, W1, W2, W3 = (1.0 / 24.0, -5.0 / 24.0, 19.0 / 24.0, 9.0 / 24.0)
TAPS = (-1.0 / 12.0, 16.0 / 12.0, -30.0 / 12.0, 16.0 / 12.0, -1.0 / 12.0)
PAD = 8
FIELDS = 4
GROUP = HALF // EDGE
BAND = WIDE // 2

f32 = jnp.float32
bf16 = jnp.bfloat16
dot = functools.partial(jnp.dot, preferred_element_type=f32)


def params(mib=24, **kw):
    return pltpu.CompilerParams(vmem_limit_bytes=mib * 1024 * 1024, **kw)


def vmem():
    return pl.BlockSpec(memory_space=pltpu.VMEM)


def hbm():
    return pl.BlockSpec(memory_space=pl.ANY)


def core_swap():
    return [(l * 16 + t, l * 16 + (t ^ 1)) for l in range(LEVELS) for t in range(16)]


def chip_swap():
    return [(l * 16 + t, l * 16 + (t + (1 if t % 2 else 15)) % 16) for l in range(LEVELS) for t in range(16)]


def level_swap(by):
    return [(l * 16 + t, (l ^ by) * 16 + t) for l in range(LEVELS) if l ^ by < LEVELS for t in range(16)]


def send(value, pairs):
    return lax.ppermute(value, ("level", "tile"), pairs)


def everyone(value):
    return lax.all_to_all(value, "level", 0, 0)


def on_first_core():
    return lax.rem(lax.axis_index("tile"), 2) == 0


def cut_kernel(state_hbm, hist_hbm, out_ref, *refs):
    lasts, (state, hist, tiles, turned, in_sem, out_sem) = refs[:LEVELS], refs[LEVELS:]
    loads = [pltpu.make_async_copy(state_hbm, state, in_sem.at[0])]
    loads += [pltpu.make_async_copy(hist_hbm.at[n], hist.at[n], in_sem.at[n + 1]) for n in range(3)]
    for load in loads:
        load.start()

    def turn(n, value):
        tiles[n] = value
        rows = [tiles[n, pl.ds(row, SPECIES, stride=ROWS), :] for row in range(ROWS)]
        return jnp.concatenate(rows, axis=0).T

    def put(n, chunk, half, value):
        start = n * WIDE
        out_ref[chunk, start + HALO + half * 128 : start + HALO + (half + 1) * 128, :] = value
        if half == 0:
            other = lax.rem(chunk + LEVELS - 1, LEVELS)
            out_ref[other, start + WIDE - HALO : start + WIDE, :] = value[:HALO]
        else:
            other = lax.rem(chunk + 1, LEVELS)
            out_ref[other, start : start + HALO, :] = value[128 - HALO :]

    def columns(chunk, half):
        return pl.ds(pl.multiple_of(chunk * CHUNK + half * 128, 128), 128)

    def last_body(i, _):
        for half in range(2):
            r = hist[2, :, columns(i, half)]
            at = pl.multiple_of(i * CHUNK + half * 128 + HALO, 8)
            turned[pl.ds(at, 128), :] = turn(3, (STEP * W0) * r)
        return 0

    def state_body(chunk, _):
        for half in range(2):
            put(0, chunk, half, turn(0, state[:, columns(chunk, half)]))
        return 0

    def hist_body(chunk, _):
        for half in range(2):
            p, q, r = (hist[n, :, columns(chunk, half)] for n in range(3))
            put(1, chunk, half, turn(1, STEP * (W0 * p + W1 * q + (W2 - 1.0) * r)))
            put(2, chunk, half, turn(2, STEP * (W0 * q + W1 * r)))
        return 0

    loads[0].wait()
    lax.fori_loop(0, LEVELS, state_body, 0)
    for load in loads[1:]:
        load.wait()
    lax.fori_loop(0, LEVELS, last_body, 0)
    turned[:HALO, :] = turned[NCOL : NCOL + HALO, :]
    turned[NCOL + HALO :, :] = turned[HALO : 2 * HALO, :]
    copies = []
    for by, last_ref in enumerate(lasts):
        base = pl.multiple_of(lax.bitwise_xor(lax.axis_index("level"), by) * CHUNK, 128)
        copies.append(pltpu.make_async_copy(turned.at[pl.ds(base, WIDE), :], last_ref, out_sem.at[by]))
        copies[-1].start()
    lax.fori_loop(0, LEVELS, hist_body, 0)
    for copy in copies:
        copy.wait()


def cut(state, hist):
    outs = pl.pallas_call(
        cut_kernel,
        out_shape=[pltpu.VMEM((LEVELS, 3 * WIDE, CELLS), f32)] + [jax.ShapeDtypeStruct((WIDE, CELLS), f32)] * LEVELS,
        in_specs=[hbm()] * 2,
        out_specs=[vmem()] + [hbm()] * LEVELS,
        scratch_shapes=[
            pltpu.VMEM((CELLS, NCOL), f32),
            pltpu.VMEM((3, CELLS, NCOL), f32),
            pltpu.VMEM((FIELDS, CELLS, 128), f32),
            pltpu.VMEM((NCOL + 2 * HALO, CELLS), f32),
            pltpu.SemaphoreType.DMA((4,)),
            pltpu.SemaphoreType.DMA((LEVELS,)),
        ],
        compiler_params=params(40),
        name="cut",
    )(state, hist)
    return outs[0], outs[1:]


def gather_kernel(*refs):
    parts, out_ref, sem = refs[:LEVELS], refs[LEVELS], refs[LEVELS + 1]
    copies = []
    for by, part in enumerate(parts):
        level = lax.bitwise_xor(lax.axis_index("level"), by)
        copies.append(pltpu.make_async_copy(part, out_ref.at[level], sem.at[by]))
        copies[-1].start()
    for copy in copies:
        copy.wait()


def gather(parts):
    return pl.pallas_call(
        gather_kernel,
        out_shape=pltpu.VMEM((LEVELS, WIDE, CELLS), f32),
        in_specs=[hbm()] * LEVELS,
        out_specs=vmem(),
        scratch_shapes=[pltpu.SemaphoreType.DMA((LEVELS,))],
        compiler_params=params(),
        name="gather",
    )(*parts)


def pack_edges(u_ref, inner_ref, outer_ref):
    lane = lax.broadcasted_iota(jnp.int32, (BAND, HALF), 1)
    first_core = on_first_core()
    for group in range(LEVELS // GROUP):
        at = slice(group * HALF, (group + 1) * HALF)
        for begin in range(0, WIDE, BAND):
            rows = slice(begin, begin + BAND)
            down = up = None
            for k in range(GROUP):
                here = (lane >= k * EDGE) & (lane < (k + 1) * EDGE)
                top = u_ref[group * GROUP + k, rows, :HALF]
                bottom = u_ref[group * GROUP + k, rows, HALF:]
                top = pltpu.roll(top, k * EDGE, 1) if k else top
                bottom = pltpu.roll(bottom, (k + 1) * EDGE, 1) if k < GROUP - 1 else bottom
                down = top if k == 0 else jnp.where(here, top, down)
                up = bottom if k == 0 else jnp.where(here, bottom, up)
            inner_ref[rows, at] = jnp.where(first_core, up, down)
            outer_ref[rows, at] = jnp.where(first_core, down, up)


def edges_kernel(fields_ref, inner_ref, outer_ref):
    pack_edges(fields_ref, inner_ref, outer_ref)


HALO_SHAPE = jax.ShapeDtypeStruct((WIDE, LEVELS * EDGE), f32)


def first_edges(fields):
    return pl.pallas_call(
        edges_kernel,
        out_shape=[HALO_SHAPE] * 2,
        in_specs=[vmem()],
        out_specs=[vmem()] * 2,
        compiler_params=params(),
        name="edges",
    )(fields)


def split(into, at, value, rows=slice(0, WIDE)):
    high_part = value.astype(bf16)
    width = value.shape[1]
    into[rows, at : at + width] = high_part
    into[rows, CELLS + at : CELLS + at + width] = (value - high_part.astype(f32)).astype(bf16)
    into[rows, 2 * CELLS + at : 2 * CELLS + at + width] = high_part


def inner_kernel(u_ref, main_ref, diff_ref, rate_ref, padded, stack):
    padded[:, :, :PAD, :] = jnp.zeros((2, 2, PAD, HALF), f32)
    padded[:, :, PAD + WIDE :, :] = jnp.zeros((2, 2, PAD, HALF), f32)
    for pair in range(LEVELS // 2):
        for k in range(2):
            for side in range(2):
                part = u_ref[2 * pair + k, :WIDE, side * HALF : (side + 1) * HALF]
                padded[k, side, PAD : PAD + WIDE, :] = part
                split(stack, side * HALF, part, slice(k * WIDE, (k + 1) * WIDE))
        products = dot(stack[...], main_ref[...])
        for k in range(2):
            for side in range(2):
                at = slice(side * HALF, (side + 1) * HALF)
                diff = diff_ref[0:1, at]
                for begin in range(0, WIDE, BAND):
                    moved = lambda by: padded[k, side, PAD + begin + by : PAD + begin + by + BAND, :]
                    rows = slice(k * WIDE + begin, k * WIDE + begin + BAND)
                    u = moved(0)
                    near = moved(-1) + moved(1)
                    far = moved(-2) + moved(2)
                    rate = products[rows, at] + diff * (16.0 * near - far)
                    rate = rate + jnp.tanh(products[rows, CELLS + side * HALF : CELLS + (side + 1) * HALF])
                    rate_ref[2 * pair + k, begin : begin + BAND, at] = rate - u * u * u * (1.0 / 3.0)


def inner_rates(step, u, weights):
    main, _, diff = weights
    return pl.pallas_call(
        inner_kernel,
        out_shape=pltpu.VMEM((LEVELS, WIDE, CELLS), f32),
        in_specs=[vmem()] * 3,
        out_specs=vmem(),
        scratch_shapes=[
            pltpu.VMEM((2, 2, WIDE + 2 * PAD, HALF), f32),
            pltpu.VMEM((2 * WIDE, 3 * CELLS), bf16),
        ],
        compiler_params=params(),
        name=f"inner_{step}",
    )(u, main, diff)


def step_kernel(step, n_in, n_out, u_ref, rate_ref, inner_ref, outer_ref, edge_ref, *refs):
    refs = list(refs)
    take = lambda n: [refs.pop(0) for _ in range(n)]
    fields_ref = take(1)[0] if step < 3 else None
    older = take(n_in)
    next_ref = take(1)[0]
    sends = take(2) if step < 3 else None
    newer = take(n_out)
    stack, edges = take(2)
    first_core = on_first_core()
    for group in range(LEVELS // GROUP):
        at = slice(group * HALF, (group + 1) * HALF)
        inner, outer = inner_ref[:, at], outer_ref[:, at]
        split(stack, 0, jnp.where(first_core, outer, inner))
        split(stack, HALF, jnp.where(first_core, inner, outer))
        edges[group] = dot(stack[...], edge_ref[...])
    lane = lax.broadcasted_iota(jnp.int32, (BAND, HALF), 1)
    for side in range(2):
        at = slice(side * HALF, (side + 1) * HALF)
        near_edge = lane >= HALF - EDGE if side else lane < EDGE
        for begin in range(0, WIDE, BAND):
            rows = slice(begin, begin + BAND)
            below = None
            for level in range(LEVELS):
                group, k = divmod(level, GROUP)
                turn = (HALF - EDGE - k * EDGE if side else HALF - k * EDGE) % HALF
                edge = edges[group, rows, at]
                edge = pltpu.roll(edge, turn, 1) if turn else edge
                scaled = STEP * (rate_ref[level, rows, at] + jnp.where(near_edge, edge, 0.0))
                value = u_ref[level, rows, at] + scaled
                next_ref[level, rows, at] = value if below is None else value + below
                below = W3 * scaled
                if n_in > 0:
                    below = below + older[0][level, rows, at]
                if step < 3:
                    start = (0 if step == 2 else (step + 1) * WIDE) + begin
                    below = below + fields_ref[level, start : start + BAND, at]
                for i, weight in zip(range(n_out), (W2 - 1.0, W1, W0)):
                    value = weight * scaled
                    if i + 1 < n_in:
                        value = value + older[i + 1][level, rows, at]
                    newer[i][level, rows, at] = value
    if step < 3:
        pack_edges(next_ref, *sends)


def one_step(step, u, rate, inner, outer, weights, fields, older, n_out):
    n_in = len(older)
    full = pltpu.VMEM((LEVELS, WIDE, CELLS), f32)
    operands = [u, rate, inner, outer, weights[1]] + ([fields] if step < 3 else []) + older
    outs = [full] + ([HALO_SHAPE] * 2 if step < 3 else []) + [full] * n_out
    outs = pl.pallas_call(
        functools.partial(step_kernel, step, n_in, n_out),
        out_shape=outs,
        in_specs=[vmem()] * len(operands),
        out_specs=[vmem()] * len(outs),
        scratch_shapes=[
            pltpu.VMEM((WIDE, 3 * CELLS), bf16),
            pltpu.VMEM((LEVELS // GROUP, WIDE, CELLS), f32),
        ],
        compiler_params=params(),
        name=f"step_{step}",
    )(*operands)
    if step < 3:
        return outs[0], outs[1], outs[2], list(outs[3:])
    return outs[0], None, None, []


def weights_kernel(lin_ref, coup_ref, diff_ref, main_ref, edge_ref, diff_out):
    exact = functools.partial(lax.dot_general, precision=lax.Precision.HIGHEST, preferred_element_type=f32)
    last = (((1,), (1,)), ((), ()))
    iota = lambda shape, dim: lax.broadcasted_iota(jnp.int32, shape, dim)
    pick = (iota((CELLS, SPECIES), 0) % SPECIES == iota((CELLS, SPECIES), 1)).astype(f32)
    source, target = iota((CELLS, CELLS), 0), iota((CELLS, CELLS), 1)
    same_row = source // SPECIES == target // SPECIES
    same_species = source % SPECIES == target % SPECIES
    diffusion = exact(diff_ref[...], pick, last)

    def tiled(matrix):
        return jnp.where(same_row, exact(exact(pick, matrix, last), pick, last), 0.0)

    def stencil(offset, middle):
        value = jnp.where(offset == 0, middle, 0.0)
        value = value + jnp.where((offset == 1) | (offset == -1), TAPS[1], 0.0)
        return value + jnp.where((offset == 2) | (offset == -2), TAPS[0], 0.0)

    def put(into, at, value):
        high_part = value.astype(bf16)
        into[:CELLS, at : at + CELLS] = high_part
        into[CELLS : 2 * CELLS, at : at + CELLS] = high_part
        into[2 * CELLS :, at : at + CELLS] = (value - high_part.astype(f32)).astype(bf16)

    offset = source // SPECIES - target // SPECIES
    spread = jnp.where(same_species, stencil(offset, 2.0 * TAPS[2]) * diffusion[0:1], 0.0)
    put(main_ref, 0, tiled(lin_ref[...]) + spread)
    put(main_ref, CELLS, tiled(coup_ref[...]))
    row_from = (source // SPECIES) % 2 + jnp.where(source < HALF, -2, ROWS)
    row_to = (target // SPECIES) % 2 + jnp.where(target < HALF, 0, ROWS - 2)
    alike = same_species & (source // EDGE == target // EDGE)
    put(edge_ref, 0, jnp.where(alike, stencil(row_from - row_to, 0.0) * diffusion[0:1], 0.0))
    diff_out[...] = diffusion * (1.0 / 12.0)


def make_weights(diffusion, linear_rates, coupling):
    return pl.pallas_call(
        weights_kernel,
        out_shape=[
            pltpu.VMEM((3 * CELLS, 2 * CELLS), bf16),
            pltpu.VMEM((3 * CELLS, CELLS), bf16),
            pltpu.VMEM((8, CELLS), f32),
        ],
        in_specs=[vmem()] * 3,
        out_specs=[vmem()] * 3,
        compiler_params=params(),
        name="weights",
    )(linear_rates, coupling, jnp.broadcast_to(diffusion[None], (8, SPECIES)))


def join_kernel(parts, out_ref, turn, whole, sem):
    copies = []
    for half in range(2):
        for slot in range(NCOL // 128):
            chunk, i = divmod(slot, CHUNK // 128)
            turn[slot] = parts[chunk, i * 128 : (i + 1) * 128, half * HALF : (half + 1) * HALF].T
            columns = slice(slot * 128, (slot + 1) * 128)
            for species in range(SPECIES):
                whole[half, species, :, columns] = turn[slot, pl.ds(species, ROWS // 2, stride=SPECIES), :]
        target = out_ref.at[:, half * (ROWS // 2) : (half + 1) * (ROWS // 2), :]
        copies.append(pltpu.make_async_copy(whole.at[half], target, sem.at[half]))
        copies[-1].start()
    for copy in copies:
        copy.wait()


def join(parts):
    return pl.pallas_call(
        join_kernel,
        out_shape=jax.ShapeDtypeStruct((SPECIES, ROWS, NCOL), f32),
        in_specs=[vmem()],
        out_specs=hbm(),
        scratch_shapes=[
            pltpu.VMEM((NCOL // 128, HALF, 128), f32),
            pltpu.VMEM((2, SPECIES, ROWS // 2, NCOL), f32),
            pltpu.SemaphoreType.DMA((2,)),
        ],
        compiler_params=params(),
        name="join",
    )(parts)


def after(value, *earlier):
    return lax.optimization_barrier((value, *earlier))[0]


WAVES = ((1, 3), (4, 2, 5), (6, 7))


def local(level_state, history, diffusion, linear_rates, coupling):
    state = level_state.reshape(CELLS, NCOL)
    hist = history.reshape(3, CELLS, NCOL)
    weights = make_weights(diffusion, linear_rates, coupling)
    first, lasts = cut(state, hist)
    fields = everyone(first)
    u = fields
    inner, outer = first_edges(fields)
    older = []
    got = {0: lasts[0]}
    edge = inner
    for step, n_out in enumerate((3, 2, 1, 0)):
        outer = send(outer, chip_swap())
        inner = send(inner, core_swap())
        earlier = list(got.values()) if step else [fields, edge]
        if step < 3:
            for by in WAVES[step]:
                got[by] = send(after(lasts[by], *earlier), level_swap(by))
        rate = inner_rates(step, after(u, *earlier) if step else u, weights)
        if step == 2:
            fields = gather([got[by] for by in range(LEVELS)])
        u, inner, outer, older = one_step(step, u, rate, inner, outer, weights, fields, older, n_out)
    return join(everyone(u[:, HALO : HALO + CHUNK, :]))[None]


def solution(mesh):
    placed = (P("level", None, "tile", None), P("level", None, None, "tile", None), P(), P(), P())
    return jax.shard_map(
        local, mesh=mesh, in_specs=placed, out_specs=P("level", None, "tile", None), check_vma=False
    )
```

time: 308 us -> 186 us (0.60)
  waiting for transfers between devices: 211 us -> 15.3 us
  blocking collectives: 0 us -> 112 us
  matrix products: 46.4 us -> 0 us
  Pallas kernels: 0 us -> 29 us
  local copies, waits for them, and re-layouts: 22.9 us -> 1.74 us
  other arithmetic: 5.02 us -> 0 us
    ppermute x12 -> x15, waiting for transfers between devices: 211 us -> 15.3 us  [send(): return lax.ppermute(value, ('level', 'tile'), pairs)]
    all_to_all x0 -> x2, blocking collectives: none -> 112 us  [everyone(): return lax.all_to_all(value, 'level', 0, 0)]
    dot_general x8 -> x0, matrix products: 46.4 us -> none  [the longest x4 32.5 us: local_rates(): jnp.einsum('ab,brc->arc', linear_rates, centre, precision=lax.Precision.H...]
    pallas_call x0 -> x13, Pallas kernels: none -> 29 us  [the longest x4 10.7 us: inner_rates(): pl.pallas_call(inner_kernel, out_shape=pltpu.VMEM((LEVELS, WIDE, CELLS),...]
    slice x21 -> x1, local copies, waits for them, and re-layouts: 16 us -> 0.14 us  [local(): return join(everyone(u[:, HALO:HALO + CHUNK, :]))[None]]
    ppermute x12 -> x15, starting transfers between devices: 22.7 us -> 24.8 us  [send(): return lax.ppermute(value, ('level', 'tile'), pairs)]
  transfers between devices with their start and end apart: 12 -> 15, of which waited for: 11 -> 4; matrix products, arithmetic and copies ran while one was open for 1% -> 0% of each run, Pallas kernels for 0% -> 9%
where the time goes in v3:
time: 186 us; the launch traced here: 183 us
  blocking collectives  112 us (60%)
  Pallas kernels  29 us (16%)
  starting transfers between devices  24.8 us (13%)
  waiting for transfers between devices  15.3 us (8%)
    all_to_all x2, blocking collectives, everyone(): return lax.all_to_all(value, 'level', 0, 0)  112 us
    ppermute x15, starting transfers between devices, send(): return lax.ppermute(value, ('level', 'tile'), pairs)  24.8 us
    ppermute x15, waiting for transfers between devices, send(): return lax.ppermute(value, ('level', 'tile'), pairs)  15.3 us
    pallas_call x4, Pallas kernels, inner_rates(): pl.pallas_call(inner_kernel, out_shape=pltpu.VMEM((LEVELS, WIDE, CELLS),...  10.7 us
    pallas_call x1, Pallas kernels, cut(): pl.pallas_call(cut_kernel, out_shape=[pltpu.VMEM((LEVELS, 3 * WIDE, CELLS...  7.98 us
    pallas_call x4, Pallas kernels, one_step(): pl.pallas_call(functools.partial(step_kernel, step, n_in, n_out), out_sha...  6.52 us
  transfers between devices with their start and end apart: 15, of which 4 were waited for; matrix products, arithmetic and copies ran while one was open for 0% of the time, Pallas kernels for 9%

profile of v3, /device:TPU:89, one launch (start us, length us, event | category | flops | bytes accessed | tf_op | source)
XLA Modules:
  0.0 183.0 jit_solution(9189318532239106846)
XLA Ops:
  0.0 1.6 copy-done
  1.6 8.0 %cut.1 = (f32[8,816,256]{2,1,0:T(8,128)S(1)}, f32[272,256]{1,0:T(8,128)S(1)}, f32[272,256]{1,0:T(8,128)S(1)}, f32[272,256]{1,0:T(8,128)S(1)}, f32[272,256]{1,0:T...) custom-call(f32[256,2048]{1,0:T(8,128)S(1)} %bitcast.3, ...), custom_call_target="tpu_custom_call" | custom-call | tf_op jit(solution)/shard_map/cut/pallas_call | solution.py:131
  9.6 80.9 %all_to_all.10.u_ref.fields_ref.refs_0_ = f32[8,816,256]{2,1,0:T(8,128)S(1)} all-to-all(f32[8,816,256]{2,1,0:T(8,128)S(1)} %get-tuple-element.44), channel_id=1, replica_groups=mesh['level'=8,'tile'=16] {'level'}, dimensions={0} | all-to-all | bytes 13369344 | tf_op jit(solution)/shard_map/all_to_all | solution.py:62
  90.5 0.5 edges.1
  91.0 1.0 collective-permute-start.2
  92.0 1.0 collective-permute-start.3
  93.0 2.3 %collective-permute-start = (f32[272,256]{1,0:T(8,128)S(1)}, f32[272,256]{1,0:T(8,128)S(1)}, u32[]{:S(2)}, u32[]{:S(2)}) collective-permute-start(f32[272,256]{1,0:T(8,128)S(1)} %get-tuple-element.47), channel_id=1, source_target_pairs={{0,1},{1,0},{2,3},{3,2},{4,5},{5,4},{6,7},{7,6},{8,9},{9,8},{10,11... | collective-permute-start | bytes 835592 | tf_op jit(solution)/shard_map/ppermute | solution.py:58
  95.2 0.9 collective-permute-start.1
  96.1 0.7 collective-permute-done.2.refs_1_
  96.8 2.1 %collective-permute-done.3.refs_3_ = f32[272,256]{1,0:T(8,128)S(1)} collective-permute-done((f32[272,256]{1,0:T(8,128)S(1)}, f32[272,256]{1,0:T(8,128)S(1)}, u32[]{:S(2)}, u32[]{:S(2)}) %collective-permute-start.3) | collective-permute-done | bytes 278560 | tf_op jit(solution)/shard_map/ppermute | solution.py:58
  98.9 2.7 %collective-permute-start.6 = (f32[272,256]{1,0:T(8,128)S(1)}, f32[272,256]{1,0:T(8,128)S(1)}, u32[]{:S(2)}, u32[]{:S(2)}) collective-permute-start(f32[272,256]{1,0:T(8,128)S(1)} %get-tuple-element.64), channel_id=1, source_target_pairs={{0,64},{1,65},{2,66},{3,67},{4,68},{5,69},{6,70},{7,71},{8,72},{9,... | collective-permute-start | bytes 835592 | tf_op jit(solution)/shard_map/ppermute | solution.py:58
  101.9 1.7 collective-permute-start.8
  103.6 1.0 weights.1
  104.6 2.7 %inner_0.1.rate_ref = f32[8,272,256]{2,1,0:T(8,128)S(1)} custom-call(f32[8,816,256]{2,1,0:T(8,128)S(1)} %all_to_all.10.u_ref.fields_ref.refs_0_, bf16[768,512]{1,0:T(8,128)(2,1)S(1)} %get-tuple-element.45.main_ref, f32[8,256]{1,0:T(8,128)S(1)} %get-tuple-element.46.diff_ref), custom_call_target="tpu_custom_call" | custom-call | tf_op jit(solution)/shard_map/inner_0/pallas_call | solution.py:246
  107.3 1.8 step_0.1
  109.0 3.8 %collective-permute-start.4 = (f32[272,256]{1,0:T(8,128)S(1)}, f32[272,256]{1,0:T(8,128)S(1)}, u32[]{:S(2)}, u32[]{:S(2)}) collective-permute-start(f32[272,256]{1,0:T(8,128)S(1)} %get-tuple-element.57), channel_id=1, source_target_pairs={{0,1},{1,0},{2,3},{3,2},{4,5},{5,4},{6,7},{7,6},{8,9},{9,8},{10,11... | collective-permute-start | bytes 835592 | tf_op jit(solution)/shard_map/ppermute | solution.py:58
  112.9 1.0 collective-permute-start.5
  113.9 2.7 %inner_1.1.rate_ref = f32[8,272,256]{2,1,0:T(8,128)S(1)} custom-call(f32[8,272,256]{2,1,0:T(8,128)S(1)} %get-tuple-element.56.u_ref, bf16[768,512]{1,0:T(8,128)(2,1)S(1)} %get-tuple-element.45.main_ref, f32[8,256]{1,0:T(8,128)S(1)} %get-tuple-element.46.diff_ref), custom_call_target="tpu_custom_call" | custom-call | tf_op jit(solution)/shard_map/inner_1/pallas_call | solution.py:246
  116.6 3.4 %collective-permute-start.11 = (f32[272,256]{1,0:T(8,128)S(1)}, f32[272,256]{1,0:T(8,128)S(1)}, u32[]{:S(2)}, u32[]{:S(2)}) collective-permute-start(f32[272,256]{1,0:T(8,128)S(1)} %get-tuple-element.73), channel_id=1, source_target_pairs={{0,96},{1,97},{2,98},{3,99},{4,100},{5,101},{6,102},{7,103},{8,104... | collective-permute-start | bytes 835592 | tf_op jit(solution)/shard_map/ppermute | solution.py:58
  120.1 2.2 %collective-permute-start.12 = (f32[272,256]{1,0:T(8,128)S(1)}, f32[272,256]{1,0:T(8,128)S(1)}, u32[]{:S(2)}, u32[]{:S(2)}) collective-permute-start(f32[272,256]{1,0:T(8,128)S(1)} %get-tuple-element.75), channel_id=1, source_target_pairs={{0,112},{1,113},{2,114},{3,115},{4,116},{5,117},{6,118},{7,119},{8... | collective-permute-start | bytes 835592 | tf_op jit(solution)/shard_map/ppermute | solution.py:58
  122.3 2.1 %step_1.1 = (f32[8,272,256]{2,1,0:T(8,128)S(1)}, f32[272,256]{1,0:T(8,128)S(1)}, f32[272,256]{1,0:T(8,128)S(1)}, f32[8,272,256]{2,1,0:T(8,128)S(1)}, f32[8,272,256]{2,1,0:T(8,128)S(1)}) custom-call(f32[8,272,256]{2,1,0:T(8,128)S(1)} %get-tuple-element.56.u_ref, f32[8,272,256]{2,1,0:T(8,128)S(1)} %inner_1.1.rate_ref, ...), custom_call_target="tpu_custom_call" | custom-call | tf_op jit(solution)/shard_map/step_1/pallas_call | solution.py:311
  124.4 0.9 collective-permute-start.9
  125.3 2.7 %collective-permute-start.10 = (f32[272,256]{1,0:T(8,128)S(1)}, f32[272,256]{1,0:T(8,128)S(1)}, u32[]{:S(2)}, u32[]{:S(2)}) collective-permute-start(f32[272,256]{1,0:T(8,128)S(1)} %get-tuple-element.71), channel_id=1, source_target_pairs={{0,15},{1,2},{2,1},{3,4},{4,3},{5,6},{6,5},{7,8},{8,7},{9,10},{10,... | collective-permute-start | bytes 835592 | tf_op jit(solution)/shard_map/ppermute | solution.py:58
  128.0 2.7 %inner_2.1.rate_ref = f32[8,272,256]{2,1,0:T(8,128)S(1)} custom-call(f32[8,272,256]{2,1,0:T(8,128)S(1)} %get-tuple-element.69.u_ref, bf16[768,512]{1,0:T(8,128)(2,1)S(1)} %get-tuple-element.45.main_ref, f32[8,256]{1,0:T(8,128)S(1)} %get-tuple-element.46.diff_ref), custom_call_target="tpu_custom_call" | custom-call | tf_op jit(solution)/shard_map/inner_2/pallas_call | solution.py:246
  130.7 7.2 %collective-permute-done.12.refs_7_ = f32[272,256]{1,0:T(8,128)S(1)} collective-permute-done((f32[272,256]{1,0:T(8,128)S(1)}, f32[272,256]{1,0:T(8,128)S(1)}, u32[]{:S(2)}, u32[]{:S(2)}) %collective-permute-start.12) | collective-permute-done | bytes 278560 | tf_op jit(solution)/shard_map/ppermute | solution.py:58
  138.3 1.7 step_2.1
  140.0 0.9 collective-permute-start.13
  140.9 2.7 %inner_3.1.rate_ref = f32[8,272,256]{2,1,0:T(8,128)S(1)} custom-call(f32[8,272,256]{2,1,0:T(8,128)S(1)} %get-tuple-element.79.u_ref, bf16[768,512]{1,0:T(8,128)(2,1)S(1)} %get-tuple-element.45.main_ref, f32[8,256]{1,0:T(8,128)S(1)} %get-tuple-element.46.diff_ref), custom_call_target="tpu_custom_call" | custom-call | tf_op jit(solution)/shard_map/inner_3/pallas_call | solution.py:246
  143.6 5.3 %collective-permute-done.14.outer_ref = f32[272,256]{1,0:T(8,128)S(1)} collective-permute-done((f32[272,256]{1,0:T(8,128)S(1)}, f32[272,256]{1,0:T(8,128)S(1)}, u32[]{:S(2)}, u32[]{:S(2)}) %collective-permute-start.14) | collective-permute-done | bytes 278560 | tf_op jit(solution)/shard_map/ppermute | solution.py:58
  149.0 0.9 step_3.1
  150.1 30.8 %all_to_all.11.parts = f32[8,256,256]{2,1,0:T(8,128)S(1)} all-to-all(f32[8,256,256]{2,1,0:T(8,128)S(1)} %slice.4), channel_id=1, replica_groups=mesh['level'=8,'tile'=16] {'level'}, dimensions={0} | all-to-all | bytes 4194304 | tf_op jit(solution)/shard_map/all_to_all | solution.py:62
  180.9 1.9 %join.1 = f32[16,16,2048]{2,1,0:T(8,128)} custom-call(f32[8,256,256]{2,1,0:T(8,128)S(1)} %all_to_all.11.parts), custom_call_target="tpu_custom_call" | custom-call | tf_op jit(solution)/shard_map/join/pallas_call | solution.py:395
  (23 shorter events, 0.9 us)
Async XLA Ops:
  0.0 1.6 copy-start
  90.5 13.1 %copy-start.3 = (f32[16]{0:T(128)S(1)}, f32[16]{0:T(128)}, u32[]{:S(2)}) copy-start(f32[16]{0:T(128)} %param.7) | copy-start | bytes 196
  90.5 13.1 %copy-start.1 = (f32[16,16]{1,0:T(8,128)S(1)}, f32[16,16]{1,0:T(8,128)}, u32[]{:S(2)}) copy-start(f32[16,16]{1,0:T(8,128)} %lin_ref.1) | copy-start | bytes 3076
  90.5 13.1 %copy-start.2 = (f32[16,16]{1,0:T(8,128)S(1)}, f32[16,16]{1,0:T(8,128)}, u32[]{:S(2)}) copy-start(f32[16,16]{1,0:T(8,128)} %coup_ref.1) | copy-start | bytes 3076
  91.0 5.8 %collective-permute-start.2 = (f32[272,256]{1,0:T(8,128)S(1)}, f32[272,256]{1,0:T(8,128)S(1)}, u32[]{:S(2)}, u32[]{:S(2)}) collective-permute-start(f32[272,256]{1,0:T(8,128)S(1)} %get-tuple-element.53), channel_id=1, source_target_pairs={{0,16},{1,17},{2,18},{3,19},{4,20},{5,21},{6,22},{7,23},{8,24},{9,... | collective-permute-start | bytes 835592 | tf_op jit(solution)/shard_map/ppermute | solution.py:58
  92.0 6.9 %collective-permute-start.3 = (f32[272,256]{1,0:T(8,128)S(1)}, f32[272,256]{1,0:T(8,128)S(1)}, u32[]{:S(2)}, u32[]{:S(2)}) collective-permute-start(f32[272,256]{1,0:T(8,128)S(1)} %get-tuple-element.55), channel_id=1, source_target_pairs={{0,48},{1,49},{2,50},{3,51},{4,52},{5,53},{6,54},{7,55},{8,56},{9,... | collective-permute-start | bytes 835592 | tf_op jit(solution)/shard_map/ppermute | solution.py:58
  93.0 14.3 %collective-permute-start = (f32[272,256]{1,0:T(8,128)S(1)}, f32[272,256]{1,0:T(8,128)S(1)}, u32[]{:S(2)}, u32[]{:S(2)}) collective-permute-start(f32[272,256]{1,0:T(8,128)S(1)} %get-tuple-element.47), channel_id=1, source_target_pairs={{0,1},{1,0},{2,3},{3,2},{4,5},{5,4},{6,7},{7,6},{8,9},{9,8},{10,11... | collective-permute-start | bytes 835592 | tf_op jit(solution)/shard_map/ppermute | solution.py:58
  95.2 12.0 %collective-permute-start.1 = (f32[272,256]{1,0:T(8,128)S(1)}, f32[272,256]{1,0:T(8,128)S(1)}, u32[]{:S(2)}, u32[]{:S(2)}) collective-permute-start(f32[272,256]{1,0:T(8,128)S(1)} %get-tuple-element.48), channel_id=1, source_target_pairs={{0,15},{1,2},{2,1},{3,4},{4,3},{5,6},{6,5},{7,8},{8,7},{9,10},{10,... | collective-permute-start | bytes 835592 | tf_op jit(solution)/shard_map/ppermute | solution.py:58
  98.9 17.7 %collective-permute-start.6 = (f32[272,256]{1,0:T(8,128)S(1)}, f32[272,256]{1,0:T(8,128)S(1)}, u32[]{:S(2)}, u32[]{:S(2)}) collective-permute-start(f32[272,256]{1,0:T(8,128)S(1)} %get-tuple-element.64), channel_id=1, source_target_pairs={{0,64},{1,65},{2,66},{3,67},{4,68},{5,69},{6,70},{7,71},{8,72},{9,... | collective-permute-start | bytes 835592 | tf_op jit(solution)/shard_map/ppermute | solution.py:58
  101.6 15.0 %collective-permute-start.7 = (f32[272,256]{1,0:T(8,128)S(1)}, f32[272,256]{1,0:T(8,128)S(1)}, u32[]{:S(2)}, u32[]{:S(2)}) collective-permute-start(f32[272,256]{1,0:T(8,128)S(1)} %get-tuple-element.66), channel_id=1, source_target_pairs={{0,32},{1,33},{2,34},{3,35},{4,36},{5,37},{6,38},{7,39},{8,40},{9,... | collective-permute-start | bytes 835592 | tf_op jit(solution)/shard_map/ppermute | solution.py:58
  101.9 14.8 %collective-permute-start.8 = (f32[272,256]{1,0:T(8,128)S(1)}, f32[272,256]{1,0:T(8,128)S(1)}, u32[]{:S(2)}, u32[]{:S(2)}) collective-permute-start(f32[272,256]{1,0:T(8,128)S(1)} %get-tuple-element.68), channel_id=1, source_target_pairs={{0,80},{1,81},{2,82},{3,83},{4,84},{5,85},{6,86},{7,87},{8,88},{9,... | collective-permute-start | bytes 835592 | tf_op jit(solution)/shard_map/ppermute | solution.py:58
  109.0 13.2 %collective-permute-start.4 = (f32[272,256]{1,0:T(8,128)S(1)}, f32[272,256]{1,0:T(8,128)S(1)}, u32[]{:S(2)}, u32[]{:S(2)}) collective-permute-start(f32[272,256]{1,0:T(8,128)S(1)} %get-tuple-element.57), channel_id=1, source_target_pairs={{0,1},{1,0},{2,3},{3,2},{4,5},{5,4},{6,7},{7,6},{8,9},{9,8},{10,11... | collective-permute-start | bytes 835592 | tf_op jit(solution)/shard_map/ppermute | solution.py:58
  112.9 9.4 %collective-permute-start.5 = (f32[272,256]{1,0:T(8,128)S(1)}, f32[272,256]{1,0:T(8,128)S(1)}, u32[]{:S(2)}, u32[]{:S(2)}) collective-permute-start(f32[272,256]{1,0:T(8,128)S(1)} %get-tuple-element.58), channel_id=1, source_target_pairs={{0,15},{1,2},{2,1},{3,4},{4,3},{5,6},{6,5},{7,8},{8,7},{9,10},{10,... | collective-permute-start | bytes 835592 | tf_op jit(solution)/shard_map/ppermute | solution.py:58
  116.6 14.0 %collective-permute-start.11 = (f32[272,256]{1,0:T(8,128)S(1)}, f32[272,256]{1,0:T(8,128)S(1)}, u32[]{:S(2)}, u32[]{:S(2)}) collective-permute-start(f32[272,256]{1,0:T(8,128)S(1)} %get-tuple-element.73), channel_id=1, source_target_pairs={{0,96},{1,97},{2,98},{3,99},{4,100},{5,101},{6,102},{7,103},{8,104... | collective-permute-start | bytes 835592 | tf_op jit(solution)/shard_map/ppermute | solution.py:58
  120.1 17.8 %collective-permute-start.12 = (f32[272,256]{1,0:T(8,128)S(1)}, f32[272,256]{1,0:T(8,128)S(1)}, u32[]{:S(2)}, u32[]{:S(2)}) collective-permute-start(f32[272,256]{1,0:T(8,128)S(1)} %get-tuple-element.75), channel_id=1, source_target_pairs={{0,112},{1,113},{2,114},{3,115},{4,116},{5,117},{6,118},{7,119},{8... | collective-permute-start | bytes 835592 | tf_op jit(solution)/shard_map/ppermute | solution.py:58
  124.4 13.9 %collective-permute-start.9 = (f32[272,256]{1,0:T(8,128)S(1)}, f32[272,256]{1,0:T(8,128)S(1)}, u32[]{:S(2)}, u32[]{:S(2)}) collective-permute-start(f32[272,256]{1,0:T(8,128)S(1)} %get-tuple-element.70), channel_id=1, source_target_pairs={{0,1},{1,0},{2,3},{3,2},{4,5},{5,4},{6,7},{7,6},{8,9},{9,8},{10,11... | collective-permute-start | bytes 835592 | tf_op jit(solution)/shard_map/ppermute | solution.py:58
  125.3 13.0 %collective-permute-start.10 = (f32[272,256]{1,0:T(8,128)S(1)}, f32[272,256]{1,0:T(8,128)S(1)}, u32[]{:S(2)}, u32[]{:S(2)}) collective-permute-start(f32[272,256]{1,0:T(8,128)S(1)} %get-tuple-element.71), channel_id=1, source_target_pairs={{0,15},{1,2},{2,1},{3,4},{4,3},{5,6},{6,5},{7,8},{8,7},{9,10},{10,... | collective-permute-start | bytes 835592 | tf_op jit(solution)/shard_map/ppermute | solution.py:58
  140.0 3.6 %collective-permute-start.13 = (f32[272,256]{1,0:T(8,128)S(1)}, f32[272,256]{1,0:T(8,128)S(1)}, u32[]{:S(2)}, u32[]{:S(2)}) collective-permute-start(f32[272,256]{1,0:T(8,128)S(1)} %get-tuple-element.80), channel_id=1, source_target_pairs={{0,1},{1,0},{2,3},{3,2},{4,5},{5,4},{6,7},{7,6},{8,9},{9,8},{10,11... | collective-permute-start | bytes 835592 | tf_op jit(solution)/shard_map/ppermute | solution.py:58
  140.9 8.1 %collective-permute-start.14 = (f32[272,256]{1,0:T(8,128)S(1)}, f32[272,256]{1,0:T(8,128)S(1)}, u32[]{:S(2)}, u32[]{:S(2)}) collective-permute-start(f32[272,256]{1,0:T(8,128)S(1)} %get-tuple-element.81), channel_id=1, source_target_pairs={{0,15},{1,2},{2,1},{3,4},{4,3},{5,6},{6,5},{7,8},{8,7},{9,10},{10,... | collective-permute-start | bytes 835592 | tf_op jit(solution)/shard_map/ppermute | solution.py:58

commit v4 on v3

--- a/solution.py
+++ b/solution.py
@@ -141,7 +141,7 @@
             pltpu.SemaphoreType.DMA((4,)),
             pltpu.SemaphoreType.DMA((LEVELS,)),
         ],
-        compiler_params=params(40),
+        compiler_params=params(54),
         name="cut",
     )(state, hist)
     return outs[0], outs[1:]

time: 186 us -> 185 us (level)
  no operation moved by 1% of the time
where the time goes in v4:
time: 185 us; the launch traced here: 182 us
  blocking collectives  112 us (61%)
  Pallas kernels  29.2 us (16%)
  starting transfers between devices  24.8 us (13%)
  waiting for transfers between devices  15.3 us (8%)
    all_to_all x2, blocking collectives, everyone(): return lax.all_to_all(value, 'level', 0, 0)  112 us
    ppermute x15, starting transfers between devices, send(): return lax.ppermute(value, ('level', 'tile'), pairs)  24.8 us
    ppermute x15, waiting for transfers between devices, send(): return lax.ppermute(value, ('level', 'tile'), pairs)  15.3 us
    pallas_call x4, Pallas kernels, inner_rates(): pl.pallas_call(inner_kernel, out_shape=pltpu.VMEM((LEVELS, WIDE, CELLS),...  10.7 us
    pallas_call x1, Pallas kernels, cut(): pl.pallas_call(cut_kernel, out_shape=[pltpu.VMEM((LEVELS, 3 * WIDE, CELLS...  8.14 us
    pallas_call x4, Pallas kernels, one_step(): pl.pallas_call(functools.partial(step_kernel, step, n_in, n_out), out_sha...  6.52 us
  transfers between devices with their start and end apart: 15, of which 4 were waited for; matrix products, arithmetic and copies ran while one was open for 0% of the time, Pallas kernels for 9%

profile of v4, /device:TPU:89, one launch (start us, length us, event | category | flops | bytes accessed | tf_op | source)
XLA Modules:
  0.0 182.0 jit_solution(13407378768041647383)
XLA Ops:
  0.0 8.1 %cut.1 = (f32[8,816,256]{2,1,0:T(8,128)S(1)}, f32[272,256]{1,0:T(8,128)}, f32[272,256]{1,0:T(8,128)}, f32[272,256]{1,0:T(8,128)}, f32[272,256]{1,0:T(8,128)}, /*...) custom-call(f32[256,2048]{1,0:T(8,128)} %bitcast.4, f32[3,256,2048]{2,1,0:T(8,128)} %bitcast.3), custom_call_target="tpu_custom_call" | custom-call | tf_op jit(solution)/shard_map/cut/pallas_call | solution.py:131
  8.1 80.9 %all_to_all.10.u_ref.fields_ref.refs_0_ = f32[8,816,256]{2,1,0:T(8,128)S(1)} all-to-all(f32[8,816,256]{2,1,0:T(8,128)S(1)} %get-tuple-element.44), channel_id=1, replica_groups=mesh['level'=8,'tile'=16] {'level'}, dimensions={0} | all-to-all | bytes 13369344 | tf_op jit(solution)/shard_map/all_to_all | solution.py:62
  89.1 0.5 edges.1
  90.0 0.9 collective-permute-start.2
  90.9 1.0 collective-permute-start.3
  91.9 2.3 %collective-permute-start = (f32[272,256]{1,0:T(8,128)S(1)}, f32[272,256]{1,0:T(8,128)S(1)}, u32[]{:S(2)}, u32[]{:S(2)}) collective-permute-start(f32[272,256]{1,0:T(8,128)S(1)} %get-tuple-element.47), channel_id=1, source_target_pairs={{0,1},{1,0},{2,3},{3,2},{4,5},{5,4},{6,7},{7,6},{8,9},{9,8},{10,11... | collective-permute-start | bytes 835592 | tf_op jit(solution)/shard_map/ppermute | solution.py:58
  94.2 0.9 collective-permute-start.1
  95.0 0.7 collective-permute-done.2.refs_1_
  95.8 2.1 %collective-permute-done.3.refs_3_ = f32[272,256]{1,0:T(8,128)S(1)} collective-permute-done((f32[272,256]{1,0:T(8,128)S(1)}, f32[272,256]{1,0:T(8,128)S(1)}, u32[]{:S(2)}, u32[]{:S(2)}) %collective-permute-start.3) | collective-permute-done | bytes 278560 | tf_op jit(solution)/shard_map/ppermute | solution.py:58
  97.8 2.7 %collective-permute-start.6 = (f32[272,256]{1,0:T(8,128)S(1)}, f32[272,256]{1,0:T(8,128)S(1)}, u32[]{:S(2)}, u32[]{:S(2)}) collective-permute-start(f32[272,256]{1,0:T(8,128)S(1)} %copy-done.8), channel_id=1, source_target_pairs={{0,64},{1,65},{2,66},{3,67},{4,68},{5,69},{6,70},{7,71},{8,72},{9,... | collective-permute-start | bytes 835592 | tf_op jit(solution)/shard_map/ppermute | solution.py:58
  100.8 1.7 collective-permute-start.8
  102.5 1.0 weights.1
  103.5 2.7 %inner_0.1.rate_ref = f32[8,272,256]{2,1,0:T(8,128)S(1)} custom-call(f32[8,816,256]{2,1,0:T(8,128)S(1)} %all_to_all.10.u_ref.fields_ref.refs_0_, bf16[768,512]{1,0:T(8,128)(2,1)S(1)} %get-tuple-element.45.main_ref, f32[8,256]{1,0:T(8,128)S(1)} %get-tuple-element.46.diff_ref), custom_call_target="tpu_custom_call" | custom-call | tf_op jit(solution)/shard_map/inner_0/pallas_call | solution.py:246
  106.2 1.8 step_0.1
  108.0 3.8 %collective-permute-start.4 = (f32[272,256]{1,0:T(8,128)S(1)}, f32[272,256]{1,0:T(8,128)S(1)}, u32[]{:S(2)}, u32[]{:S(2)}) collective-permute-start(f32[272,256]{1,0:T(8,128)S(1)} %get-tuple-element.57), channel_id=1, source_target_pairs={{0,1},{1,0},{2,3},{3,2},{4,5},{5,4},{6,7},{7,6},{8,9},{9,8},{10,11... | collective-permute-start | bytes 835592 | tf_op jit(solution)/shard_map/ppermute | solution.py:58
  111.8 1.0 collective-permute-start.5
  112.8 2.7 %inner_1.1.rate_ref = f32[8,272,256]{2,1,0:T(8,128)S(1)} custom-call(f32[8,272,256]{2,1,0:T(8,128)S(1)} %get-tuple-element.56.u_ref, bf16[768,512]{1,0:T(8,128)(2,1)S(1)} %get-tuple-element.45.main_ref, f32[8,256]{1,0:T(8,128)S(1)} %get-tuple-element.46.diff_ref), custom_call_target="tpu_custom_call" | custom-call | tf_op jit(solution)/shard_map/inner_1/pallas_call | solution.py:246
  115.6 3.4 %collective-permute-start.11 = (f32[272,256]{1,0:T(8,128)S(1)}, f32[272,256]{1,0:T(8,128)S(1)}, u32[]{:S(2)}, u32[]{:S(2)}) collective-permute-start(f32[272,256]{1,0:T(8,128)S(1)} %copy-done.5), channel_id=1, source_target_pairs={{0,96},{1,97},{2,98},{3,99},{4,100},{5,101},{6,102},{7,103},{8,104... | collective-permute-start | bytes 835592 | tf_op jit(solution)/shard_map/ppermute | solution.py:58
  119.0 2.2 %collective-permute-start.12 = (f32[272,256]{1,0:T(8,128)S(1)}, f32[272,256]{1,0:T(8,128)S(1)}, u32[]{:S(2)}, u32[]{:S(2)}) collective-permute-start(f32[272,256]{1,0:T(8,128)S(1)} %copy-done.4), channel_id=1, source_target_pairs={{0,112},{1,113},{2,114},{3,115},{4,116},{5,117},{6,118},{7,119},{8... | collective-permute-start | bytes 835592 | tf_op jit(solution)/shard_map/ppermute | solution.py:58
  121.2 2.1 %step_1.1 = (f32[8,272,256]{2,1,0:T(8,128)S(1)}, f32[272,256]{1,0:T(8,128)S(1)}, f32[272,256]{1,0:T(8,128)S(1)}, f32[8,272,256]{2,1,0:T(8,128)S(1)}, f32[8,272,256]{2,1,0:T(8,128)S(1)}) custom-call(f32[8,272,256]{2,1,0:T(8,128)S(1)} %get-tuple-element.56.u_ref, f32[8,272,256]{2,1,0:T(8,128)S(1)} %inner_1.1.rate_ref, ...), custom_call_target="tpu_custom_call" | custom-call | tf_op jit(solution)/shard_map/step_1/pallas_call | solution.py:311
  123.3 0.9 collective-permute-start.9
  124.3 2.7 %collective-permute-start.10 = (f32[272,256]{1,0:T(8,128)S(1)}, f32[272,256]{1,0:T(8,128)S(1)}, u32[]{:S(2)}, u32[]{:S(2)}) collective-permute-start(f32[272,256]{1,0:T(8,128)S(1)} %get-tuple-element.71), channel_id=1, source_target_pairs={{0,15},{1,2},{2,1},{3,4},{4,3},{5,6},{6,5},{7,8},{8,7},{9,10},{10,... | collective-permute-start | bytes 835592 | tf_op jit(solution)/shard_map/ppermute | solution.py:58
  126.9 2.7 %inner_2.1.rate_ref = f32[8,272,256]{2,1,0:T(8,128)S(1)} custom-call(f32[8,272,256]{2,1,0:T(8,128)S(1)} %get-tuple-element.69.u_ref, bf16[768,512]{1,0:T(8,128)(2,1)S(1)} %get-tuple-element.45.main_ref, f32[8,256]{1,0:T(8,128)S(1)} %get-tuple-element.46.diff_ref), custom_call_target="tpu_custom_call" | custom-call | tf_op jit(solution)/shard_map/inner_2/pallas_call | solution.py:246
  129.6 7.2 %collective-permute-done.12.refs_7_ = f32[272,256]{1,0:T(8,128)S(1)} collective-permute-done((f32[272,256]{1,0:T(8,128)S(1)}, f32[272,256]{1,0:T(8,128)S(1)}, u32[]{:S(2)}, u32[]{:S(2)}) %collective-permute-start.12) | collective-permute-done | bytes 278560 | tf_op jit(solution)/shard_map/ppermute | solution.py:58
  136.8 0.4 gather.1.refs_0_
  137.2 1.7 step_2.1
  139.0 0.9 collective-permute-start.13
  139.9 2.7 %inner_3.1.rate_ref = f32[8,272,256]{2,1,0:T(8,128)S(1)} custom-call(f32[8,272,256]{2,1,0:T(8,128)S(1)} %get-tuple-element.79.u_ref, bf16[768,512]{1,0:T(8,128)(2,1)S(1)} %get-tuple-element.45.main_ref, f32[8,256]{1,0:T(8,128)S(1)} %get-tuple-element.46.diff_ref), custom_call_target="tpu_custom_call" | custom-call | tf_op jit(solution)/shard_map/inner_3/pallas_call | solution.py:246
  142.6 5.3 %collective-permute-done.14.outer_ref = f32[272,256]{1,0:T(8,128)S(1)} collective-permute-done((f32[272,256]{1,0:T(8,128)S(1)}, f32[272,256]{1,0:T(8,128)S(1)}, u32[]{:S(2)}, u32[]{:S(2)}) %collective-permute-start.14) | collective-permute-done | bytes 278560 | tf_op jit(solution)/shard_map/ppermute | solution.py:58
  147.9 0.9 step_3.1
  149.0 30.9 %all_to_all.11.parts = f32[8,256,256]{2,1,0:T(8,128)S(1)} all-to-all(f32[8,256,256]{2,1,0:T(8,128)S(1)} %slice.4), channel_id=1, replica_groups=mesh['level'=8,'tile'=16] {'level'}, dimensions={0} | all-to-all | bytes 4194304 | tf_op jit(solution)/shard_map/all_to_all | solution.py:62
  179.9 1.9 %join.1 = f32[16,16,2048]{2,1,0:T(8,128)} custom-call(f32[8,256,256]{2,1,0:T(8,128)S(1)} %all_to_all.11.parts), custom_call_target="tpu_custom_call" | custom-call | tf_op jit(solution)/shard_map/join/pallas_call | solution.py:395
  (37 shorter events, 1.0 us)
Async XLA Ops:
  89.1 1.0 copy-start.10
  89.1 1.8 %copy-start.9 = (f32[272,256]{1,0:T(8,128)S(1)}, f32[272,256]{1,0:T(8,128)}, u32[]{:S(2)}) copy-start(f32[272,256]{1,0:T(8,128)} %get-tuple-element.55) | copy-start | bytes 835588
  89.1 8.8 %copy-start.8 = (f32[272,256]{1,0:T(8,128)S(1)}, f32[272,256]{1,0:T(8,128)}, u32[]{:S(2)}) copy-start(f32[272,256]{1,0:T(8,128)} %get-tuple-element.64) | copy-start | bytes 835588
  89.1 11.5 %copy-start.7 = (f32[272,256]{1,0:T(8,128)S(1)}, f32[272,256]{1,0:T(8,128)}, u32[]{:S(2)}) copy-start(f32[272,256]{1,0:T(8,128)} %get-tuple-element.66) | copy-start | bytes 835588
  89.1 11.7 %copy-start.6 = (f32[272,256]{1,0:T(8,128)S(1)}, f32[272,256]{1,0:T(8,128)}, u32[]{:S(2)}) copy-start(f32[272,256]{1,0:T(8,128)} %get-tuple-element.68) | copy-start | bytes 835588
  89.1 13.4 %copy-start.3 = (f32[16]{0:T(128)S(1)}, f32[16]{0:T(128)}, u32[]{:S(2)}) copy-start(f32[16]{0:T(128)} %param.7) | copy-start | bytes 196
  89.1 13.4 %copy-start.1 = (f32[16,16]{1,0:T(8,128)S(1)}, f32[16,16]{1,0:T(8,128)}, u32[]{:S(2)}) copy-start(f32[16,16]{1,0:T(8,128)} %lin_ref.1) | copy-start | bytes 3076
  89.1 13.4 %copy-start.2 = (f32[16,16]{1,0:T(8,128)S(1)}, f32[16,16]{1,0:T(8,128)}, u32[]{:S(2)}) copy-start(f32[16,16]{1,0:T(8,128)} %coup_ref.1) | copy-start | bytes 3076
  90.0 5.7 %collective-permute-start.2 = (f32[272,256]{1,0:T(8,128)S(1)}, f32[272,256]{1,0:T(8,128)S(1)}, u32[]{:S(2)}, u32[]{:S(2)}) collective-permute-start(f32[272,256]{1,0:T(8,128)S(1)} %copy-done.10), channel_id=1, source_target_pairs={{0,16},{1,17},{2,18},{3,19},{4,20},{5,21},{6,22},{7,23},{8,24},{9,... | collective-permute-start | bytes 835592 | tf_op jit(solution)/shard_map/ppermute | solution.py:58
  90.9 6.9 %collective-permute-start.3 = (f32[272,256]{1,0:T(8,128)S(1)}, f32[272,256]{1,0:T(8,128)S(1)}, u32[]{:S(2)}, u32[]{:S(2)}) collective-permute-start(f32[272,256]{1,0:T(8,128)S(1)} %copy-done.9), channel_id=1, source_target_pairs={{0,48},{1,49},{2,50},{3,51},{4,52},{5,53},{6,54},{7,55},{8,56},{9,... | collective-permute-start | bytes 835592 | tf_op jit(solution)/shard_map/ppermute | solution.py:58
  91.9 14.3 %collective-permute-start = (f32[272,256]{1,0:T(8,128)S(1)}, f32[272,256]{1,0:T(8,128)S(1)}, u32[]{:S(2)}, u32[]{:S(2)}) collective-permute-start(f32[272,256]{1,0:T(8,128)S(1)} %get-tuple-element.47), channel_id=1, source_target_pairs={{0,1},{1,0},{2,3},{3,2},{4,5},{5,4},{6,7},{7,6},{8,9},{9,8},{10,11... | collective-permute-start | bytes 835592 | tf_op jit(solution)/shard_map/ppermute | solution.py:58
  94.2 12.0 %collective-permute-start.1 = (f32[272,256]{1,0:T(8,128)S(1)}, f32[272,256]{1,0:T(8,128)S(1)}, u32[]{:S(2)}, u32[]{:S(2)}) collective-permute-start(f32[272,256]{1,0:T(8,128)S(1)} %get-tuple-element.48), channel_id=1, source_target_pairs={{0,15},{1,2},{2,1},{3,4},{4,3},{5,6},{6,5},{7,8},{8,7},{9,10},{10,... | collective-permute-start | bytes 835592 | tf_op jit(solution)/shard_map/ppermute | solution.py:58
  97.8 17.7 %collective-permute-start.6 = (f32[272,256]{1,0:T(8,128)S(1)}, f32[272,256]{1,0:T(8,128)S(1)}, u32[]{:S(2)}, u32[]{:S(2)}) collective-permute-start(f32[272,256]{1,0:T(8,128)S(1)} %copy-done.8), channel_id=1, source_target_pairs={{0,64},{1,65},{2,66},{3,67},{4,68},{5,69},{6,70},{7,71},{8,72},{9,... | collective-permute-start | bytes 835592 | tf_op jit(solution)/shard_map/ppermute | solution.py:58
  100.5 15.0 %collective-permute-start.7 = (f32[272,256]{1,0:T(8,128)S(1)}, f32[272,256]{1,0:T(8,128)S(1)}, u32[]{:S(2)}, u32[]{:S(2)}) collective-permute-start(f32[272,256]{1,0:T(8,128)S(1)} %copy-done.7), channel_id=1, source_target_pairs={{0,32},{1,33},{2,34},{3,35},{4,36},{5,37},{6,38},{7,39},{8,40},{9,... | collective-permute-start | bytes 835592 | tf_op jit(solution)/shard_map/ppermute | solution.py:58
  100.8 14.7 %collective-permute-start.8 = (f32[272,256]{1,0:T(8,128)S(1)}, f32[272,256]{1,0:T(8,128)S(1)}, u32[]{:S(2)}, u32[]{:S(2)}) collective-permute-start(f32[272,256]{1,0:T(8,128)S(1)} %copy-done.6), channel_id=1, source_target_pairs={{0,80},{1,81},{2,82},{3,83},{4,84},{5,85},{6,86},{7,87},{8,88},{9,... | collective-permute-start | bytes 835592 | tf_op jit(solution)/shard_map/ppermute | solution.py:58
  108.0 13.3 %collective-permute-start.4 = (f32[272,256]{1,0:T(8,128)S(1)}, f32[272,256]{1,0:T(8,128)S(1)}, u32[]{:S(2)}, u32[]{:S(2)}) collective-permute-start(f32[272,256]{1,0:T(8,128)S(1)} %get-tuple-element.57), channel_id=1, source_target_pairs={{0,1},{1,0},{2,3},{3,2},{4,5},{5,4},{6,7},{7,6},{8,9},{9,8},{10,11... | collective-permute-start | bytes 835592 | tf_op jit(solution)/shard_map/ppermute | solution.py:58
  111.8 9.4 %collective-permute-start.5 = (f32[272,256]{1,0:T(8,128)S(1)}, f32[272,256]{1,0:T(8,128)S(1)}, u32[]{:S(2)}, u32[]{:S(2)}) collective-permute-start(f32[272,256]{1,0:T(8,128)S(1)} %get-tuple-element.58), channel_id=1, source_target_pairs={{0,15},{1,2},{2,1},{3,4},{4,3},{5,6},{6,5},{7,8},{8,7},{9,10},{10,... | collective-permute-start | bytes 835592 | tf_op jit(solution)/shard_map/ppermute | solution.py:58
  112.8 2.8 %copy-start.5 = (f32[272,256]{1,0:T(8,128)S(1)}, f32[272,256]{1,0:T(8,128)}, u32[]{:S(2)}) copy-start(f32[272,256]{1,0:T(8,128)} %get-tuple-element.73) | copy-start | bytes 835588
  112.8 6.2 %copy-start.4 = (f32[272,256]{1,0:T(8,128)S(1)}, f32[272,256]{1,0:T(8,128)}, u32[]{:S(2)}) copy-start(f32[272,256]{1,0:T(8,128)} %get-tuple-element.75) | copy-start | bytes 835588
  115.6 14.1 %collective-permute-start.11 = (f32[272,256]{1,0:T(8,128)S(1)}, f32[272,256]{1,0:T(8,128)S(1)}, u32[]{:S(2)}, u32[]{:S(2)}) collective-permute-start(f32[272,256]{1,0:T(8,128)S(1)} %copy-done.5), channel_id=1, source_target_pairs={{0,96},{1,97},{2,98},{3,99},{4,100},{5,101},{6,102},{7,103},{8,104... | collective-permute-start | bytes 835592 | tf_op jit(solution)/shard_map/ppermute | solution.py:58
  119.0 17.8 %collective-permute-start.12 = (f32[272,256]{1,0:T(8,128)S(1)}, f32[272,256]{1,0:T(8,128)S(1)}, u32[]{:S(2)}, u32[]{:S(2)}) collective-permute-start(f32[272,256]{1,0:T(8,128)S(1)} %copy-done.4), channel_id=1, source_target_pairs={{0,112},{1,113},{2,114},{3,115},{4,116},{5,117},{6,118},{7,119},{8... | collective-permute-start | bytes 835592 | tf_op jit(solution)/shard_map/ppermute | solution.py:58
  123.3 13.9 %collective-permute-start.9 = (f32[272,256]{1,0:T(8,128)S(1)}, f32[272,256]{1,0:T(8,128)S(1)}, u32[]{:S(2)}, u32[]{:S(2)}) collective-permute-start(f32[272,256]{1,0:T(8,128)S(1)} %get-tuple-element.70), channel_id=1, source_target_pairs={{0,1},{1,0},{2,3},{3,2},{4,5},{5,4},{6,7},{7,6},{8,9},{9,8},{10,11... | collective-permute-start | bytes 835592 | tf_op jit(solution)/shard_map/ppermute | solution.py:58
  124.3 13.0 %collective-permute-start.10 = (f32[272,256]{1,0:T(8,128)S(1)}, f32[272,256]{1,0:T(8,128)S(1)}, u32[]{:S(2)}, u32[]{:S(2)}) collective-permute-start(f32[272,256]{1,0:T(8,128)S(1)} %get-tuple-element.71), channel_id=1, source_target_pairs={{0,15},{1,2},{2,1},{3,4},{4,3},{5,6},{6,5},{7,8},{8,7},{9,10},{10,... | collective-permute-start | bytes 835592 | tf_op jit(solution)/shard_map/ppermute | solution.py:58
  126.9 9.9 %copy-start = (f32[272,256]{1,0:T(8,128)S(1)}, f32[272,256]{1,0:T(8,128)}, u32[]{:S(2)}) copy-start(f32[272,256]{1,0:T(8,128)} %get-tuple-element.51.refs_0_) | copy-start | bytes 835588
  139.0 3.6 %collective-permute-start.13 = (f32[272,256]{1,0:T(8,128)S(1)}, f32[272,256]{1,0:T(8,128)S(1)}, u32[]{:S(2)}, u32[]{:S(2)}) collective-permute-start(f32[272,256]{1,0:T(8,128)S(1)} %get-tuple-element.80), channel_id=1, source_target_pairs={{0,1},{1,0},{2,3},{3,2},{4,5},{5,4},{6,7},{7,6},{8,9},{9,8},{10,11... | collective-permute-start | bytes 835592 | tf_op jit(solution)/shard_map/ppermute | solution.py:58
  139.8 8.1 %collective-permute-start.14 = (f32[272,256]{1,0:T(8,128)S(1)}, f32[272,256]{1,0:T(8,128)S(1)}, u32[]{:S(2)}, u32[]{:S(2)}) collective-permute-start(f32[272,256]{1,0:T(8,128)S(1)} %get-tuple-element.81), channel_id=1, source_target_pairs={{0,15},{1,2},{2,1},{3,4},{4,3},{5,6},{6,5},{7,8},{8,7},{9,10},{10,... | collective-permute-start | bytes 835592 | tf_op jit(solution)/shard_map/ppermute | solution.py:58

commit v5 on v4

--- a/solution.py
+++ b/solution.py
@@ -287,7 +287,12 @@
                 edge = pltpu.roll(edge, turn, 1) if turn else edge
                 scaled = STEP * (rate_ref[level, rows, at] + jnp.where(near_edge, edge, 0.0))
                 value = u_ref[level, rows, at] + scaled
-                next_ref[level, rows, at] = value if below is None else value + below
+                value = value if below is None else value + below
+                if step < 3:
+                    next_ref[level, rows, at] = value
+                else:
+                    low, high = max(begin, HALO), min(begin + BAND, HALO + CHUNK)
+                    next_ref[level, low - HALO : high - HALO, at] = value[low - begin : high - begin]
                 below = W3 * scaled
                 if n_in > 0:
                     below = below + older[0][level, rows, at]
@@ -307,7 +312,8 @@
     n_in = len(older)
     full = pltpu.VMEM((LEVELS, WIDE, CELLS), f32)
     operands = [u, rate, inner, outer, weights[1]] + ([fields] if step < 3 else []) + older
-    outs = [full] + ([HALO_SHAPE] * 2 if step < 3 else []) + [full] * n_out
+    state = full if step < 3 else pltpu.VMEM((LEVELS, CHUNK, CELLS), f32)
+    outs = [state] + ([HALO_SHAPE] * 2 if step < 3 else []) + [full] * n_out
     outs = pl.pallas_call(
         functools.partial(step_kernel, step, n_in, n_out),
         out_shape=outs,
@@ -411,7 +417,7 @@
     return lax.optimization_barrier((value, *earlier))[0]
 
 
-WAVES = ((1, 3), (4, 2, 5), (6, 7))
+WAVES = ((4, 1, 3), (2, 5), (6, 7))
 
 
 def local(level_state, history, diffusion, linear_rates, coupling):
@@ -436,7 +442,7 @@
         if step == 2:
             fields = gather([got[by] for by in range(LEVELS)])
         u, inner, outer, older = one_step(step, u, rate, inner, outer, weights, fields, older, n_out)
-    return join(everyone(u[:, HALO : HALO + CHUNK, :]))[None]
+    return join(everyone(u))[None]
 
 
 def solution(mesh):

time: 185 us -> 185 us (level)
  no operation moved by 1% of the time
where the time goes in v5:
time: 185 us; the launch traced here: 181 us
  blocking collectives  112 us (61%)
  Pallas kernels  29.1 us (16%)
  starting transfers between devices  25 us (14%)
  waiting for transfers between devices  14.7 us (8%)
    all_to_all x2, blocking collectives, everyone(): return lax.all_to_all(value, 'level', 0, 0)  112 us
    ppermute x15, starting transfers between devices, send(): return lax.ppermute(value, ('level', 'tile'), pairs)  25 us
    ppermute x15, waiting for transfers between devices, send(): return lax.ppermute(value, ('level', 'tile'), pairs)  14.7 us
    pallas_call x4, Pallas kernels, inner_rates(): pl.pallas_call(inner_kernel, out_shape=pltpu.VMEM((LEVELS, WIDE, CELLS),...  10.7 us
    pallas_call x1, Pallas kernels, cut(): pl.pallas_call(cut_kernel, out_shape=[pltpu.VMEM((LEVELS, 3 * WIDE, CELLS...  8.14 us
    pallas_call x4, Pallas kernels, one_step(): pl.pallas_call(functools.partial(step_kernel, step, n_in, n_out), out_sha...  6.48 us
  transfers between devices with their start and end apart: 15, of which 4 were waited for; matrix products, arithmetic and copies ran while one was open for 0% of the time, Pallas kernels for 9%

profile of v5, /device:TPU:89, one launch (start us, length us, event | category | flops | bytes accessed | tf_op | source)
XLA Modules:
  0.0 181.2 jit_solution(4988924820117311653)
XLA Ops:
  0.0 8.1 %cut.1 = (f32[8,816,256]{2,1,0:T(8,128)S(1)}, f32[272,256]{1,0:T(8,128)}, f32[272,256]{1,0:T(8,128)}, f32[272,256]{1,0:T(8,128)}, f32[272,256]{1,0:T(8,128)}, /*...) custom-call(f32[256,2048]{1,0:T(8,128)} %bitcast.4, f32[3,256,2048]{2,1,0:T(8,128)} %bitcast.3), custom_call_target="tpu_custom_call" | custom-call | tf_op jit(solution)/shard_map/cut/pallas_call | solution.py:131
  8.1 80.9 %all_to_all.10.u_ref.fields_ref.refs_0_ = f32[8,816,256]{2,1,0:T(8,128)S(1)} all-to-all(f32[8,816,256]{2,1,0:T(8,128)S(1)} %get-tuple-element.44), channel_id=1, replica_groups=mesh['level'=8,'tile'=16] {'level'}, dimensions={0} | all-to-all | bytes 13369344 | tf_op jit(solution)/shard_map/all_to_all | solution.py:62
  89.1 0.5 edges.1
  90.0 2.7 %collective-permute-start.2 = (f32[272,256]{1,0:T(8,128)S(1)}, f32[272,256]{1,0:T(8,128)S(1)}, u32[]{:S(2)}, u32[]{:S(2)}) collective-permute-start(f32[272,256]{1,0:T(8,128)S(1)} %copy-done.10), channel_id=1, source_target_pairs={{0,64},{1,65},{2,66},{3,67},{4,68},{5,69},{6,70},{7,71},{8,72},{9,... | collective-permute-start | bytes 835592 | tf_op jit(solution)/shard_map/ppermute | solution.py:58
  92.7 0.9 collective-permute-start.3
  93.6 0.4 collective-permute-start.4
  94.0 3.1 %collective-permute-start = (f32[272,256]{1,0:T(8,128)S(1)}, f32[272,256]{1,0:T(8,128)S(1)}, u32[]{:S(2)}, u32[]{:S(2)}) collective-permute-start(f32[272,256]{1,0:T(8,128)S(1)} %get-tuple-element.47), channel_id=1, source_target_pairs={{0,1},{1,0},{2,3},{3,2},{4,5},{5,4},{6,7},{7,6},{8,9},{9,8},{10,11... | collective-permute-start | bytes 835592 | tf_op jit(solution)/shard_map/ppermute | solution.py:58
  97.1 0.9 collective-permute-start.1
  98.4 1.8 collective-permute-done.4.refs_3_
  100.2 0.6 collective-permute-start.7
  100.8 1.4 collective-permute-start.8
  102.3 1.0 weights.1
  103.2 2.7 %inner_0.1.rate_ref = f32[8,272,256]{2,1,0:T(8,128)S(1)} custom-call(f32[8,816,256]{2,1,0:T(8,128)S(1)} %all_to_all.10.u_ref.fields_ref.refs_0_, bf16[768,512]{1,0:T(8,128)(2,1)S(1)} %get-tuple-element.45.main_ref, f32[8,256]{1,0:T(8,128)S(1)} %get-tuple-element.46.diff_ref), custom_call_target="tpu_custom_call" | custom-call | tf_op jit(solution)/shard_map/inner_0/pallas_call | solution.py:246
  105.9 1.8 step_0.1
  107.7 3.8 %collective-permute-start.5 = (f32[272,256]{1,0:T(8,128)S(1)}, f32[272,256]{1,0:T(8,128)S(1)}, u32[]{:S(2)}, u32[]{:S(2)}) collective-permute-start(f32[272,256]{1,0:T(8,128)S(1)} %get-tuple-element.59), channel_id=1, source_target_pairs={{0,1},{1,0},{2,3},{3,2},{4,5},{5,4},{6,7},{7,6},{8,9},{9,8},{10,11... | collective-permute-start | bytes 835592 | tf_op jit(solution)/shard_map/ppermute | solution.py:58
  111.5 1.0 collective-permute-start.6
  112.5 2.7 %inner_1.1.rate_ref = f32[8,272,256]{2,1,0:T(8,128)S(1)} custom-call(f32[8,272,256]{2,1,0:T(8,128)S(1)} %get-tuple-element.58.u_ref, bf16[768,512]{1,0:T(8,128)(2,1)S(1)} %get-tuple-element.45.main_ref, f32[8,256]{1,0:T(8,128)S(1)} %get-tuple-element.46.diff_ref), custom_call_target="tpu_custom_call" | custom-call | tf_op jit(solution)/shard_map/inner_1/pallas_call | solution.py:246
  115.3 3.7 %collective-permute-start.11 = (f32[272,256]{1,0:T(8,128)S(1)}, f32[272,256]{1,0:T(8,128)S(1)}, u32[]{:S(2)}, u32[]{:S(2)}) collective-permute-start(f32[272,256]{1,0:T(8,128)S(1)} %copy-done.5), channel_id=1, source_target_pairs={{0,96},{1,97},{2,98},{3,99},{4,100},{5,101},{6,102},{7,103},{8,104... | collective-permute-start | bytes 835592 | tf_op jit(solution)/shard_map/ppermute | solution.py:58
  119.0 1.9 %collective-permute-start.12 = (f32[272,256]{1,0:T(8,128)S(1)}, f32[272,256]{1,0:T(8,128)S(1)}, u32[]{:S(2)}, u32[]{:S(2)}) collective-permute-start(f32[272,256]{1,0:T(8,128)S(1)} %copy-done.4), channel_id=1, source_target_pairs={{0,112},{1,113},{2,114},{3,115},{4,116},{5,117},{6,118},{7,119},{8... | collective-permute-start | bytes 835592 | tf_op jit(solution)/shard_map/ppermute | solution.py:58
  120.9 2.1 %step_1.1 = (f32[8,272,256]{2,1,0:T(8,128)S(1)}, f32[272,256]{1,0:T(8,128)S(1)}, f32[272,256]{1,0:T(8,128)S(1)}, f32[8,272,256]{2,1,0:T(8,128)S(1)}, f32[8,272,256]{2,1,0:T(8,128)S(1)}) custom-call(f32[8,272,256]{2,1,0:T(8,128)S(1)} %get-tuple-element.58.u_ref, f32[8,272,256]{2,1,0:T(8,128)S(1)} %inner_1.1.rate_ref, ...), custom_call_target="tpu_custom_call" | custom-call | tf_op jit(solution)/shard_map/step_1/pallas_call | solution.py:317
  123.0 0.9 collective-permute-start.9
  124.0 2.7 %collective-permute-start.10 = (f32[272,256]{1,0:T(8,128)S(1)}, f32[272,256]{1,0:T(8,128)S(1)}, u32[]{:S(2)}, u32[]{:S(2)}) collective-permute-start(f32[272,256]{1,0:T(8,128)S(1)} %get-tuple-element.71), channel_id=1, source_target_pairs={{0,15},{1,2},{2,1},{3,4},{4,3},{5,6},{6,5},{7,8},{8,7},{9,10},{10,... | collective-permute-start | bytes 835592 | tf_op jit(solution)/shard_map/ppermute | solution.py:58
  126.7 2.7 %inner_2.1.rate_ref = f32[8,272,256]{2,1,0:T(8,128)S(1)} custom-call(f32[8,272,256]{2,1,0:T(8,128)S(1)} %get-tuple-element.69.u_ref, bf16[768,512]{1,0:T(8,128)(2,1)S(1)} %get-tuple-element.45.main_ref, f32[8,256]{1,0:T(8,128)S(1)} %get-tuple-element.46.diff_ref), custom_call_target="tpu_custom_call" | custom-call | tf_op jit(solution)/shard_map/inner_2/pallas_call | solution.py:246
  129.3 7.2 %collective-permute-done.12.refs_7_ = f32[272,256]{1,0:T(8,128)S(1)} collective-permute-done((f32[272,256]{1,0:T(8,128)S(1)}, f32[272,256]{1,0:T(8,128)S(1)}, u32[]{:S(2)}, u32[]{:S(2)}) %collective-permute-start.12) | collective-permute-done | bytes 278560 | tf_op jit(solution)/shard_map/ppermute | solution.py:58
  136.5 0.4 gather.1.refs_0_
  136.9 1.7 step_2.1
  138.7 0.9 collective-permute-start.13
  139.6 2.7 %inner_3.1.rate_ref = f32[8,272,256]{2,1,0:T(8,128)S(1)} custom-call(f32[8,272,256]{2,1,0:T(8,128)S(1)} %get-tuple-element.79.u_ref, bf16[768,512]{1,0:T(8,128)(2,1)S(1)} %get-tuple-element.45.main_ref, f32[8,256]{1,0:T(8,128)S(1)} %get-tuple-element.46.diff_ref), custom_call_target="tpu_custom_call" | custom-call | tf_op jit(solution)/shard_map/inner_3/pallas_call | solution.py:246
  142.3 5.3 %collective-permute-done.14.outer_ref = f32[272,256]{1,0:T(8,128)S(1)} collective-permute-done((f32[272,256]{1,0:T(8,128)S(1)}, f32[272,256]{1,0:T(8,128)S(1)}, u32[]{:S(2)}, u32[]{:S(2)}) %collective-permute-start.14) | collective-permute-done | bytes 278560 | tf_op jit(solution)/shard_map/ppermute | solution.py:58
  147.6 0.9 step_3.1
  148.5 30.6 %all_to_all.11.parts = f32[8,256,256]{2,1,0:T(8,128)S(1)} all-to-all(f32[8,256,256]{2,1,0:T(8,128)S(1)} %step_3.1), channel_id=1, replica_groups=mesh['level'=8,'tile'=16] {'level'}, dimensions={0} | all-to-all | bytes 4194304 | tf_op jit(solution)/shard_map/all_to_all | solution.py:62
  179.2 1.9 %join.1 = f32[16,16,2048]{2,1,0:T(8,128)} custom-call(f32[8,256,256]{2,1,0:T(8,128)S(1)} %all_to_all.11.parts), custom_call_target="tpu_custom_call" | custom-call | tf_op jit(solution)/shard_map/join/pallas_call | solution.py:401
  (36 shorter events, 0.9 us)
Async XLA Ops:
  89.1 1.0 copy-start.10
  89.1 3.6 %copy-start.9 = (f32[272,256]{1,0:T(8,128)S(1)}, f32[272,256]{1,0:T(8,128)}, u32[]{:S(2)}) copy-start(f32[272,256]{1,0:T(8,128)} %get-tuple-element.55) | copy-start | bytes 835588
  89.1 4.5 %copy-start.8 = (f32[272,256]{1,0:T(8,128)S(1)}, f32[272,256]{1,0:T(8,128)}, u32[]{:S(2)}) copy-start(f32[272,256]{1,0:T(8,128)} %get-tuple-element.57) | copy-start | bytes 835588
  89.1 11.1 %copy-start.7 = (f32[272,256]{1,0:T(8,128)S(1)}, f32[272,256]{1,0:T(8,128)}, u32[]{:S(2)}) copy-start(f32[272,256]{1,0:T(8,128)} %get-tuple-element.66) | copy-start | bytes 835588
  89.1 11.7 %copy-start.6 = (f32[272,256]{1,0:T(8,128)S(1)}, f32[272,256]{1,0:T(8,128)}, u32[]{:S(2)}) copy-start(f32[272,256]{1,0:T(8,128)} %get-tuple-element.68) | copy-start | bytes 835588
  89.1 13.2 %copy-start.3 = (f32[16]{0:T(128)S(1)}, f32[16]{0:T(128)}, u32[]{:S(2)}) copy-start(f32[16]{0:T(128)} %param.7) | copy-start | bytes 196
  89.1 13.2 %copy-start.1 = (f32[16,16]{1,0:T(8,128)S(1)}, f32[16,16]{1,0:T(8,128)}, u32[]{:S(2)}) copy-start(f32[16,16]{1,0:T(8,128)} %lin_ref.1) | copy-start | bytes 3076
  89.1 13.2 %copy-start.2 = (f32[16,16]{1,0:T(8,128)S(1)}, f32[16,16]{1,0:T(8,128)}, u32[]{:S(2)}) copy-start(f32[16,16]{1,0:T(8,128)} %coup_ref.1) | copy-start | bytes 3076
  90.0 8.0 %collective-permute-start.2 = (f32[272,256]{1,0:T(8,128)S(1)}, f32[272,256]{1,0:T(8,128)S(1)}, u32[]{:S(2)}, u32[]{:S(2)}) collective-permute-start(f32[272,256]{1,0:T(8,128)S(1)} %copy-done.10), channel_id=1, source_target_pairs={{0,64},{1,65},{2,66},{3,67},{4,68},{5,69},{6,70},{7,71},{8,72},{9,... | collective-permute-start | bytes 835592 | tf_op jit(solution)/shard_map/ppermute | solution.py:58
  92.7 5.7 %collective-permute-start.3 = (f32[272,256]{1,0:T(8,128)S(1)}, f32[272,256]{1,0:T(8,128)S(1)}, u32[]{:S(2)}, u32[]{:S(2)}) collective-permute-start(f32[272,256]{1,0:T(8,128)S(1)} %copy-done.9), channel_id=1, source_target_pairs={{0,16},{1,17},{2,18},{3,19},{4,20},{5,21},{6,22},{7,23},{8,24},{9,... | collective-permute-start | bytes 835592 | tf_op jit(solution)/shard_map/ppermute | solution.py:58
  93.6 6.6 %collective-permute-start.4 = (f32[272,256]{1,0:T(8,128)S(1)}, f32[272,256]{1,0:T(8,128)S(1)}, u32[]{:S(2)}, u32[]{:S(2)}) collective-permute-start(f32[272,256]{1,0:T(8,128)S(1)} %copy-done.8), channel_id=1, source_target_pairs={{0,48},{1,49},{2,50},{3,51},{4,52},{5,53},{6,54},{7,55},{8,56},{9,... | collective-permute-start | bytes 835592 | tf_op jit(solution)/shard_map/ppermute | solution.py:58
  94.0 11.9 %collective-permute-start = (f32[272,256]{1,0:T(8,128)S(1)}, f32[272,256]{1,0:T(8,128)S(1)}, u32[]{:S(2)}, u32[]{:S(2)}) collective-permute-start(f32[272,256]{1,0:T(8,128)S(1)} %get-tuple-element.47), channel_id=1, source_target_pairs={{0,1},{1,0},{2,3},{3,2},{4,5},{5,4},{6,7},{7,6},{8,9},{9,8},{10,11... | collective-permute-start | bytes 835592 | tf_op jit(solution)/shard_map/ppermute | solution.py:58
  97.1 8.8 %collective-permute-start.1 = (f32[272,256]{1,0:T(8,128)S(1)}, f32[272,256]{1,0:T(8,128)S(1)}, u32[]{:S(2)}, u32[]{:S(2)}) collective-permute-start(f32[272,256]{1,0:T(8,128)S(1)} %get-tuple-element.48), channel_id=1, source_target_pairs={{0,15},{1,2},{2,1},{3,4},{4,3},{5,6},{6,5},{7,8},{8,7},{9,10},{10,... | collective-permute-start | bytes 835592 | tf_op jit(solution)/shard_map/ppermute | solution.py:58
  100.2 15.1 %collective-permute-start.7 = (f32[272,256]{1,0:T(8,128)S(1)}, f32[272,256]{1,0:T(8,128)S(1)}, u32[]{:S(2)}, u32[]{:S(2)}) collective-permute-start(f32[272,256]{1,0:T(8,128)S(1)} %copy-done.7), channel_id=1, source_target_pairs={{0,32},{1,33},{2,34},{3,35},{4,36},{5,37},{6,38},{7,39},{8,40},{9,... | collective-permute-start | bytes 835592 | tf_op jit(solution)/shard_map/ppermute | solution.py:58
  100.8 14.5 %collective-permute-start.8 = (f32[272,256]{1,0:T(8,128)S(1)}, f32[272,256]{1,0:T(8,128)S(1)}, u32[]{:S(2)}, u32[]{:S(2)}) collective-permute-start(f32[272,256]{1,0:T(8,128)S(1)} %copy-done.6), channel_id=1, source_target_pairs={{0,80},{1,81},{2,82},{3,83},{4,84},{5,85},{6,86},{7,87},{8,88},{9,... | collective-permute-start | bytes 835592 | tf_op jit(solution)/shard_map/ppermute | solution.py:58
  107.7 13.3 %collective-permute-start.5 = (f32[272,256]{1,0:T(8,128)S(1)}, f32[272,256]{1,0:T(8,128)S(1)}, u32[]{:S(2)}, u32[]{:S(2)}) collective-permute-start(f32[272,256]{1,0:T(8,128)S(1)} %get-tuple-element.59), channel_id=1, source_target_pairs={{0,1},{1,0},{2,3},{3,2},{4,5},{5,4},{6,7},{7,6},{8,9},{9,8},{10,11... | collective-permute-start | bytes 835592 | tf_op jit(solution)/shard_map/ppermute | solution.py:58
  111.5 9.4 %collective-permute-start.6 = (f32[272,256]{1,0:T(8,128)S(1)}, f32[272,256]{1,0:T(8,128)S(1)}, u32[]{:S(2)}, u32[]{:S(2)}) collective-permute-start(f32[272,256]{1,0:T(8,128)S(1)} %get-tuple-element.60), channel_id=1, source_target_pairs={{0,15},{1,2},{2,1},{3,4},{4,3},{5,6},{6,5},{7,8},{8,7},{9,10},{10,... | collective-permute-start | bytes 835592 | tf_op jit(solution)/shard_map/ppermute | solution.py:58
  112.5 2.8 %copy-start.5 = (f32[272,256]{1,0:T(8,128)S(1)}, f32[272,256]{1,0:T(8,128)}, u32[]{:S(2)}) copy-start(f32[272,256]{1,0:T(8,128)} %get-tuple-element.73) | copy-start | bytes 835588
  112.5 6.5 %copy-start.4 = (f32[272,256]{1,0:T(8,128)S(1)}, f32[272,256]{1,0:T(8,128)}, u32[]{:S(2)}) copy-start(f32[272,256]{1,0:T(8,128)} %get-tuple-element.75) | copy-start | bytes 835588
  115.3 14.0 %collective-permute-start.11 = (f32[272,256]{1,0:T(8,128)S(1)}, f32[272,256]{1,0:T(8,128)S(1)}, u32[]{:S(2)}, u32[]{:S(2)}) collective-permute-start(f32[272,256]{1,0:T(8,128)S(1)} %copy-done.5), channel_id=1, source_target_pairs={{0,96},{1,97},{2,98},{3,99},{4,100},{5,101},{6,102},{7,103},{8,104... | collective-permute-start | bytes 835592 | tf_op jit(solution)/shard_map/ppermute | solution.py:58
  119.0 17.5 %collective-permute-start.12 = (f32[272,256]{1,0:T(8,128)S(1)}, f32[272,256]{1,0:T(8,128)S(1)}, u32[]{:S(2)}, u32[]{:S(2)}) collective-permute-start(f32[272,256]{1,0:T(8,128)S(1)} %copy-done.4), channel_id=1, source_target_pairs={{0,112},{1,113},{2,114},{3,115},{4,116},{5,117},{6,118},{7,119},{8... | collective-permute-start | bytes 835592 | tf_op jit(solution)/shard_map/ppermute | solution.py:58
  123.0 13.9 %collective-permute-start.9 = (f32[272,256]{1,0:T(8,128)S(1)}, f32[272,256]{1,0:T(8,128)S(1)}, u32[]{:S(2)}, u32[]{:S(2)}) collective-permute-start(f32[272,256]{1,0:T(8,128)S(1)} %get-tuple-element.70), channel_id=1, source_target_pairs={{0,1},{1,0},{2,3},{3,2},{4,5},{5,4},{6,7},{7,6},{8,9},{9,8},{10,11... | collective-permute-start | bytes 835592 | tf_op jit(solution)/shard_map/ppermute | solution.py:58
  124.0 13.0 %collective-permute-start.10 = (f32[272,256]{1,0:T(8,128)S(1)}, f32[272,256]{1,0:T(8,128)S(1)}, u32[]{:S(2)}, u32[]{:S(2)}) collective-permute-start(f32[272,256]{1,0:T(8,128)S(1)} %get-tuple-element.71), channel_id=1, source_target_pairs={{0,15},{1,2},{2,1},{3,4},{4,3},{5,6},{6,5},{7,8},{8,7},{9,10},{10,... | collective-permute-start | bytes 835592 | tf_op jit(solution)/shard_map/ppermute | solution.py:58
  126.7 9.9 %copy-start = (f32[272,256]{1,0:T(8,128)S(1)}, f32[272,256]{1,0:T(8,128)}, u32[]{:S(2)}) copy-start(f32[272,256]{1,0:T(8,128)} %get-tuple-element.51.refs_0_) | copy-start | bytes 835588
  138.7 3.6 %collective-permute-start.13 = (f32[272,256]{1,0:T(8,128)S(1)}, f32[272,256]{1,0:T(8,128)S(1)}, u32[]{:S(2)}, u32[]{:S(2)}) collective-permute-start(f32[272,256]{1,0:T(8,128)S(1)} %get-tuple-element.80), channel_id=1, source_target_pairs={{0,1},{1,0},{2,3},{3,2},{4,5},{5,4},{6,7},{7,6},{8,9},{9,8},{10,11... | collective-permute-start | bytes 835592 | tf_op jit(solution)/shard_map/ppermute | solution.py:58
  139.6 8.1 %collective-permute-start.14 = (f32[272,256]{1,0:T(8,128)S(1)}, f32[272,256]{1,0:T(8,128)S(1)}, u32[]{:S(2)}, u32[]{:S(2)}) collective-permute-start(f32[272,256]{1,0:T(8,128)S(1)} %get-tuple-element.81), channel_id=1, source_target_pairs={{0,15},{1,2},{2,1},{3,4},{4,3},{5,6},{6,5},{7,8},{8,7},{9,10},{10,... | collective-permute-start | bytes 835592 | tf_op jit(solution)/shard_map/ppermute | solution.py:58

commit v6 on v5

--- a/solution.py
+++ b/solution.py
@@ -417,7 +417,7 @@
     return lax.optimization_barrier((value, *earlier))[0]
 
 
-WAVES = ((4, 1, 3), (2, 5), (6, 7))
+WAVES = ((4, 1, 3), (6, 5), (2, 7))
 
 
 def local(level_state, history, diffusion, linear_rates, coupling):

time: 185 us -> 185 us (level)
  transfers between devices with their start and end apart: 15 -> 15, of which waited for: 4 -> 5; matrix products, arithmetic and copies ran while one was open for 0% -> 0% of each run, Pallas kernels for 9% -> 9%
where the time goes in v6:
time: 185 us; the launch traced here: 181 us
  blocking collectives  111 us (60%)
  Pallas kernels  29.1 us (16%)
  starting transfers between devices  24.3 us (13%)
  waiting for transfers between devices  16.1 us (9%)
    all_to_all x2, blocking collectives, everyone(): return lax.all_to_all(value, 'level', 0, 0)  111 us
    ppermute x15, starting transfers between devices, send(): return lax.ppermute(value, ('level', 'tile'), pairs)  24.3 us
    ppermute x15, waiting for transfers between devices, send(): return lax.ppermute(value, ('level', 'tile'), pairs)  16.1 us
    pallas_call x4, Pallas kernels, inner_rates(): pl.pallas_call(inner_kernel, out_shape=pltpu.VMEM((LEVELS, WIDE, CELLS),...  10.7 us
    pallas_call x1, Pallas kernels, cut(): pl.pallas_call(cut_kernel, out_shape=[pltpu.VMEM((LEVELS, 3 * WIDE, CELLS...  8.14 us
    pallas_call x4, Pallas kernels, one_step(): pl.pallas_call(functools.partial(step_kernel, step, n_in, n_out), out_sha...  6.47 us
  transfers between devices with their start and end apart: 15, of which 5 were waited for; matrix products, arithmetic and copies ran while one was open for 0% of the time, Pallas kernels for 9%

profile of v6, /device:TPU:89, one launch (start us, length us, event | category | flops | bytes accessed | tf_op | source)
XLA Modules:
  0.0 181.1 jit_solution(16187697822799720285)
XLA Ops:
  0.0 8.1 %cut.1 = (f32[8,816,256]{2,1,0:T(8,128)S(1)}, f32[272,256]{1,0:T(8,128)}, f32[272,256]{1,0:T(8,128)}, f32[272,256]{1,0:T(8,128)}, f32[272,256]{1,0:T(8,128)}, /*...) custom-call(f32[256,2048]{1,0:T(8,128)} %bitcast.4, f32[3,256,2048]{2,1,0:T(8,128)} %bitcast.3), custom_call_target="tpu_custom_call" | custom-call | tf_op jit(solution)/shard_map/cut/pallas_call | solution.py:131
  8.1 80.9 %all_to_all.10.u_ref.fields_ref.refs_0_ = f32[8,816,256]{2,1,0:T(8,128)S(1)} all-to-all(f32[8,816,256]{2,1,0:T(8,128)S(1)} %get-tuple-element.44), channel_id=1, replica_groups=mesh['level'=8,'tile'=16] {'level'}, dimensions={0} | all-to-all | bytes 13369344 | tf_op jit(solution)/shard_map/all_to_all | solution.py:62
  89.1 0.5 edges.1
  90.0 2.7 %collective-permute-start.2 = (f32[272,256]{1,0:T(8,128)S(1)}, f32[272,256]{1,0:T(8,128)S(1)}, u32[]{:S(2)}, u32[]{:S(2)}) collective-permute-start(f32[272,256]{1,0:T(8,128)S(1)} %copy-done.10), channel_id=1, source_target_pairs={{0,64},{1,65},{2,66},{3,67},{4,68},{5,69},{6,70},{7,71},{8,72},{9,... | collective-permute-start | bytes 835592 | tf_op jit(solution)/shard_map/ppermute | solution.py:58
  92.7 0.9 collective-permute-start.3
  93.6 0.4 collective-permute-start.4
  94.0 3.1 %collective-permute-start = (f32[272,256]{1,0:T(8,128)S(1)}, f32[272,256]{1,0:T(8,128)S(1)}, u32[]{:S(2)}, u32[]{:S(2)}) collective-permute-start(f32[272,256]{1,0:T(8,128)S(1)} %get-tuple-element.47), channel_id=1, source_target_pairs={{0,1},{1,0},{2,3},{3,2},{4,5},{5,4},{6,7},{7,6},{8,9},{9,8},{10,11... | collective-permute-start | bytes 835592 | tf_op jit(solution)/shard_map/ppermute | solution.py:58
  97.1 0.9 collective-permute-start.1
  98.4 1.8 collective-permute-done.4.refs_3_
  100.2 1.2 collective-permute-start.7
  101.4 2.4 %collective-permute-start.8 = (f32[272,256]{1,0:T(8,128)S(1)}, f32[272,256]{1,0:T(8,128)S(1)}, u32[]{:S(2)}, u32[]{:S(2)}) collective-permute-start(f32[272,256]{1,0:T(8,128)S(1)} %copy-done.6), channel_id=1, source_target_pairs={{0,80},{1,81},{2,82},{3,83},{4,84},{5,85},{6,86},{7,87},{8,88},{9,... | collective-permute-start | bytes 835592 | tf_op jit(solution)/shard_map/ppermute | solution.py:58
  103.8 1.0 weights.1
  104.7 2.7 %inner_0.1.rate_ref = f32[8,272,256]{2,1,0:T(8,128)S(1)} custom-call(f32[8,816,256]{2,1,0:T(8,128)S(1)} %all_to_all.10.u_ref.fields_ref.refs_0_, bf16[768,512]{1,0:T(8,128)(2,1)S(1)} %get-tuple-element.45.main_ref, f32[8,256]{1,0:T(8,128)S(1)} %get-tuple-element.46.diff_ref), custom_call_target="tpu_custom_call" | custom-call | tf_op jit(solution)/shard_map/inner_0/pallas_call | solution.py:246
  107.4 1.8 step_0.1
  109.2 4.5 %collective-permute-start.5 = (f32[272,256]{1,0:T(8,128)S(1)}, f32[272,256]{1,0:T(8,128)S(1)}, u32[]{:S(2)}, u32[]{:S(2)}) collective-permute-start(f32[272,256]{1,0:T(8,128)S(1)} %get-tuple-element.59), channel_id=1, source_target_pairs={{0,1},{1,0},{2,3},{3,2},{4,5},{5,4},{6,7},{7,6},{8,9},{9,8},{10,11... | collective-permute-start | bytes 835592 | tf_op jit(solution)/shard_map/ppermute | solution.py:58
  113.7 1.0 collective-permute-start.6
  114.7 2.7 %inner_1.1.rate_ref = f32[8,272,256]{2,1,0:T(8,128)S(1)} custom-call(f32[8,272,256]{2,1,0:T(8,128)S(1)} %get-tuple-element.58.u_ref, bf16[768,512]{1,0:T(8,128)(2,1)S(1)} %get-tuple-element.45.main_ref, f32[8,256]{1,0:T(8,128)S(1)} %get-tuple-element.46.diff_ref), custom_call_target="tpu_custom_call" | custom-call | tf_op jit(solution)/shard_map/inner_1/pallas_call | solution.py:246
  117.4 2.2 %collective-permute-start.11 = (f32[272,256]{1,0:T(8,128)S(1)}, f32[272,256]{1,0:T(8,128)S(1)}, u32[]{:S(2)}, u32[]{:S(2)}) collective-permute-start(f32[272,256]{1,0:T(8,128)S(1)} %copy-done.5), channel_id=1, source_target_pairs={{0,32},{1,33},{2,34},{3,35},{4,36},{5,37},{6,38},{7,39},{8,40},{9,... | collective-permute-start | bytes 835592 | tf_op jit(solution)/shard_map/ppermute | solution.py:58
  119.6 0.7 collective-permute-start.12
  120.3 1.4 collective-permute-done.6.outer_ref
  121.8 2.1 %step_1.1 = (f32[8,272,256]{2,1,0:T(8,128)S(1)}, f32[272,256]{1,0:T(8,128)S(1)}, f32[272,256]{1,0:T(8,128)S(1)}, f32[8,272,256]{2,1,0:T(8,128)S(1)}, f32[8,272,256]{2,1,0:T(8,128)S(1)}) custom-call(f32[8,272,256]{2,1,0:T(8,128)S(1)} %get-tuple-element.58.u_ref, f32[8,272,256]{2,1,0:T(8,128)S(1)} %inner_1.1.rate_ref, ...), custom_call_target="tpu_custom_call" | custom-call | tf_op jit(solution)/shard_map/step_1/pallas_call | solution.py:317
  123.9 2.4 %collective-permute-start.9 = (f32[272,256]{1,0:T(8,128)S(1)}, f32[272,256]{1,0:T(8,128)S(1)}, u32[]{:S(2)}, u32[]{:S(2)}) collective-permute-start(f32[272,256]{1,0:T(8,128)S(1)} %get-tuple-element.70), channel_id=1, source_target_pairs={{0,1},{1,0},{2,3},{3,2},{4,5},{5,4},{6,7},{7,6},{8,9},{9,8},{10,11... | collective-permute-start | bytes 835592 | tf_op jit(solution)/shard_map/ppermute | solution.py:58
  126.3 1.0 collective-permute-start.10
  127.3 2.7 %inner_2.1.rate_ref = f32[8,272,256]{2,1,0:T(8,128)S(1)} custom-call(f32[8,272,256]{2,1,0:T(8,128)S(1)} %get-tuple-element.69.u_ref, bf16[768,512]{1,0:T(8,128)(2,1)S(1)} %get-tuple-element.45.main_ref, f32[8,256]{1,0:T(8,128)S(1)} %get-tuple-element.46.diff_ref), custom_call_target="tpu_custom_call" | custom-call | tf_op jit(solution)/shard_map/inner_2/pallas_call | solution.py:246
  129.9 7.1 %collective-permute-done.12.refs_7_ = f32[272,256]{1,0:T(8,128)S(1)} collective-permute-done((f32[272,256]{1,0:T(8,128)S(1)}, f32[272,256]{1,0:T(8,128)S(1)}, u32[]{:S(2)}, u32[]{:S(2)}) %collective-permute-start.12) | collective-permute-done | bytes 278560 | tf_op jit(solution)/shard_map/ppermute | solution.py:58
  137.4 1.7 step_2.1
  139.2 1.0 collective-permute-start.13
  140.1 2.7 %inner_3.1.rate_ref = f32[8,272,256]{2,1,0:T(8,128)S(1)} custom-call(f32[8,272,256]{2,1,0:T(8,128)S(1)} %get-tuple-element.79.u_ref, bf16[768,512]{1,0:T(8,128)(2,1)S(1)} %get-tuple-element.45.main_ref, f32[8,256]{1,0:T(8,128)S(1)} %get-tuple-element.46.diff_ref), custom_call_target="tpu_custom_call" | custom-call | tf_op jit(solution)/shard_map/inner_3/pallas_call | solution.py:246
  142.8 5.4 %collective-permute-done.14.outer_ref = f32[272,256]{1,0:T(8,128)S(1)} collective-permute-done((f32[272,256]{1,0:T(8,128)S(1)}, f32[272,256]{1,0:T(8,128)S(1)}, u32[]{:S(2)}, u32[]{:S(2)}) %collective-permute-start.14) | collective-permute-done | bytes 278560 | tf_op jit(solution)/shard_map/ppermute | solution.py:58
  148.2 0.9 step_3.1
  149.1 29.9 %all_to_all.11.parts = f32[8,256,256]{2,1,0:T(8,128)S(1)} all-to-all(f32[8,256,256]{2,1,0:T(8,128)S(1)} %step_3.1), channel_id=1, replica_groups=mesh['level'=8,'tile'=16] {'level'}, dimensions={0} | all-to-all | bytes 4194304 | tf_op jit(solution)/shard_map/all_to_all | solution.py:62
  179.1 1.9 %join.1 = f32[16,16,2048]{2,1,0:T(8,128)} custom-call(f32[8,256,256]{2,1,0:T(8,128)S(1)} %all_to_all.11.parts), custom_call_target="tpu_custom_call" | custom-call | tf_op jit(solution)/shard_map/join/pallas_call | solution.py:401
  (36 shorter events, 1.2 us)
Async XLA Ops:
  89.1 1.0 copy-start.10
  89.1 3.6 %copy-start.9 = (f32[272,256]{1,0:T(8,128)S(1)}, f32[272,256]{1,0:T(8,128)}, u32[]{:S(2)}) copy-start(f32[272,256]{1,0:T(8,128)} %get-tuple-element.55) | copy-start | bytes 835588
  89.1 4.5 %copy-start.8 = (f32[272,256]{1,0:T(8,128)S(1)}, f32[272,256]{1,0:T(8,128)}, u32[]{:S(2)}) copy-start(f32[272,256]{1,0:T(8,128)} %get-tuple-element.57) | copy-start | bytes 835588
  89.1 11.1 %copy-start.7 = (f32[272,256]{1,0:T(8,128)S(1)}, f32[272,256]{1,0:T(8,128)}, u32[]{:S(2)}) copy-start(f32[272,256]{1,0:T(8,128)} %get-tuple-element.66) | copy-start | bytes 835588
  89.1 12.3 %copy-start.6 = (f32[272,256]{1,0:T(8,128)S(1)}, f32[272,256]{1,0:T(8,128)}, u32[]{:S(2)}) copy-start(f32[272,256]{1,0:T(8,128)} %get-tuple-element.68) | copy-start | bytes 835588
  89.1 14.7 %copy-start.3 = (f32[16]{0:T(128)S(1)}, f32[16]{0:T(128)}, u32[]{:S(2)}) copy-start(f32[16]{0:T(128)} %param.7) | copy-start | bytes 196
  89.1 14.7 %copy-start.1 = (f32[16,16]{1,0:T(8,128)S(1)}, f32[16,16]{1,0:T(8,128)}, u32[]{:S(2)}) copy-start(f32[16,16]{1,0:T(8,128)} %lin_ref.1) | copy-start | bytes 3076
  89.1 14.7 %copy-start.2 = (f32[16,16]{1,0:T(8,128)S(1)}, f32[16,16]{1,0:T(8,128)}, u32[]{:S(2)}) copy-start(f32[16,16]{1,0:T(8,128)} %coup_ref.1) | copy-start | bytes 3076
  90.0 8.0 %collective-permute-start.2 = (f32[272,256]{1,0:T(8,128)S(1)}, f32[272,256]{1,0:T(8,128)S(1)}, u32[]{:S(2)}, u32[]{:S(2)}) collective-permute-start(f32[272,256]{1,0:T(8,128)S(1)} %copy-done.10), channel_id=1, source_target_pairs={{0,64},{1,65},{2,66},{3,67},{4,68},{5,69},{6,70},{7,71},{8,72},{9,... | collective-permute-start | bytes 835592 | tf_op jit(solution)/shard_map/ppermute | solution.py:58
  92.7 5.7 %collective-permute-start.3 = (f32[272,256]{1,0:T(8,128)S(1)}, f32[272,256]{1,0:T(8,128)S(1)}, u32[]{:S(2)}, u32[]{:S(2)}) collective-permute-start(f32[272,256]{1,0:T(8,128)S(1)} %copy-done.9), channel_id=1, source_target_pairs={{0,16},{1,17},{2,18},{3,19},{4,20},{5,21},{6,22},{7,23},{8,24},{9,... | collective-permute-start | bytes 835592 | tf_op jit(solution)/shard_map/ppermute | solution.py:58
  93.6 6.6 %collective-permute-start.4 = (f32[272,256]{1,0:T(8,128)S(1)}, f32[272,256]{1,0:T(8,128)S(1)}, u32[]{:S(2)}, u32[]{:S(2)}) collective-permute-start(f32[272,256]{1,0:T(8,128)S(1)} %copy-done.8), channel_id=1, source_target_pairs={{0,48},{1,49},{2,50},{3,51},{4,52},{5,53},{6,54},{7,55},{8,56},{9,... | collective-permute-start | bytes 835592 | tf_op jit(solution)/shard_map/ppermute | solution.py:58
  94.0 13.4 %collective-permute-start = (f32[272,256]{1,0:T(8,128)S(1)}, f32[272,256]{1,0:T(8,128)S(1)}, u32[]{:S(2)}, u32[]{:S(2)}) collective-permute-start(f32[272,256]{1,0:T(8,128)S(1)} %get-tuple-element.47), channel_id=1, source_target_pairs={{0,1},{1,0},{2,3},{3,2},{4,5},{5,4},{6,7},{7,6},{8,9},{9,8},{10,11... | collective-permute-start | bytes 835592 | tf_op jit(solution)/shard_map/ppermute | solution.py:58
  97.1 10.3 %collective-permute-start.1 = (f32[272,256]{1,0:T(8,128)S(1)}, f32[272,256]{1,0:T(8,128)S(1)}, u32[]{:S(2)}, u32[]{:S(2)}) collective-permute-start(f32[272,256]{1,0:T(8,128)S(1)} %get-tuple-element.48), channel_id=1, source_target_pairs={{0,15},{1,2},{2,1},{3,4},{4,3},{5,6},{6,5},{7,8},{8,7},{9,10},{10,... | collective-permute-start | bytes 835592 | tf_op jit(solution)/shard_map/ppermute | solution.py:58
  100.2 17.2 %collective-permute-start.7 = (f32[272,256]{1,0:T(8,128)S(1)}, f32[272,256]{1,0:T(8,128)S(1)}, u32[]{:S(2)}, u32[]{:S(2)}) collective-permute-start(f32[272,256]{1,0:T(8,128)S(1)} %copy-done.7), channel_id=1, source_target_pairs={{0,96},{1,97},{2,98},{3,99},{4,100},{5,101},{6,102},{7,103},{8,104... | collective-permute-start | bytes 835592 | tf_op jit(solution)/shard_map/ppermute | solution.py:58
  101.4 16.0 %collective-permute-start.8 = (f32[272,256]{1,0:T(8,128)S(1)}, f32[272,256]{1,0:T(8,128)S(1)}, u32[]{:S(2)}, u32[]{:S(2)}) collective-permute-start(f32[272,256]{1,0:T(8,128)S(1)} %copy-done.6), channel_id=1, source_target_pairs={{0,80},{1,81},{2,82},{3,83},{4,84},{5,85},{6,86},{7,87},{8,88},{9,... | collective-permute-start | bytes 835592 | tf_op jit(solution)/shard_map/ppermute | solution.py:58
  109.2 11.1 %collective-permute-start.5 = (f32[272,256]{1,0:T(8,128)S(1)}, f32[272,256]{1,0:T(8,128)S(1)}, u32[]{:S(2)}, u32[]{:S(2)}) collective-permute-start(f32[272,256]{1,0:T(8,128)S(1)} %get-tuple-element.59), channel_id=1, source_target_pairs={{0,1},{1,0},{2,3},{3,2},{4,5},{5,4},{6,7},{7,6},{8,9},{9,8},{10,11... | collective-permute-start | bytes 835592 | tf_op jit(solution)/shard_map/ppermute | solution.py:58
  113.7 8.1 %collective-permute-start.6 = (f32[272,256]{1,0:T(8,128)S(1)}, f32[272,256]{1,0:T(8,128)S(1)}, u32[]{:S(2)}, u32[]{:S(2)}) collective-permute-start(f32[272,256]{1,0:T(8,128)S(1)} %get-tuple-element.60), channel_id=1, source_target_pairs={{0,15},{1,2},{2,1},{3,4},{4,3},{5,6},{6,5},{7,8},{8,7},{9,10},{10,... | collective-permute-start | bytes 835592 | tf_op jit(solution)/shard_map/ppermute | solution.py:58
  114.7 2.8 %copy-start.5 = (f32[272,256]{1,0:T(8,128)S(1)}, f32[272,256]{1,0:T(8,128)}, u32[]{:S(2)}) copy-start(f32[272,256]{1,0:T(8,128)} %get-tuple-element.73) | copy-start | bytes 835588
  114.7 4.9 %copy-start.4 = (f32[272,256]{1,0:T(8,128)S(1)}, f32[272,256]{1,0:T(8,128)}, u32[]{:S(2)}) copy-start(f32[272,256]{1,0:T(8,128)} %get-tuple-element.75) | copy-start | bytes 835588
  117.4 12.5 %collective-permute-start.11 = (f32[272,256]{1,0:T(8,128)S(1)}, f32[272,256]{1,0:T(8,128)S(1)}, u32[]{:S(2)}, u32[]{:S(2)}) collective-permute-start(f32[272,256]{1,0:T(8,128)S(1)} %copy-done.5), channel_id=1, source_target_pairs={{0,32},{1,33},{2,34},{3,35},{4,36},{5,37},{6,38},{7,39},{8,40},{9,... | collective-permute-start | bytes 835592 | tf_op jit(solution)/shard_map/ppermute | solution.py:58
  119.6 17.4 %collective-permute-start.12 = (f32[272,256]{1,0:T(8,128)S(1)}, f32[272,256]{1,0:T(8,128)S(1)}, u32[]{:S(2)}, u32[]{:S(2)}) collective-permute-start(f32[272,256]{1,0:T(8,128)S(1)} %copy-done.4), channel_id=1, source_target_pairs={{0,112},{1,113},{2,114},{3,115},{4,116},{5,117},{6,118},{7,119},{8... | collective-permute-start | bytes 835592 | tf_op jit(solution)/shard_map/ppermute | solution.py:58
  123.9 13.6 %collective-permute-start.9 = (f32[272,256]{1,0:T(8,128)S(1)}, f32[272,256]{1,0:T(8,128)S(1)}, u32[]{:S(2)}, u32[]{:S(2)}) collective-permute-start(f32[272,256]{1,0:T(8,128)S(1)} %get-tuple-element.70), channel_id=1, source_target_pairs={{0,1},{1,0},{2,3},{3,2},{4,5},{5,4},{6,7},{7,6},{8,9},{9,8},{10,11... | collective-permute-start | bytes 835592 | tf_op jit(solution)/shard_map/ppermute | solution.py:58
  126.3 11.1 %collective-permute-start.10 = (f32[272,256]{1,0:T(8,128)S(1)}, f32[272,256]{1,0:T(8,128)S(1)}, u32[]{:S(2)}, u32[]{:S(2)}) collective-permute-start(f32[272,256]{1,0:T(8,128)S(1)} %get-tuple-element.71), channel_id=1, source_target_pairs={{0,15},{1,2},{2,1},{3,4},{4,3},{5,6},{6,5},{7,8},{8,7},{9,10},{10,... | collective-permute-start | bytes 835592 | tf_op jit(solution)/shard_map/ppermute | solution.py:58
  127.3 9.8 %copy-start = (f32[272,256]{1,0:T(8,128)S(1)}, f32[272,256]{1,0:T(8,128)}, u32[]{:S(2)}) copy-start(f32[272,256]{1,0:T(8,128)} %get-tuple-element.51.refs_0_) | copy-start | bytes 835588
  139.2 3.6 %collective-permute-start.13 = (f32[272,256]{1,0:T(8,128)S(1)}, f32[272,256]{1,0:T(8,128)S(1)}, u32[]{:S(2)}, u32[]{:S(2)}) collective-permute-start(f32[272,256]{1,0:T(8,128)S(1)} %get-tuple-element.80), channel_id=1, source_target_pairs={{0,1},{1,0},{2,3},{3,2},{4,5},{5,4},{6,7},{7,6},{8,9},{9,8},{10,11... | collective-permute-start | bytes 835592 | tf_op jit(solution)/shard_map/ppermute | solution.py:58
  140.1 8.1 %collective-permute-start.14 = (f32[272,256]{1,0:T(8,128)S(1)}, f32[272,256]{1,0:T(8,128)S(1)}, u32[]{:S(2)}, u32[]{:S(2)}) collective-permute-start(f32[272,256]{1,0:T(8,128)S(1)} %get-tuple-element.81), channel_id=1, source_target_pairs={{0,15},{1,2},{2,1},{3,4},{4,3},{5,6},{6,5},{7,8},{8,7},{9,10},{10,... | collective-permute-start | bytes 835592 | tf_op jit(solution)/shard_map/ppermute | solution.py:58
